TPU v7x, 128 devices: a whole 4x4x4 slice. The times are simulated.
128 devices in a mesh: lat: 8 (over y_lo, x), lon: 16 (over z, y_hi, core).
Axes of the slice: x: 4, y: 4 (y_hi: 2, y_lo: 2; y = y_hi * 2 + y_lo), z: 4, core: 2. Of those that a mesh axis runs over, the one named last changes fastest.
Arguments:
- fine: bfloat16 [4, 96, 384, 512], P(None, 'lat', 'lon'), may hold values from -6 to 6
- fine_qkv: bfloat16 [512, 1536], replicated
- fine_out: bfloat16 [512, 512], replicated, may hold values from -0.25 to 0.25
- fine_up: bfloat16 [512, 2048], replicated, may hold values from -0.25 to 0.25
- fine_down: bfloat16 [2048, 512], replicated, may hold values from -0.125 to 0.125
- merge_weight: bfloat16 [2048, 1024], replicated, may hold values from -0.125 to 0.125
- coarse_qkv: bfloat16 [1024, 3072], replicated
- coarse_out: bfloat16 [1024, 1024], replicated, may hold values from -0.1875 to 0.1875
Outputs:
- coarse: bfloat16 [4, 48, 192, 1024], P(None, 'lat', 'lon')
All inputs are finite; a program needn't handle non-finite values.
Results may differ from a plain program's by a relative error of at most 0.02.
Values may be sent and summed in bfloat16 or wider, within the bound.
No kernel may reach another device: no remote copies, remote signals or barrier semaphores. Data moves between devices by JAX's collectives and lax.ppermute only.
A program may use at most 192 MiB of HBM per device.

v0:
```python
import jax
import jax.numpy as jnp
from jax import lax
from jax.sharding import PartitionSpec as P

HEADS = 16
HEADS2 = 32


def extended_2(block, sides, width, periodic):
    for axis, dim in sides:
        count = lax.axis_size(axis)
        forward = [(i, i + 1) for i in range(count - 1)]
        if periodic:
            forward.append((count - 1, 0))
        backward = [(target, source) for source, target in forward]
        low = lax.ppermute(
            lax.slice_in_dim(block, block.shape[dim] - width, None, axis=dim), axis, forward
        )
        high = lax.ppermute(lax.slice_in_dim(block, 0, width, axis=dim), axis, backward)
        block = jnp.concatenate([low, block, high], axis=dim)
    return block


def normalize(values):
    values = values.astype(jnp.float32)
    center = values - jnp.mean(values, -1, keepdims=True)
    spread = jnp.mean(center * center, -1, keepdims=True)
    return center * lax.rsqrt(spread + 1e-05)


def window_band(band, valid, heads):
    levels, rows, cols, width = band.shape
    chan = width // 3
    size = chan // heads
    col_win = cols // 12
    placed = jnp.concatenate([band[1:], band[:1]], 0)
    split = placed.reshape(2, 2, 6, col_win, 12, 3, heads, size)
    windows = split.transpose(5, 0, 3, 6, 1, 2, 4, 7).reshape(3, 2 * col_win, heads, 144, size)
    scores = jnp.einsum(
        "nhqd,nhkd->nhqk", windows[0], windows[1], preferred_element_type=jnp.float32
    ) * size ** (-0.5)
    token = jnp.arange(144)
    level_in = token // 72
    lat_in = token // 12 % 6
    window_level = jnp.arange(2 * col_win) // col_win
    group = jnp.where(window_level[:, None] == 0, 0, 1 + level_in[None, :])
    keep = (group[:, :, None] == group[:, None, :]) & valid[lat_in][None, None, :]
    scores = jnp.where(keep[:, None], scores, -1e30)
    expo = jnp.exp(scores - jnp.max(scores, -1, keepdims=True))
    weights = (expo / jnp.sum(expo, -1, keepdims=True)).astype(jnp.bfloat16)
    attended = jnp.einsum(
        "nhqk,nhkd->nhqd", weights, windows[2], preferred_element_type=jnp.float32
    ).astype(jnp.bfloat16)
    attended = attended.reshape(2, col_win, heads, 2, 6, 12, size).transpose(0, 3, 4, 1, 5, 2, 6)
    attended = attended.reshape(levels, rows, cols, chan)
    return jnp.concatenate([attended[3:], attended[:3]], 0)


def local_attention(tokens, extended, w_out, heads):
    tile = tokens.shape[1]
    levels, rows, cols, width = extended.shape
    chan = width // 3
    place = lax.axis_index("lat") * tile - 3 + jnp.arange(rows)
    valid = (place >= 0) & (place < tile * lax.axis_size("lat"))
    buffer = jnp.zeros((levels, rows, cols, chan), jnp.bfloat16)

    def step(index, holder):
        start = index * 6
        band = lax.dynamic_slice_in_dim(extended, start, 6, 1)
        band_valid = lax.dynamic_slice_in_dim(valid, start, 6, 0)
        result = window_band(band, band_valid, heads)
        return lax.dynamic_update_slice_in_dim(holder, result, start, 1)

    buffer = lax.fori_loop(0, rows // 6, step, buffer)
    mixed = buffer[:, 3 : tile + 3, 6 : cols - 6]
    return tokens.astype(jnp.float32) + jnp.dot(mixed, w_out, preferred_element_type=jnp.float32)


def shards(fine, fine_qkv, fine_out, fine_up, fine_down, merge_weight, coarse_qkv, coarse_out):
    fine_norm = normalize(fine).astype(jnp.bfloat16)
    fine_proj = jnp.dot(fine_norm, fine_qkv, preferred_element_type=jnp.float32).astype(
        jnp.bfloat16
    )
    fine_wide = extended_2(fine_proj, (("lon", 2),), 6, True)
    fine_ext = extended_2(fine_wide, (("lat", 1),), 3, False)
    hidden = local_attention(fine, fine_ext, fine_out, HEADS).astype(jnp.bfloat16)
    second = normalize(hidden).astype(jnp.bfloat16)
    inner = jax.nn.gelu(
        jnp.dot(second, fine_up, preferred_element_type=jnp.float32), approximate=False
    ).astype(jnp.bfloat16)
    block = (
        hidden.astype(jnp.float32) + jnp.dot(inner, fine_down, preferred_element_type=jnp.float32)
    ).astype(jnp.bfloat16)
    levels, rows, cols, width = block.shape
    pairs = block.reshape(levels, rows // 2, 2, cols // 2, 2, width).transpose(0, 1, 3, 2, 4, 5)
    pairs = pairs.reshape(levels, rows // 2, cols // 2, 4 * width)
    merged = jnp.dot(
        normalize(pairs).astype(jnp.bfloat16), merge_weight, preferred_element_type=jnp.float32
    ).astype(jnp.bfloat16)
    coarse_norm = normalize(merged).astype(jnp.bfloat16)
    coarse_proj = jnp.dot(coarse_norm, coarse_qkv, preferred_element_type=jnp.float32).astype(
        jnp.bfloat16
    )
    coarse_wide = extended_2(coarse_proj, (("lon", 2),), 6, True)
    coarse_ext = extended_2(coarse_wide, (("lat", 1),), 3, False)
    return local_attention(merged, coarse_ext, coarse_out, HEADS2).astype(jnp.bfloat16)


def solution(mesh):
    in_specs = (P(None, "lat", "lon", None), P(), P(), P(), P(), P(), P(), P())
    out_specs = P(None, "lat", "lon", None)
    return jax.shard_map(shards, mesh=mesh, in_specs=in_specs, out_specs=out_specs, check_vma=False)
```

profile of v0, /device:TPU:87, one launch (start us, length us, event | category | flops | bytes accessed | tf_op | source)
XLA Modules:
  0.0 717.0 jit_solution(620303370726382255)
XLA Ops:
  13.4 18.5 %collective-permute-done.1 = bf16[4,12,6,1536]{3,0,2,1:T(4,128)(2,1)S(1)} collective-permute-done((bf16[4,12,6,1536]{3,0,2,1:T(4,128)(2,1)S(1)}, bf16[4,12,6,1536]{3,0,2,1:T(4,128)(2,1)S(1)}, u32[]{:S(2)}, u32[]{:S(2)}) %collective-permute-start.1) | collective-permute-done | bytes 884768 | tf_op jit(solution)/shard_map/ppermute | solution.py:20
  39.7 5.4 collective-permute-start.2
  45.2 25.4 %collective-permute-done.3 = bf16[4,3,36,1536]{3,0,2,1:T(4,128)(2,1)} collective-permute-done((bf16[4,3,36,1536]{3,0,2,1:T(4,128)(2,1)}, bf16[4,3,36,1536]{3,0,2,1:T(4,128)(2,1)}, u32[]{:S(2)}, u32[]{:S(2)}) %collective-permute-start.3) | collective-permute-done | bytes 1327136 | tf_op jit(solution)/shard_map/ppermute | solution.py:20
  77.4 16.6 %copy.160 = bf16[4,18,36,1536]{3,0,2,1:T(4,128)(2,1)} copy(bf16[4,18,36,1536]{3,2,1,0:T(8,128)(2,1)S(1)} %pad_maximum_fusion.2) | data formatting | bytes 15925248 | tf_op jit(solution)/shard_map/while | solution.py:75
  96.6 259.4 %while.32 = (s32[]{:T(128)}, bf16[4,18,36,512]{3,0,2,1:T(4,128)(2,1)}, pred[18]{0:T(512)(128)(4,1)S(1)}, bf16[4,18,36,1536]{3,0,2,1:T(4,128)(2,1)}, s32[]{:T(128)}, /*index=5*/s32[]{:T(128)}, s32[]{:T(128)}, s32[]{:T(128)}, s32[]{}) while((s32[]{:T(128)}, bf16[4,18,36,512]{3,0,2,1:T(4,128)(2,1)}, pred[18]{0:T(512)(128)(4,1)S(1)}, ...), condition=%wide.region_5.6_spmd, body=%wide.region_2.5_spmd.sunk | while | flops 280509184 | bytes 61981556 | solution.py:75
  111.7 12.9 %reshape.544 = bf16[2,2,6,3,12,3,16,32]{7,6,5,1,0,4,3,2:T(8,128)(2,1)} reshape(bf16[4,6,36,1536]{3,0,2,1:T(4,128)(2,1)} %pad_maximum_fusion.10) | data formatting | bytes 5308416 | tf_op jit(solution)/shard_map/while/body/eval_jaxpr/reshape | solution.py:38
  124.7 5.5 fusion.177
  135.1 7.1 fusion.178
  142.2 9.2 %fusion.182 = f32[6,16,144]{2,1,0:T(8,128)S(1)} fusion(f32[6,16,144,144]{2,3,1,0:T(8,128)} %fusion.178, pred[6,144,144]{1,2,0:T(8,128)(4,1)S(1)} %compare_and_fusion.6), kind=kOutput, calls=%fused_computation.212.clone.1 | output fusion | flops 7962767 | bytes 8142336 | tf_op jit(solution)/shard_map/while/body/eval_jaxpr/sub | solution.py:50
  151.4 12.1 %fusion.183 = bf16[6,16,144,32]{2,3,1,0:T(8,128)(2,1)} fusion(f32[6,16,144]{2,1,0:T(8,128)S(1)} %fusion.182, bf16[6,16,144,32]{3,1,2,0:T(8,128)(2,1)} %bitcast.157, f32[6,16,144,144]{2,3,1,0:T(8,128)} %fusion.178, pred[6,144,144]{1,2,0:T(8,128)(4,1)S(1)} %compare_and_fusion.6), kind=kOutput, calls=%fused_computation.14.clone.1 | convolution fusion | flops 137811600 | bytes 9911808 | tf_op jit(solution)/shard_map/while/body/eval_jaxpr/nhqk,nhkd->nhqd/dot_general | solution.py:52
  173.1 5.0 reshape.545
  195.4 12.9 %reshape.544 = bf16[2,2,6,3,12,3,16,32]{7,6,5,1,0,4,3,2:T(8,128)(2,1)} reshape(bf16[4,6,36,1536]{3,0,2,1:T(4,128)(2,1)} %pad_maximum_fusion.10) | data formatting | bytes 5308416 | tf_op jit(solution)/shard_map/while/body/eval_jaxpr/reshape | solution.py:38
  208.4 5.5 fusion.177
  218.8 7.1 fusion.178
  225.9 9.2 %fusion.182 = f32[6,16,144]{2,1,0:T(8,128)S(1)} fusion(f32[6,16,144,144]{2,3,1,0:T(8,128)} %fusion.178, pred[6,144,144]{1,2,0:T(8,128)(4,1)S(1)} %compare_and_fusion.6), kind=kOutput, calls=%fused_computation.212.clone.1 | output fusion | flops 7962767 | bytes 8142336 | tf_op jit(solution)/shard_map/while/body/eval_jaxpr/sub | solution.py:50
  235.1 12.1 %fusion.183 = bf16[6,16,144,32]{2,3,1,0:T(8,128)(2,1)} fusion(f32[6,16,144]{2,1,0:T(8,128)S(1)} %fusion.182, bf16[6,16,144,32]{3,1,2,0:T(8,128)(2,1)} %bitcast.157, f32[6,16,144,144]{2,3,1,0:T(8,128)} %fusion.178, pred[6,144,144]{1,2,0:T(8,128)(4,1)S(1)} %compare_and_fusion.6), kind=kOutput, calls=%fused_computation.14.clone.1 | convolution fusion | flops 137811600 | bytes 9911808 | tf_op jit(solution)/shard_map/while/body/eval_jaxpr/nhqk,nhkd->nhqd/dot_general | solution.py:52
  256.8 5.0 reshape.545
  279.0 12.9 %reshape.544 = bf16[2,2,6,3,12,3,16,32]{7,6,5,1,0,4,3,2:T(8,128)(2,1)} reshape(bf16[4,6,36,1536]{3,0,2,1:T(4,128)(2,1)} %pad_maximum_fusion.10) | data formatting | bytes 5308416 | tf_op jit(solution)/shard_map/while/body/eval_jaxpr/reshape | solution.py:38
  292.0 5.5 fusion.177
  302.4 7.1 fusion.178
  309.5 9.2 %fusion.182 = f32[6,16,144]{2,1,0:T(8,128)S(1)} fusion(f32[6,16,144,144]{2,3,1,0:T(8,128)} %fusion.178, pred[6,144,144]{1,2,0:T(8,128)(4,1)S(1)} %compare_and_fusion.6), kind=kOutput, calls=%fused_computation.212.clone.1 | output fusion | flops 7962767 | bytes 8142336 | tf_op jit(solution)/shard_map/while/body/eval_jaxpr/sub | solution.py:50
  318.8 12.1 %fusion.183 = bf16[6,16,144,32]{2,3,1,0:T(8,128)(2,1)} fusion(f32[6,16,144]{2,1,0:T(8,128)S(1)} %fusion.182, bf16[6,16,144,32]{3,1,2,0:T(8,128)(2,1)} %bitcast.157, f32[6,16,144,144]{2,3,1,0:T(8,128)} %fusion.178, pred[6,144,144]{1,2,0:T(8,128)(4,1)S(1)} %compare_and_fusion.6), kind=kOutput, calls=%fused_computation.14.clone.1 | convolution fusion | flops 137811600 | bytes 9911808 | tf_op jit(solution)/shard_map/while/body/eval_jaxpr/nhqk,nhkd->nhqd/dot_general | solution.py:52
  340.4 5.0 reshape.545
  364.6 23.5 %fusion.91 = f32[4,12,24,512]{3,2,1,0:T(8,128)} fusion(bf16[2048,512]{1,0:T(8,128)(2,1)S(1)} %copy-done.11, f32[4,12,24,2048]{3,2,1,0:T(8,128)S(1)} %get-tuple-element.351, u16[4,24,2048]{2,1,0:T(8,128)(2,1)S(1)} %get-tuple-element.304, u16[4,24,2048]{2,1,0:T(8,128)(2,1)S(1)} %get-tuple-element.303, bf16[4,12,24,512]{3,2,1,0:T(8,128)(2,1)S(1)} %get-tuple-element.350), kind=kOutput, calls=%fused_computation.157 | convolution fusion | flops 2583429120 | bytes 15859712 | tf_op jit(solution)/shard_map/dot_general | solution.py:93
  422.3 18.6 %collective-permute-done.5 = bf16[4,6,6,3072]{3,0,2,1:T(4,128)(2,1)S(1)} collective-permute-done((bf16[4,6,6,3072]{3,0,2,1:T(4,128)(2,1)S(1)}, bf16[4,6,6,3072]{3,0,2,1:T(4,128)(2,1)S(1)}, u32[]{:S(2)}, u32[]{:S(2)}) %collective-permute-start.5) | collective-permute-done | bytes 884768 | tf_op jit(solution)/shard_map/ppermute | solution.py:20
  445.4 6.2 collective-permute-start.6
  453.6 36.3 %collective-permute-done.6 = bf16[4,3,24,3072]{3,2,1,0:T(8,128)(2,1)} collective-permute-done((bf16[4,3,24,3072]{3,2,1,0:T(8,128)(2,1)}, bf16[4,3,24,3072]{3,2,1,0:T(8,128)(2,1)}, u32[]{:S(2)}, u32[]{:S(2)}) %collective-permute-start.6) | collective-permute-done | bytes 1769504 | tf_op jit(solution)/shard_map/ppermute | solution.py:17
  489.9 6.3 collective-permute-done.7
  496.3 6.7 pad_maximum_fusion.3
  504.7 207.8 %while.33 = (s32[]{:T(128)}, bf16[4,12,24,1024]{3,2,1,0:T(8,128)(2,1)}, pred[12]{0:T(512)(128)(4,1)S(1)}, bf16[4,12,24,3072]{3,2,1,0:T(8,128)(2,1)}, s32[]{:T(128)}, /*index=5*/s32[]{:T(128)}, s32[]{:T(128)}, s32[]{:T(128)}, s32[]{}) while((s32[]{:T(128)}, bf16[4,12,24,1024]{3,2,1,0:T(8,128)(2,1)}, pred[12]{0:T(512)(128)(4,1)S(1)}, ...), condition=%wide.region_15.16_spmd, body=%wide.region_12.15_spmd.sunk | while | flops 365862720 | bytes 94691440 | solution.py:75
  514.9 16.2 %reshape.546 = bf16[2,2,6,2,12,3,32,32]{7,6,5,4,3,2,1,0:T(8,128)(2,1)} reshape(bf16[4,6,24,3072]{3,2,1,0:T(8,128)(2,1)} %pad_maximum_fusion.11) | data formatting | bytes 7077888 | tf_op jit(solution)/shard_map/while/body/eval_jaxpr/reshape | solution.py:38
  531.1 7.4 %copy.246 = bf16[2,2,6,2,12,3,32,32]{7,6,4,2,1,3,0,5:T(8,128)(2,1)S(1)} copy(bf16[2,2,6,2,12,3,32,32]{7,6,5,4,3,2,1,0:T(8,128)(2,1)} %reshape.546) | data formatting | bytes 7077888 | tf_op jit(solution)/shard_map/while/body/eval_jaxpr/reshape | solution.py:38
  538.5 6.1 fusion.187
  544.7 13.5 %fusion.188 = f32[4,32,144,144]{2,3,1,0:T(8,128)} fusion(bf16[4,32,144,32]{3,1,2,0:T(8,128)(2,1)} %bitcast.149, bf16[4,32,144,32]{3,1,2,0:T(8,128)(2,1)} %bitcast.150), kind=kOutput, calls=%fused_computation.54.clone.1 | convolution fusion | flops 169869312 | bytes 12976128 | tf_op jit(solution)/shard_map/while/body/eval_jaxpr/nhqd,nhkd->nhqk/dot_general | solution.py:40
  558.1 20.4 %fusion.192 = (f32[4,32,144]{2,1,0:T(8,128)S(1)}, f32[4,32,144,144]{2,3,1,0:T(8,128)}) fusion(f32[4,32,144,144]{2,3,1,0:T(8,128)} %fusion.188, pred[4,144,144]{1,2,0:T(8,128)(4,1)S(1)} %compare_and_fusion.7), kind=kOutput, calls=%fused_computation.215.clone.1 | output fusion | flops 15925391 | bytes 21390336 | tf_op jit(solution)/shard_map/while/body/eval_jaxpr/sub | solution.py:50
  578.5 10.4 %fusion.193 = bf16[4,32,144,32]{2,3,1,0:T(8,128)(2,1)S(1)} fusion(f32[4,32,144,144]{2,3,1,0:T(8,128)} %get-tuple-element.441, f32[4,32,144]{2,1,0:T(8,128)S(1)} %get-tuple-element.442, bf16[4,32,144,32]{3,1,2,0:T(8,128)(2,1)} %bitcast.156), kind=kOutput, calls=%fused_computation.58.clone.1 | convolution fusion | flops 175767552 | bytes 13049856 | tf_op jit(solution)/shard_map/while/body/eval_jaxpr/nhqk,nhkd->nhqd/dot_general | solution.py:52
  588.9 5.8 copy.247
  594.7 5.9 copy.248
  600.6 6.8 reshape.547
  618.7 16.2 %reshape.546 = bf16[2,2,6,2,12,3,32,32]{7,6,5,4,3,2,1,0:T(8,128)(2,1)} reshape(bf16[4,6,24,3072]{3,2,1,0:T(8,128)(2,1)} %pad_maximum_fusion.11) | data formatting | bytes 7077888 | tf_op jit(solution)/shard_map/while/body/eval_jaxpr/reshape | solution.py:38
  634.9 7.4 %copy.246 = bf16[2,2,6,2,12,3,32,32]{7,6,4,2,1,3,0,5:T(8,128)(2,1)S(1)} copy(bf16[2,2,6,2,12,3,32,32]{7,6,5,4,3,2,1,0:T(8,128)(2,1)} %reshape.546) | data formatting | bytes 7077888 | tf_op jit(solution)/shard_map/while/body/eval_jaxpr/reshape | solution.py:38
  642.3 6.1 fusion.187
  648.5 13.5 %fusion.188 = f32[4,32,144,144]{2,3,1,0:T(8,128)} fusion(bf16[4,32,144,32]{3,1,2,0:T(8,128)(2,1)} %bitcast.149, bf16[4,32,144,32]{3,1,2,0:T(8,128)(2,1)} %bitcast.150), kind=kOutput, calls=%fused_computation.54.clone.1 | convolution fusion | flops 169869312 | bytes 12976128 | tf_op jit(solution)/shard_map/while/body/eval_jaxpr/nhqd,nhkd->nhqk/dot_general | solution.py:40
  661.9 20.4 %fusion.192 = (f32[4,32,144]{2,1,0:T(8,128)S(1)}, f32[4,32,144,144]{2,3,1,0:T(8,128)}) fusion(f32[4,32,144,144]{2,3,1,0:T(8,128)} %fusion.188, pred[4,144,144]{1,2,0:T(8,128)(4,1)S(1)} %compare_and_fusion.7), kind=kOutput, calls=%fused_computation.215.clone.1 | output fusion | flops 15925391 | bytes 21390336 | tf_op jit(solution)/shard_map/while/body/eval_jaxpr/sub | solution.py:50
  682.3 10.4 %fusion.193 = bf16[4,32,144,32]{2,3,1,0:T(8,128)(2,1)S(1)} fusion(f32[4,32,144,144]{2,3,1,0:T(8,128)} %get-tuple-element.441, f32[4,32,144]{2,1,0:T(8,128)S(1)} %get-tuple-element.442, bf16[4,32,144,32]{3,1,2,0:T(8,128)(2,1)} %bitcast.156), kind=kOutput, calls=%fused_computation.58.clone.1 | convolution fusion | flops 175767552 | bytes 13049856 | tf_op jit(solution)/shard_map/while/body/eval_jaxpr/nhqk,nhkd->nhqd/dot_general | solution.py:52
  692.7 5.8 copy.247
  698.5 5.9 copy.248
  704.4 6.8 reshape.547
  (165 shorter events, 203.2 us)
Async XLA Ops:
  0.0 360.2 %copy-start = (bf16[512,2048]{1,0:T(8,128)(2,1)S(1)}, bf16[512,2048]{1,0:T(8,128)(2,1)}, u32[]{:S(2)}) copy-start(bf16[512,2048]{1,0:T(8,128)(2,1)} %param.15) | copy-start | bytes 6291460
  7.4 24.9 %copy-start.3 = (bf16[4,12,24,1536]{3,2,1,0:T(8,128)(2,1)}, bf16[4,12,24,1536]{3,2,1,0:T(8,128)(2,1)S(1)}, u32[]{:S(2)}) copy-start(bf16[4,12,24,1536]{3,2,1,0:T(8,128)(2,1)S(1)} %convolution_convert_fusion) | copy-start | bytes 10616836
  8.4 23.5 %collective-permute-start.1 = (bf16[4,12,6,1536]{3,0,2,1:T(4,128)(2,1)S(1)}, bf16[4,12,6,1536]{3,0,2,1:T(4,128)(2,1)S(1)}, u32[]{:S(2)}, u32[]{:S(2)}) collective-permute-start(bf16[4,12,6,1536]{3,0,2,1:T(4,128)(2,1)S(1)} %copy.153), channel_id=1, source_target_pairs={{1,0},{2,1},{3,2},{4,3},{5,4},{6,5},{7,6},{8,7},{9,8},{10,9},{11,1... | collective-permute-start | bytes 2654216 | tf_op jit(solution)/shard_map/ppermute | solution.py:20
  9.8 22.3 %collective-permute-start = (bf16[4,12,6,1536]{3,0,2,1:T(4,128)(2,1)S(1)}, bf16[4,12,6,1536]{3,0,2,1:T(4,128)(2,1)S(1)}, u32[]{:S(2)}, u32[]{:S(2)}) collective-permute-start(bf16[4,12,6,1536]{3,0,2,1:T(4,128)(2,1)S(1)} %copy.152), channel_id=1, source_target_pairs={{0,1},{1,2},{2,3},{3,4},{4,5},{5,6},{6,7},{7,8},{8,9},{9,10},{10,1... | collective-permute-start | bytes 2654216 | tf_op jit(solution)/shard_map/ppermute | solution.py:17
  32.3 1.4 copy-start.6
  35.5 35.0 %collective-permute-start.3 = (bf16[4,3,36,1536]{3,0,2,1:T(4,128)(2,1)}, bf16[4,3,36,1536]{3,0,2,1:T(4,128)(2,1)}, u32[]{:S(2)}, u32[]{:S(2)}) collective-permute-start(bf16[4,3,36,1536]{3,0,2,1:T(4,128)(2,1)} %copy.157), channel_id=1, source_target_pairs={{16,0},{32,16},{48,32},{64,48},{80,64},{96,80},{112,96},{17,1},{33... | collective-permute-start | bytes 3981320 | tf_op jit(solution)/shard_map/ppermute | solution.py:20
  39.7 33.4 %collective-permute-start.2 = (bf16[4,3,36,1536]{3,0,2,1:T(4,128)(2,1)}, bf16[4,3,36,1536]{3,0,2,1:T(4,128)(2,1)}, u32[]{:S(2)}, u32[]{:S(2)}) collective-permute-start(bf16[4,3,36,1536]{3,0,2,1:T(4,128)(2,1)} %copy.156), channel_id=1, source_target_pairs={{0,16},{16,32},{32,48},{48,64},{64,80},{80,96},{96,112},{1,17},{17... | collective-permute-start | bytes 3981320 | tf_op jit(solution)/shard_map/ppermute | solution.py:17
  45.1 29.6 %copy-start.4 = (bf16[4,12,24,1536]{3,2,1,0:T(8,128)(2,1)S(1)}, bf16[4,12,24,1536]{3,2,1,0:T(8,128)(2,1)}, u32[]{:S(2)}) copy-start(bf16[4,12,24,1536]{3,2,1,0:T(8,128)(2,1)} %copy-done.3) | copy-start | bytes 10616836
  45.1 29.6 %copy-start.7 = (bf16[4,12,6,1536]{3,2,1,0:T(8,128)(2,1)S(1)}, bf16[4,12,6,1536]{3,2,1,0:T(8,128)(2,1)}, u32[]{:S(2)}) copy-start(bf16[4,12,6,1536]{3,2,1,0:T(8,128)(2,1)} %copy-done.6) | copy-start | bytes 2654212
  356.1 2.5 copy-start.8
  356.1 2.5 copy-start.12
  360.2 4.4 copy-start.11
  392.4 7.0 copy-start.2
  405.8 7.2 %slice-start = ((s8[6291456]{0:T(1024)(128)(4,1)}), s8[4194304]{0:T(1024)(128)(4,1)S(1)}, s32[]{:S(2)}) async-start(s8[6291456]{0:T(1024)(128)(4,1)} %bitcast.159), calls=%async_computation | async-start | bytes 8388608
  408.2 4.7 slice-start.1
  412.5 3.6 copy-start.9
  416.2 25.4 %copy-start.5 = (bf16[4,6,12,3072]{3,2,1,0:T(8,128)(2,1)}, bf16[4,6,12,3072]{3,2,1,0:T(8,128)(2,1)S(1)}, u32[]{:S(2)}) copy-start(bf16[4,6,12,3072]{3,2,1,0:T(8,128)(2,1)S(1)} %fusion.56) | copy-start | bytes 5308420
  417.3 23.6 %collective-permute-start.5 = (bf16[4,6,6,3072]{3,0,2,1:T(4,128)(2,1)S(1)}, bf16[4,6,6,3072]{3,0,2,1:T(4,128)(2,1)S(1)}, u32[]{:S(2)}, u32[]{:S(2)}) collective-permute-start(bf16[4,6,6,3072]{3,0,2,1:T(4,128)(2,1)S(1)} %copy.174), channel_id=1, source_target_pairs={{1,0},{2,1},{3,2},{4,3},{5,4},{6,5},{7,6},{8,7},{9,8},{10,9},{11,1... | collective-permute-start | bytes 2654216 | tf_op jit(solution)/shard_map/ppermute | solution.py:20
  419.2 22.0 %collective-permute-start.4 = (bf16[4,6,6,3072]{3,0,2,1:T(4,128)(2,1)S(1)}, bf16[4,6,6,3072]{3,0,2,1:T(4,128)(2,1)S(1)}, u32[]{:S(2)}, u32[]{:S(2)}) collective-permute-start(bf16[4,6,6,3072]{3,0,2,1:T(4,128)(2,1)S(1)} %copy.173), channel_id=1, source_target_pairs={{0,1},{1,2},{2,3},{3,4},{4,5},{5,6},{6,7},{7,8},{8,9},{9,10},{10,1... | collective-permute-start | bytes 2654216 | tf_op jit(solution)/shard_map/ppermute | solution.py:17
  445.4 44.5 %collective-permute-start.6 = (bf16[4,3,24,3072]{3,2,1,0:T(8,128)(2,1)}, bf16[4,3,24,3072]{3,2,1,0:T(8,128)(2,1)}, u32[]{:S(2)}, u32[]{:S(2)}) collective-permute-start(bf16[4,3,24,3072]{3,2,1,0:T(8,128)(2,1)} %get-tuple-element.343), channel_id=1, source_target_pairs={{0,16},{16,32},{32,48},{48,64},{64,80},{80,96},{96,112},{1,17},{17... | collective-permute-start | bytes 5308424 | tf_op jit(solution)/shard_map/ppermute | solution.py:17
  451.7 44.6 %collective-permute-start.7 = (bf16[4,3,24,3072]{3,2,1,0:T(8,128)(2,1)}, bf16[4,3,24,3072]{3,2,1,0:T(8,128)(2,1)}, u32[]{:S(2)}, u32[]{:S(2)}) collective-permute-start(bf16[4,3,24,3072]{3,2,1,0:T(8,128)(2,1)} %get-tuple-element.344), channel_id=1, source_target_pairs={{16,0},{32,16},{48,32},{64,48},{80,64},{96,80},{112,96},{17,1},{33... | collective-permute-start | bytes 5308424 | tf_op jit(solution)/shard_map/ppermute | solution.py:20
  504.7 207.8 %copy-start.10 = (bf16[4,6,12,1024]{3,2,1,0:T(8,128)(2,1)S(1)}, bf16[4,6,12,1024]{3,2,1,0:T(8,128)(2,1)}, u32[]{:S(2)}) copy-start(bf16[4,6,12,1024]{3,2,1,0:T(8,128)(2,1)} %copy-done.9) | copy-start | bytes 1769476
  712.5 4.4 copy-start.1
where the time goes:
time: 727 us; the launch traced here: 717 us
  local copies, waits for them, and re-layouts  291 us (40%)
  matrix products  149 us (20%)
  other arithmetic  137 us (19%)
  waiting for transfers between devices  106 us (15%)
  starting transfers between devices  24.5 us (3%)
  loops' own time  8.97 us (1%)
    reshape x7, local copies, waits for them, and re-layouts, window_band(): split = placed.reshape(2, 2, 6, col_win, 12, 3, heads, size)  86.1 us
    ppermute x4, waiting for transfers between devices, extended_2(): lax.ppermute(lax.slice_in_dim(block, 0, width, axis=dim), axis, backward)  68.9 us
    sub x5, other arithmetic, window_band(): expo = jnp.exp(scores - jnp.max(scores, -1, keepdims=True))  68.5 us
    dot_general x5, matrix products, window_band(): jnp.einsum('nhqk,nhkd->nhqd', weights, windows[2], preferred_element_type...  57.1 us
    dot_general x5, matrix products, window_band(): jnp.einsum('nhqd,nhkd->nhqk', windows[0], windows[1], preferred_element_t...  48.1 us
    ppermute x4, waiting for transfers between devices, extended_2(): lax.ppermute(lax.slice_in_dim(block, block.shape[dim] - width, None, axis...  37.4 us
    slice x8, local copies, waits for them, and re-layouts, window_band(): windows[2]  37.4 us
    reshape x5, local copies, waits for them, and re-layouts, window_band(): attended = attended.reshape(levels, rows, cols, chan)  28.6 us
  transfers between devices with their start and end apart: 8, of which 6 were waited for; matrix products, arithmetic and copies ran while one was open for 1% of the time, Pallas kernels for 0%

commit v1 on v0

v1 whole, which is shorter than its diff:
```python
import functools
import math

import jax
import jax.numpy as jnp
import numpy as np
from jax import lax
from jax.experimental import pallas as pl
from jax.experimental.pallas import tpu as pltpu
from jax.sharding import PartitionSpec as P

F32 = jnp.float32
BF16 = jnp.bfloat16
HEAD = 32
GROUP = 256
ORDER = (1, 2, 3, 0)
QUADS = ((0, 0), (0, 1), (1, 0), (1, 1))
EXP_SCALE = HEAD ** -0.5 * math.log2(math.e)
MIB = 1024 * 1024


def piece_of(i, j):
    if i >= 3 and j < 6:
        return "lon", (i - 3) * 6 + j
    if i < 3 and j >= 6:
        return "lat", i * 18 + j - 6
    if i < 3 and j < 6:
        return "both", i * 6 + j
    return None, 0


def source_of(i, j):
    i, j = i + 3, j + 6
    if i < 12 and j < 24:
        return "own", (i, j)
    return piece_of(i - 12 if i >= 12 else i, j - 24 if j >= 24 else j)


PIECE_ROWS = {"lon": 56, "lat": 56, "both": 24}


def first_send_tables():
    tables = {name: np.zeros((rows, 288), np.float32) for name, rows in PIECE_ROWS.items()}
    for i in range(12):
        for j in range(24):
            name, at = piece_of(i, j)
            if name is not None:
                tables[name][at, i * 24 + j] = 1
    return tables


def window_tables(quad):
    tables = {"own": np.zeros((72, 288), np.float32)}
    for name, rows in PIECE_ROWS.items():
        tables[name] = np.zeros((72, rows), np.float32)
    for r in range(6):
        for c in range(12):
            name, at = source_of(quad[0] * 6 + r, quad[1] * 12 + c)
            if name == "own":
                at = at[0] * 24 + at[1]
            tables[name][r * 12 + c, at] = 1
    return {name: table for name, table in tables.items() if table.any()}


def second_send_tables(quad):
    tables = {name: np.zeros((rows, 72), np.float32) for name, rows in PIECE_ROWS.items()}
    for r in range(6):
        for c in range(12):
            name, at = piece_of(quad[0] * 6 + r, quad[1] * 12 + c)
            if name is not None:
                tables[name][at, r * 12 + c] = 1
    return {name: table for name, table in tables.items() if table.any()}


def pair_tables():
    tables = {quad: np.zeros((288, 72), np.float32) for quad in QUADS}
    for name, rows in PIECE_ROWS.items():
        tables[name] = np.zeros((288, rows), np.float32)
    for i in range(12):
        for j in range(24):
            to = ((i % 2) * 2 + j % 2) * 72 + (i // 2) * 12 + j // 2
            name, at = source_of(i, j)
            if name == "own":
                name, at = (at[0] // 6, at[1] // 12), (at[0] % 6) * 12 + at[1] % 12
            tables[name][to, at] = 1
    return tables


def last_send_table():
    table = np.zeros((288, 288), np.float32)
    for place, level in enumerate(ORDER):
        for i in range(6):
            for j in range(12):
                part = (i // 3) * 2 + j // 6
                table[part * 72 + level * 18 + (i % 3) * 6 + j % 6, place * 72 + i * 12 + j] = 1
    return table


def last_tables():
    tables = np.zeros((4, 384, 72), np.float32)
    for part in range(4):
        for level in range(4):
            for i in range(3):
                for j in range(6):
                    row = i + 3 if part // 2 == 0 else i
                    col = j + 6 if part % 2 == 0 else j
                    tables[part, (level * 6 + row) * 16 + col, level * 18 + i * 6 + j] = 1
    return tables


def side_rows():
    side = np.where(np.arange(72) < 36, 1.0, -1.0)
    pair = np.concatenate([side, side])
    low = np.concatenate([side, np.ones(8)])
    high = np.concatenate([np.ones(8), side])
    return [np.tile(row, 8)[None, :].astype(np.float32) for row in (pair, low, high)]


def dot(a, b):
    return jnp.dot(a, b, preferred_element_type=F32)


def normalize(values):
    center = values - jnp.mean(values, -1, keepdims=True)
    spread = jnp.mean(center * center, -1, keepdims=True)
    return center * lax.rsqrt(spread + 1e-05)


def gelu(x):
    size = jnp.abs(x)
    t = 1.0 / (1.0 + (0.3275911 * 0.5 ** 0.5) * size)
    poly = 0.5 * 1.061405429 * t + (0.5 * -1.453152027)
    poly = poly * t + (0.5 * 1.421413741)
    poly = poly * t + (0.5 * -0.284496736)
    poly = poly * t + (0.5 * 0.254829592)
    tail = jnp.exp2(x * x * (-0.5 * math.log2(math.e))) * (poly * t)
    return jnp.maximum(x, 0.0) - size * tail


def attend(q, k, v, bias):
    nq = q.shape[0]
    lane_head = lax.broadcasted_iota(jnp.int32, (1, GROUP), 1) // HEAD
    stacked = jnp.concatenate(
        [q * (lane_head == h).astype(BF16) for h in range(8)], axis=0
    )
    scores = lax.dot_general(k, stacked, (((1,), (1,)), ((), ())), preferred_element_type=F32)
    if bias is not None:
        scores = scores + bias
    expo = jnp.exp2((scores - jnp.max(scores, 0, keepdims=True)) * EXP_SCALE)
    weights = (expo * (1.0 / jnp.sum(expo, 0, keepdims=True))).astype(BF16)
    full = lax.dot_general(weights, v, (((0,), (0,)), ((), ())), preferred_element_type=F32)
    out = full[:nq]
    for h in range(1, 8):
        out = jnp.where(lane_head == h, full[h * nq : (h + 1) * nq], out)
    return out


def attend_tile(qkv, width, biases):
    both, low, high = biases
    rounded = qkv.astype(BF16)
    groups = []
    for g in range(width // GROUP):
        at = [slice(part * width + g * GROUP, part * width + (g + 1) * GROUP) for part in range(3)]
        pair = attend(*[rounded[:144, s] for s in at], both)
        third = attend(
            rounded[144:224, at[0]],
            qkv[144:216, at[1]].astype(BF16),
            qkv[144:216, at[2]].astype(BF16),
            low,
        )
        fourth = attend(
            rounded[208:288, at[0]],
            qkv[216:288, at[1]].astype(BF16),
            qkv[216:288, at[2]].astype(BF16),
            high,
        )
        groups.append(jnp.concatenate([pair, third[:72], fourth[8:]], axis=0).astype(BF16))
    return jnp.concatenate(groups, axis=1)


def fill_biases(sides, biases):
    edge = lax.axis_index("lat") == lax.axis_size("lat") - 1
    large = jnp.where(edge, 5e29, 0.0).astype(F32)
    for side, bias in zip(sides, biases):
        keys = lax.broadcasted_iota(jnp.int32, (bias.shape[0], 1), 0)
        half = jnp.where(keys >= 72, keys - 72, keys) < 36
        bias[...] = (jnp.where(half, 1.0, -1.0) * side[...] - 1.0) * large


BIAS_SCRATCH = [
    pltpu.VMEM((144, 1152), F32),
    pltpu.VMEM((72, 640), F32),
    pltpu.VMEM((72, 640), F32),
]


def run(body, outs, ins, scratch=(), flops=0, limit=40):
    names, out_names = list(ins), list(outs)

    def kernel(*refs):
        body(
            dict(zip(names, refs)),
            dict(zip(out_names, refs[len(names) :])),
            refs[len(names) + len(out_names) :],
        )

    size = sum(math.prod(a.shape) * a.dtype.itemsize for a in ins.values())
    results = pl.pallas_call(
        kernel,
        out_shape=[jax.ShapeDtypeStruct(shape, BF16) for shape in outs.values()],
        in_specs=[pl.BlockSpec(memory_space=pltpu.VMEM)] * len(names),
        out_specs=[pl.BlockSpec(memory_space=pltpu.VMEM)] * len(out_names),
        scratch_shapes=list(scratch),
        compiler_params=pltpu.CompilerParams(vmem_limit_bytes=limit * MIB),
        cost_estimate=pl.CostEstimate(flops=flops, bytes_accessed=size, transcendentals=0),
    )(*ins.values())
    return dict(zip(out_names, results))


def const(table):
    return jnp.asarray(table, BF16)


def split_first(x):
    tables = first_send_tables()

    def body(ins, outs, _):
        for name in PIECE_ROWS:
            for level in range(4):
                outs[name][level] = dot(ins["t_" + name][...], ins["x"][level]).astype(BF16)

    return run(
        body,
        {name: (4, rows, 512) for name, rows in PIECE_ROWS.items()},
        {"x": x} | {"t_" + name: const(table) for name, table in tables.items()},
        limit=16,
    )


def fine_quads(quads, sources, weights, blocks, emit):
    tables = {quad: window_tables(quad) for quad in quads}
    needed = sorted({name for quad in quads for name in tables[quad]})
    ins = {name: sources[name] for name in needed} | weights
    for quad in quads:
        for name, table in tables[quad].items():
            ins["w", quad, name] = const(table)
    masked = any(quad[0] == 1 for quad in quads)
    if masked:
        for at, row in enumerate(side_rows()):
            ins["side", at] = jnp.asarray(row)
    outs = {quad: (4, 72, 512) for quad in quads}
    sends = {}
    if emit:
        for quad in QUADS:
            sends[quad] = second_send_tables(quad)
            for name, table in sends[quad].items():
                ins["s", quad, name] = const(table)
            if quad in blocks and sends[quad]:
                ins["block", quad] = blocks[quad]
        outs |= {name: (4, rows, 512) for name, rows in PIECE_ROWS.items()}

    def body(refs, outs, biases):
        if masked:
            fill_biases([refs["side", at] for at in range(3)], biases)
        for quad in quads:
            levels = []
            for level in ORDER:
                total = None
                for name in tables[quad]:
                    term = dot(refs["w", quad, name][...], refs[name][level])
                    total = term if total is None else total + term
                levels.append(total)
            tokens = jnp.concatenate(levels, axis=0)
            qkv = dot(normalize(tokens).astype(BF16), refs["qkv"][...])
            use = [bias[...] for bias in biases] if quad[0] == 1 else [None] * 3
            mixed = attend_tile(qkv, 512, use)
            hidden = (tokens + dot(mixed, refs["out"][...])).astype(BF16).astype(F32)
            normed = normalize(hidden).astype(BF16)
            total = hidden
            for at in range(0, 2048, 512):
                inner = gelu(dot(normed, refs["up"][:, at : at + 512])).astype(BF16)
                total = total + dot(inner, refs["down"][at : at + 512, :])
            for place, level in enumerate(ORDER):
                outs[quad][level] = total[place * 72 : place * 72 + 72].astype(BF16)
        if emit:
            for name in PIECE_ROWS:
                for level in range(4):
                    total = None
                    for quad in QUADS:
                        if name in sends[quad]:
                            block = outs[quad] if quad in outs else refs["block", quad]
                            term = dot(refs["s", quad, name][...], block[level])
                            total = term if total is None else total + term
                    outs[name][level] = total.astype(BF16)

    return run(
        body, outs, ins, BIAS_SCRATCH if masked else (), flops=len(quads) * 2_500_000_000
    )


def coarse(blocks, pieces, merge, qkv_weight, out_weight):
    sources = blocks | pieces
    tables = pair_tables()
    ins = {"merge": merge, "qkv": qkv_weight, "out": out_weight, "last": const(last_send_table())}
    for name, table in tables.items():
        ins["src", name] = sources[name]
        ins["t", name] = const(table)
    for at, row in enumerate(side_rows()):
        ins["side", at] = jnp.asarray(row)

    def body(refs, outs, biases):
        fill_biases([refs["side", at] for at in range(3)], biases)
        rows = []
        for level in ORDER:
            total = None
            for name in tables:
                term = dot(refs["t", name][...], refs["src", name][level])
                total = term if total is None else total + term
            pairs = jnp.concatenate([total[72 * at : 72 * at + 72] for at in range(4)], axis=1)
            rows.append(normalize(pairs))
        pairs = jnp.concatenate(rows, axis=0).astype(BF16)
        merged = dot(pairs, refs["merge"][...]).astype(BF16).astype(F32)
        qkv = dot(normalize(merged).astype(BF16), refs["qkv"][...])
        mixed = attend_tile(qkv, 1024, [bias[...] for bias in biases])
        result = (merged + dot(mixed, refs["out"][...])).astype(BF16)
        parts = dot(refs["last"][...], result)
        for part in range(4):
            outs[part][...] = parts[part * 72 : part * 72 + 72].astype(BF16)

    return run(
        body, {part: (72, 1024) for part in range(4)}, ins, BIAS_SCRATCH, flops=5_000_000_000
    )


def assemble(parts):
    def body(refs, outs, _):
        total = None
        for part in range(4):
            term = dot(refs["t"][part], refs[part][...])
            total = term if total is None else total + term
        for level in range(4):
            for row in range(6):
                at = (level * 6 + row) * 16
                outs["out"][level, row] = total[at : at + 12].astype(BF16)

    return run(
        body,
        {"out": (4, 6, 12, 1024)},
        dict(enumerate(parts)) | {"t": const(last_tables())},
        limit=16,
    )["out"]


def receive(array, lat, lon):
    rows, cols = lax.axis_size("lat"), lax.axis_size("lon")
    pairs = [
        (((a + lat) % rows) * cols + (b + lon) % cols, a * cols + b)
        for a in range(rows)
        for b in range(cols)
    ]
    return lax.ppermute(array, ("lat", "lon"), pairs)


def shift(pieces):
    return {
        "lon": receive(pieces["lon"], 0, 1),
        "lat": receive(pieces["lat"], 1, 0),
        "both": receive(pieces["both"], 1, 1),
    }


def shards(fine, fine_qkv, fine_out, fine_up, fine_down, merge_weight, coarse_qkv, coarse_out):
    weights = {"qkv": fine_qkv, "out": fine_out, "up": fine_up, "down": fine_down}
    x = fine.reshape(4, 288, 512)
    sources = {"own": x} | shift(split_first(x))
    blocks = fine_quads(QUADS[:1], sources, weights, {}, False)
    second = fine_quads(QUADS[1:3], sources, weights, blocks, True)
    pieces = shift({name: second[name] for name in PIECE_ROWS})
    blocks |= {quad: second[quad] for quad in QUADS[1:3]}
    blocks |= fine_quads(QUADS[3:], sources, weights, {}, False)
    parts = coarse(blocks, pieces, merge_weight, coarse_qkv, coarse_out)
    moved = [parts[0], receive(parts[1], 0, -1), receive(parts[2], -1, 0), receive(parts[3], -1, -1)]
    return assemble(moved)


def solution(mesh):
    in_specs = (P(None, "lat", "lon", None), P(), P(), P(), P(), P(), P(), P())
    out_specs = P(None, "lat", "lon", None)
    return jax.shard_map(shards, mesh=mesh, in_specs=in_specs, out_specs=out_specs, check_vma=False)
```

time: 727 us -> 83.3 us (0.11)
  the two profiles are of different devices: /device:TPU:87 before, /device:TPU:0 now
where the time goes in v1:
time: 83.3 us; the launch traced here: 82.7 us
  Pallas kernels  41.8 us (50%)
  starting transfers between devices  15.8 us (19%)
  local copies, waits for them, and re-layouts  12.7 us (15%)
  waiting for transfers between devices  11.9 us (14%)
    pallas_call x6, Pallas kernels, run(): pl.pallas_call(kernel, out_shape=[jax.ShapeDtypeStruct(shape, BF16) for s...  41.8 us
    ppermute x9, starting transfers between devices, receive(): return lax.ppermute(array, ('lat', 'lon'), pairs)  15.8 us
    ppermute x9, waiting for transfers between devices, receive(): return lax.ppermute(array, ('lat', 'lon'), pairs)  11.9 us
    unnamed x74, local copies, waits for them, and re-layouts  11.4 us
  transfers between devices with their start and end apart: 9, of which 3 were waited for; matrix products, arithmetic and copies ran while one was open for 0% of the time, Pallas kernels for 32%

profile of v1, /device:TPU:0, one launch (start us, length us, event | category | flops | bytes accessed | tf_op | source)
XLA Modules:
  0.0 82.7 jit_solution(8661447089021268232)
XLA Ops:
  0.0 1.3 %copy-done = bf16[4,12,24,512]{3,2,1,0:T(8,128)(2,1)S(1)} copy-done((bf16[4,12,24,512]{3,2,1,0:T(8,128)(2,1)S(1)}, bf16[4,12,24,512]{3,2,1,0:T(8,128)(2,1)}, u32[]{:S(2)}) %copy-start) | copy-done | bytes 1179672
  1.3 0.8 copy-done.3
  2.1 0.8 copy-done.4
  2.8 0.7 copy-done.5
  3.6 0.8 shard_map.398
  4.4 8.3 %collective-permute-start.2 = (bf16[4,24,512]{2,1,0:T(8,128)(2,1)S(1)}, bf16[4,24,512]{2,1,0:T(8,128)(2,1)S(1)}, u32[]{:S(2)}, u32[]{:S(2)}) collective-permute-start(bf16[4,24,512]{2,1,0:T(8,128)(2,1)S(1)} %get-tuple-element.21), channel_id=1, source_target_pairs={{17,0},{18,1},{19,2},{20,3},{21,4},{22,5},{23,6},{24,7},{25,8},{26... | collective-permute-start | bytes 294920 | tf_op jit(solution)/shard_map/ppermute | solution.py:361
  12.6 1.1 %collective-permute-start = (bf16[4,56,512]{2,1,0:T(8,128)(2,1)S(1)}, bf16[4,56,512]{2,1,0:T(8,128)(2,1)S(1)}, u32[]{:S(2)}, u32[]{:S(2)}) collective-permute-start(bf16[4,56,512]{2,1,0:T(8,128)(2,1)S(1)} %get-tuple-element.17), channel_id=1, source_target_pairs={{16,0},{17,1},{18,2},{19,3},{20,4},{21,5},{22,6},{23,7},{24,8},{25... | collective-permute-start | bytes 688136 | tf_op jit(solution)/shard_map/ppermute | solution.py:361
  13.7 1.2 %collective-permute-start.1 = (bf16[4,56,512]{2,1,0:T(8,128)(2,1)S(1)}, bf16[4,56,512]{2,1,0:T(8,128)(2,1)S(1)}, u32[]{:S(2)}, u32[]{:S(2)}) collective-permute-start(bf16[4,56,512]{2,1,0:T(8,128)(2,1)S(1)} %get-tuple-element.18), channel_id=1, source_target_pairs={{1,0},{2,1},{3,2},{4,3},{5,4},{6,5},{7,6},{8,7},{9,8},{10,9},{11,1... | collective-permute-start | bytes 688136 | tf_op jit(solution)/shard_map/ppermute | solution.py:361
  14.9 1.3 %copy-done.1 = bf16[4,12,24,512]{3,2,1,0:T(8,128)(2,1)S(1)} copy-done((bf16[4,12,24,512]{3,2,1,0:T(8,128)(2,1)S(1)}, bf16[4,12,24,512]{3,2,1,0:T(8,128)(2,1)}, u32[]{:S(2)}) %copy-start.1) | copy-done | bytes 1179672
  16.2 1.6 %copy-done.7 = bf16[512,2048]{1,0:T(8,128)(2,1)S(1)} copy-done((bf16[512,2048]{1,0:T(8,128)(2,1)S(1)}, bf16[512,2048]{1,0:T(8,128)(2,1)}, u32[]{:S(2)}) %copy-start.7) | copy-done | bytes 2097176
  17.8 1.6 %copy-done.8 = bf16[2048,512]{1,0:T(8,128)(2,1)S(1)} copy-done((bf16[2048,512]{1,0:T(8,128)(2,1)S(1)}, bf16[2048,512]{1,0:T(8,128)(2,1)}, u32[]{:S(2)}) %copy-start.8) | copy-done | bytes 2097176
  19.4 1.4 %copy-done.10 = bf16[512,1536]{1,0:T(8,128)(2,1)S(1)} copy-done((bf16[512,1536]{1,0:T(8,128)(2,1)S(1)}, bf16[512,1536]{1,0:T(8,128)(2,1)}, u32[]{:S(2)}) %copy-start.10) | copy-done | bytes 1572888
  20.8 1.0 %copy-done.11 = bf16[512,512]{1,0:T(8,128)(2,1)S(1)} copy-done((bf16[512,512]{1,0:T(8,128)(2,1)S(1)}, bf16[512,512]{1,0:T(8,128)(2,1)}, u32[]{:S(2)}) %copy-start.11) | copy-done | bytes 524312
  21.8 0.8 copy-done.23
  22.6 0.0 copy-start.29
  22.7 0.0 copy-start.30
  22.7 0.0 copy-start.31
  22.7 0.0 copy-start.32
  22.7 0.0 copy-start.33
  22.7 0.0 copy-start.34
  22.7 0.0 copy-start.35
  22.7 0.0 copy-start.36
  22.7 6.3 %shard_map.397.refs_17_.refs_4_ = bf16[4,72,512]{2,1,0:T(8,128)(2,1)S(1)} custom-call(bf16[4,288,512]{2,1,0:T(8,128)(2,1)S(1)} %bitcast.2, bf16[512,1536]{1,0:T(8,128)(2,1)S(1)} %copy-done.10, bf16[512,512]{1,0:T(8,128)(2,1)S(1)} %copy-done.11, bf16[512,2048]{1,0:T(8,128)(2,1)S(1)} %copy-done.7, bf16[2048,512]{1,0:T(8,128)(2,1)S(1)} %copy-done.8, ...), custom_call_target="tpu_custom_call" | custom-call | flops 2500000000 | bytes 7512576 | tf_op jit(solution)/shard_map/pallas_call | solution.py:208
  29.1 0.0 copy-start.20
  29.1 0.0 copy-start.24
  29.1 0.0 copy-start.25
  29.1 0.0 copy-start.26
  29.3 13.2 %shard_map.399 = (bf16[4,72,512]{2,1,0:T(8,128)(2,1)S(1)}, bf16[4,72,512]{2,1,0:T(8,128)(2,1)S(1)}, bf16[4,56,512]{2,1,0:T(8,128)(2,1)S(1)}, bf16[4,56,512]{2,1,0:T(8,128)(2,1)S(1)}, bf16[4,24,512]{2,1,0:T(8,128)(2,1)S(1)}) custom-call(bf16[4,56,512]{2,1,0:T(8,128)(2,1)S(1)} %collective-permute-done.refs_0_.refs_1_, ...), custom_call_target="tpu_custom_call" | custom-call | flops 5000000000 | bytes 8369280 | tf_op jit(solution)/shard_map/pallas_call | solution.py:208
  42.5 0.1 collective-permute-start.5
  42.5 1.5 %collective-permute-start.3 = (bf16[4,56,512]{2,1,0:T(8,128)(2,1)S(1)}, bf16[4,56,512]{2,1,0:T(8,128)(2,1)S(1)}, u32[]{:S(2)}, u32[]{:S(2)}) collective-permute-start(bf16[4,56,512]{2,1,0:T(8,128)(2,1)S(1)} %get-tuple-element.22), channel_id=1, source_target_pairs={{1,0},{2,1},{3,2},{4,3},{5,4},{6,5},{7,6},{8,7},{9,8},{10,9},{11,1... | collective-permute-start | bytes 688136 | tf_op jit(solution)/shard_map/ppermute | solution.py:361
  44.0 0.0 copy-start.14
  44.0 0.0 copy-start.15
  44.1 0.0 copy-start.16
  44.1 0.0 copy-start.17
  44.1 0.0 copy-start.18
  44.1 0.0 copy-start.19
  44.1 0.1 collective-permute-start.4
  44.2 6.6 %shard_map.400.refs_10_ = bf16[4,72,512]{2,1,0:T(8,128)(2,1)S(1)} custom-call(bf16[4,24,512]{2,1,0:T(8,128)(2,1)S(1)} %collective-permute-done.2.refs_0_, bf16[4,56,512]{2,1,0:T(8,128)(2,1)S(1)} %collective-permute-done.refs_0_.refs_1_, bf16[4,56,512]{2,1,0:T(8,128)(2,1)S(1)} %collective-permute-done.1.refs_1_.refs_2_, bf16[4,288,512]{2,1,0:T(8,128)(2,1)S(1)} %bitcast.4, ...), custom_call_target="tpu_custom_call" | custom-call | flops 2500000000 | bytes 8098944 | tf_op jit(solution)/shard_map/pallas_call | solution.py:208
  50.9 1.7 %collective-permute-done.4.refs_14_ = bf16[4,56,512]{2,1,0:T(8,128)(2,1)S(1)} collective-permute-done((bf16[4,56,512]{2,1,0:T(8,128)(2,1)S(1)}, bf16[4,56,512]{2,1,0:T(8,128)(2,1)S(1)}, u32[]{:S(2)}, u32[]{:S(2)}) %collective-permute-start.4) | collective-permute-done | bytes 229408 | tf_op jit(solution)/shard_map/ppermute | solution.py:361
  52.6 0.0 copy-start.2
  52.6 14.0 %shard_map.401 = (bf16[72,1024]{1,0:T(8,128)(2,1)S(1)}, bf16[72,1024]{1,0:T(8,128)(2,1)S(1)}, bf16[72,1024]{1,0:T(8,128)(2,1)S(1)}, bf16[72,1024]{1,0:T(8,128)(2,1)S(1)}) custom-call(bf16[2048,1024]{1,0:T(8,128)(2,1)S(1)} %copy-done.6, bf16[1024,3072]{1,0:T(8,128)(2,1)} %refs_1_.4, bf16[1024,1024]{1,0:T(8,128)(2,1)S(1)} %copy-done.9, ...), custom_call_target="tpu_custom_call" | custom-call | flops 5000000000 | bytes 14739456 | tf_op jit(solution)/shard_map/pallas_call | solution.py:208
  66.6 0.1 collective-permute-start.6
  66.7 1.3 %collective-permute-start.7 = (bf16[72,1024]{1,0:T(8,128)(2,1)S(1)}, bf16[72,1024]{1,0:T(8,128)(2,1)S(1)}, u32[]{:S(2)}, u32[]{:S(2)}) collective-permute-start(bf16[72,1024]{1,0:T(8,128)(2,1)S(1)} %get-tuple-element.27), channel_id=1, source_target_pairs={{112,0},{113,1},{114,2},{115,3},{116,4},{117,5},{118,6},{119,7},{1... | collective-permute-start | bytes 442376 | tf_op jit(solution)/shard_map/ppermute | solution.py:361
  68.0 2.3 %collective-permute-start.8 = (bf16[72,1024]{1,0:T(8,128)(2,1)S(1)}, bf16[72,1024]{1,0:T(8,128)(2,1)S(1)}, u32[]{:S(2)}, u32[]{:S(2)}) collective-permute-start(bf16[72,1024]{1,0:T(8,128)(2,1)S(1)} %get-tuple-element.28), channel_id=1, source_target_pairs={{127,0},{112,1},{113,2},{114,3},{115,4},{116,5},{117,6},{118,7},{1... | collective-permute-start | bytes 442376 | tf_op jit(solution)/shard_map/ppermute | solution.py:361
  70.3 8.3 %collective-permute-done.6.refs_1_ = bf16[72,1024]{1,0:T(8,128)(2,1)S(1)} collective-permute-done((bf16[72,1024]{1,0:T(8,128)(2,1)S(1)}, bf16[72,1024]{1,0:T(8,128)(2,1)S(1)}, u32[]{:S(2)}, u32[]{:S(2)}) %collective-permute-start.6) | collective-permute-done | bytes 147488 | tf_op jit(solution)/shard_map/ppermute | solution.py:361
  78.6 1.9 %collective-permute-done.8.refs_3_ = bf16[72,1024]{1,0:T(8,128)(2,1)S(1)} collective-permute-done((bf16[72,1024]{1,0:T(8,128)(2,1)S(1)}, bf16[72,1024]{1,0:T(8,128)(2,1)S(1)}, u32[]{:S(2)}, u32[]{:S(2)}) %collective-permute-start.8) | collective-permute-done | bytes 147488 | tf_op jit(solution)/shard_map/ppermute | solution.py:361
  80.5 0.9 %shard_map.402 = bf16[4,6,12,1024]{3,2,1,0:T(8,128)(2,1)S(1)} custom-call(bf16[72,1024]{1,0:T(8,128)(2,1)S(1)} %get-tuple-element.25.refs_0_, bf16[72,1024]{1,0:T(8,128)(2,1)S(1)} %collective-permute-done.6.refs_1_, bf16[72,1024]{1,0:T(8,128)(2,1)S(1)} %collective-permute-done.7.refs_2_, bf16[72,1024]{1,0:T(8,128)(2,1)S(1)} %collective-permute-done.8.refs_3_, ...), custom_call_target="tpu_custom_call" | custom-call | bytes 811008 | tf_op jit(solution)/shard_map/pallas_call | solution.py:208
  81.5 1.3 %copy.44 = bf16[4,6,12,1024]{3,0,2,1:T(4,128)(2,1)} copy(bf16[4,6,12,1024]{3,2,1,0:T(8,128)(2,1)S(1)} %shard_map.402) | data formatting | bytes 1179648 | tf_op jit(solution)/shard_map/pallas_call | solution.py:208
  (51 shorter events, 0.1 us)
Async XLA Ops:
  0.0 1.3 %copy-start = (bf16[4,12,24,512]{3,2,1,0:T(8,128)(2,1)S(1)}, bf16[4,12,24,512]{3,2,1,0:T(8,128)(2,1)}, u32[]{:S(2)}) copy-start(bf16[4,12,24,512]{3,2,1,0:T(8,128)(2,1)} %param.43) | copy-start | bytes 3538948
  1.3 0.8 copy-start.3
  2.1 0.8 copy-start.4
  2.8 0.7 copy-start.5
  4.4 39.8 %collective-permute-start.2 = (bf16[4,24,512]{2,1,0:T(8,128)(2,1)S(1)}, bf16[4,24,512]{2,1,0:T(8,128)(2,1)S(1)}, u32[]{:S(2)}, u32[]{:S(2)}) collective-permute-start(bf16[4,24,512]{2,1,0:T(8,128)(2,1)S(1)} %get-tuple-element.21), channel_id=1, source_target_pairs={{17,0},{18,1},{19,2},{20,3},{21,4},{22,5},{23,6},{24,7},{25,8},{26... | collective-permute-start | bytes 294920 | tf_op jit(solution)/shard_map/ppermute | solution.py:361
  12.6 16.5 %collective-permute-start = (bf16[4,56,512]{2,1,0:T(8,128)(2,1)S(1)}, bf16[4,56,512]{2,1,0:T(8,128)(2,1)S(1)}, u32[]{:S(2)}, u32[]{:S(2)}) collective-permute-start(bf16[4,56,512]{2,1,0:T(8,128)(2,1)S(1)} %get-tuple-element.17), channel_id=1, source_target_pairs={{16,0},{17,1},{18,2},{19,3},{20,4},{21,5},{22,6},{23,7},{24,8},{25... | collective-permute-start | bytes 688136 | tf_op jit(solution)/shard_map/ppermute | solution.py:361
  13.7 15.4 %collective-permute-start.1 = (bf16[4,56,512]{2,1,0:T(8,128)(2,1)S(1)}, bf16[4,56,512]{2,1,0:T(8,128)(2,1)S(1)}, u32[]{:S(2)}, u32[]{:S(2)}) collective-permute-start(bf16[4,56,512]{2,1,0:T(8,128)(2,1)S(1)} %get-tuple-element.18), channel_id=1, source_target_pairs={{1,0},{2,1},{3,2},{4,3},{5,4},{6,5},{7,6},{8,7},{9,8},{10,9},{11,1... | collective-permute-start | bytes 688136 | tf_op jit(solution)/shard_map/ppermute | solution.py:361
  14.9 1.3 %copy-start.1 = (bf16[4,12,24,512]{3,2,1,0:T(8,128)(2,1)S(1)}, bf16[4,12,24,512]{3,2,1,0:T(8,128)(2,1)}, u32[]{:S(2)}) copy-start(bf16[4,12,24,512]{3,2,1,0:T(8,128)(2,1)} %param.43) | copy-start | bytes 3538948
  16.2 1.6 %copy-start.7 = (bf16[512,2048]{1,0:T(8,128)(2,1)S(1)}, bf16[512,2048]{1,0:T(8,128)(2,1)}, u32[]{:S(2)}) copy-start(bf16[512,2048]{1,0:T(8,128)(2,1)} %refs_6_.3) | copy-start | bytes 6291460
  17.8 1.6 %copy-start.8 = (bf16[2048,512]{1,0:T(8,128)(2,1)S(1)}, bf16[2048,512]{1,0:T(8,128)(2,1)}, u32[]{:S(2)}) copy-start(bf16[2048,512]{1,0:T(8,128)(2,1)} %refs_7_.3) | copy-start | bytes 6291460
  19.4 1.4 %copy-start.10 = (bf16[512,1536]{1,0:T(8,128)(2,1)S(1)}, bf16[512,1536]{1,0:T(8,128)(2,1)}, u32[]{:S(2)}) copy-start(bf16[512,1536]{1,0:T(8,128)(2,1)} %refs_4_.6) | copy-start | bytes 4718596
  20.8 1.0 %copy-start.11 = (bf16[512,512]{1,0:T(8,128)(2,1)S(1)}, bf16[512,512]{1,0:T(8,128)(2,1)}, u32[]{:S(2)}) copy-start(bf16[512,512]{1,0:T(8,128)(2,1)} %refs_5_.5) | copy-start | bytes 1572868
  21.8 0.8 copy-start.23
  22.6 6.5 %copy-start.21 = (bf16[72,288]{1,0:T(8,128)(2,1)S(1)}, bf16[72,288]{1,0:T(8,128)(2,1)}, u32[]{:S(2)}) copy-start(bf16[72,288]{1,0:T(8,128)(2,1)} %constant.64.clone.refs_9_) | copy-start | bytes 124420
  22.6 6.5 %copy-start.22 = (bf16[72,288]{1,0:T(8,128)(2,1)S(1)}, bf16[72,288]{1,0:T(8,128)(2,1)}, u32[]{:S(2)}) copy-start(bf16[72,288]{1,0:T(8,128)(2,1)} %constant.62.clone.refs_7_) | copy-start | bytes 124420
  22.6 6.5 %copy-start.27 = (bf16[72,56]{1,0:T(8,128)(2,1)S(1)}, bf16[72,56]{1,0:T(8,128)(2,1)}, u32[]{:S(2)}) copy-start(bf16[72,56]{1,0:T(8,128)(2,1)} %constant.65.clone.refs_10_) | copy-start | bytes 24196
  22.6 6.5 %copy-start.28 = (bf16[72,56]{1,0:T(8,128)(2,1)S(1)}, bf16[72,56]{1,0:T(8,128)(2,1)}, u32[]{:S(2)}) copy-start(bf16[72,56]{1,0:T(8,128)(2,1)} %constant.63.clone.refs_8_) | copy-start | bytes 24196
  22.6 6.5 %copy-start.29 = (bf16[56,72]{1,0:T(8,128)(2,1)S(1)}, bf16[56,72]{1,0:T(8,128)(2,1)}, u32[]{:S(2)}) copy-start(bf16[56,72]{1,0:T(8,128)(2,1)} %constant.73.clone.refs_19_) | copy-start | bytes 24196
  22.7 6.5 %copy-start.30 = (bf16[56,72]{1,0:T(8,128)(2,1)S(1)}, bf16[56,72]{1,0:T(8,128)(2,1)}, u32[]{:S(2)}) copy-start(bf16[56,72]{1,0:T(8,128)(2,1)} %constant.72.clone.refs_18_) | copy-start | bytes 24196
  22.7 6.5 %copy-start.31 = (bf16[56,72]{1,0:T(8,128)(2,1)S(1)}, bf16[56,72]{1,0:T(8,128)(2,1)}, u32[]{:S(2)}) copy-start(bf16[56,72]{1,0:T(8,128)(2,1)} %constant.70.clone.refs_15_) | copy-start | bytes 24196
  22.7 6.5 %copy-start.32 = (bf16[56,72]{1,0:T(8,128)(2,1)S(1)}, bf16[56,72]{1,0:T(8,128)(2,1)}, u32[]{:S(2)}) copy-start(bf16[56,72]{1,0:T(8,128)(2,1)} %constant.69.clone.refs_14_) | copy-start | bytes 24196
  22.7 6.5 %copy-start.33 = (bf16[24,72]{1,0:T(8,128)(2,1)S(1)}, bf16[24,72]{1,0:T(8,128)(2,1)}, u32[]{:S(2)}) copy-start(bf16[24,72]{1,0:T(8,128)(2,1)} %constant.71.clone.refs_16_) | copy-start | bytes 10372
  22.7 6.5 %copy-start.34 = (f32[1,1152]{1,0:T(1,128)S(1)}, f32[1,1152]{1,0:T(1,128)}, u32[]{:S(2)}) copy-start(f32[1,1152]{1,0:T(1,128)} %constant.66.clone.refs_11_.refs_12_.refs_18_) | copy-start | bytes 13828
  22.7 6.5 %copy-start.35 = (f32[1,640]{1,0:T(1,128)S(1)}, f32[1,640]{1,0:T(1,128)}, u32[]{:S(2)}) copy-start(f32[1,640]{1,0:T(1,128)} %constant.68.clone.refs_13_.refs_14_.refs_20_) | copy-start | bytes 7684
  22.7 6.5 %copy-start.36 = (f32[1,640]{1,0:T(1,128)S(1)}, f32[1,640]{1,0:T(1,128)}, u32[]{:S(2)}) copy-start(f32[1,640]{1,0:T(1,128)} %constant.67.clone.refs_12_.refs_13_.refs_19_) | copy-start | bytes 7684
  29.1 15.1 %copy-start.20 = (bf16[72,288]{1,0:T(8,128)(2,1)S(1)}, bf16[72,288]{1,0:T(8,128)(2,1)}, u32[]{:S(2)}) copy-start(bf16[72,288]{1,0:T(8,128)(2,1)} %constant.74.clone.refs_8_) | copy-start | bytes 124420
  29.1 15.1 %copy-start.24 = (bf16[72,24]{1,0:T(8,128)(2,1)S(1)}, bf16[72,24]{1,0:T(8,128)(2,1)}, u32[]{:S(2)}) copy-start(bf16[72,24]{1,0:T(8,128)(2,1)} %constant.77.clone.refs_11_) | copy-start | bytes 10372
  29.1 15.1 %copy-start.25 = (bf16[72,56]{1,0:T(8,128)(2,1)S(1)}, bf16[72,56]{1,0:T(8,128)(2,1)}, u32[]{:S(2)}) copy-start(bf16[72,56]{1,0:T(8,128)(2,1)} %constant.76.clone.refs_10_) | copy-start | bytes 24196
  29.1 15.1 %copy-start.26 = (bf16[72,56]{1,0:T(8,128)(2,1)S(1)}, bf16[72,56]{1,0:T(8,128)(2,1)}, u32[]{:S(2)}) copy-start(bf16[72,56]{1,0:T(8,128)(2,1)} %constant.75.clone.refs_9_) | copy-start | bytes 24196
  42.5 8.4 %collective-permute-start.5 = (bf16[4,24,512]{2,1,0:T(8,128)(2,1)S(1)}, bf16[4,24,512]{2,1,0:T(8,128)(2,1)S(1)}, u32[]{:S(2)}, u32[]{:S(2)}) collective-permute-start(bf16[4,24,512]{2,1,0:T(8,128)(2,1)S(1)} %get-tuple-element.24), channel_id=1, source_target_pairs={{17,0},{18,1},{19,2},{20,3},{21,4},{22,5},{23,6},{24,7},{25,8},{26... | collective-permute-start | bytes 294920 | tf_op jit(solution)/shard_map/ppermute | solution.py:361
  42.5 8.3 %collective-permute-start.3 = (bf16[4,56,512]{2,1,0:T(8,128)(2,1)S(1)}, bf16[4,56,512]{2,1,0:T(8,128)(2,1)S(1)}, u32[]{:S(2)}, u32[]{:S(2)}) collective-permute-start(bf16[4,56,512]{2,1,0:T(8,128)(2,1)S(1)} %get-tuple-element.22), channel_id=1, source_target_pairs={{1,0},{2,1},{3,2},{4,3},{5,4},{6,5},{7,6},{8,7},{9,8},{10,9},{11,1... | collective-permute-start | bytes 688136 | tf_op jit(solution)/shard_map/ppermute | solution.py:361
  44.0 8.5 %copy-start.6 = (bf16[2048,1024]{1,0:T(8,128)(2,1)S(1)}, bf16[2048,1024]{1,0:T(8,128)(2,1)}, u32[]{:S(2)}) copy-start(bf16[2048,1024]{1,0:T(8,128)(2,1)} %refs_0_.1) | copy-start | bytes 12582916
  44.0 8.5 %copy-start.9 = (bf16[1024,1024]{1,0:T(8,128)(2,1)S(1)}, bf16[1024,1024]{1,0:T(8,128)(2,1)}, u32[]{:S(2)}) copy-start(bf16[1024,1024]{1,0:T(8,128)(2,1)} %refs_2_.4) | copy-start | bytes 6291460
  44.0 8.5 %copy-start.12 = (bf16[288,288]{1,0:T(8,128)(2,1)S(1)}, bf16[288,288]{1,0:T(8,128)(2,1)}, u32[]{:S(2)}) copy-start(bf16[288,288]{1,0:T(8,128)(2,1)} %constant.78.clone.refs_3_) | copy-start | bytes 497668
  44.0 8.5 %copy-start.13 = (bf16[288,24]{1,0:T(8,128)(2,1)S(1)}, bf16[288,24]{1,0:T(8,128)(2,1)}, u32[]{:S(2)}) copy-start(bf16[288,24]{1,0:T(8,128)(2,1)} %constant.85.clone.refs_17_) | copy-start | bytes 41476
  44.0 8.5 %copy-start.14 = (bf16[288,56]{1,0:T(8,128)(2,1)S(1)}, bf16[288,56]{1,0:T(8,128)(2,1)}, u32[]{:S(2)}) copy-start(bf16[288,56]{1,0:T(8,128)(2,1)} %constant.84.clone.refs_15_) | copy-start | bytes 96772
  44.0 8.5 %copy-start.15 = (bf16[288,56]{1,0:T(8,128)(2,1)S(1)}, bf16[288,56]{1,0:T(8,128)(2,1)}, u32[]{:S(2)}) copy-start(bf16[288,56]{1,0:T(8,128)(2,1)} %constant.83.clone.refs_13_) | copy-start | bytes 96772
  44.1 8.5 %copy-start.16 = (bf16[288,72]{1,0:T(8,128)(2,1)S(1)}, bf16[288,72]{1,0:T(8,128)(2,1)}, u32[]{:S(2)}) copy-start(bf16[288,72]{1,0:T(8,128)(2,1)} %constant.82.clone.refs_11_) | copy-start | bytes 124420
  44.1 8.5 %copy-start.17 = (bf16[288,72]{1,0:T(8,128)(2,1)S(1)}, bf16[288,72]{1,0:T(8,128)(2,1)}, u32[]{:S(2)}) copy-start(bf16[288,72]{1,0:T(8,128)(2,1)} %constant.81.clone.refs_9_) | copy-start | bytes 124420
  44.1 8.5 %copy-start.18 = (bf16[288,72]{1,0:T(8,128)(2,1)S(1)}, bf16[288,72]{1,0:T(8,128)(2,1)}, u32[]{:S(2)}) copy-start(bf16[288,72]{1,0:T(8,128)(2,1)} %constant.80.clone.refs_7_) | copy-start | bytes 124420
  44.1 8.5 %copy-start.19 = (bf16[288,72]{1,0:T(8,128)(2,1)S(1)}, bf16[288,72]{1,0:T(8,128)(2,1)}, u32[]{:S(2)}) copy-start(bf16[288,72]{1,0:T(8,128)(2,1)} %constant.79.clone.refs_5_) | copy-start | bytes 124420
  44.1 8.4 %collective-permute-start.4 = (bf16[4,56,512]{2,1,0:T(8,128)(2,1)S(1)}, bf16[4,56,512]{2,1,0:T(8,128)(2,1)S(1)}, u32[]{:S(2)}, u32[]{:S(2)}) collective-permute-start(bf16[4,56,512]{2,1,0:T(8,128)(2,1)S(1)} %get-tuple-element.23), channel_id=1, source_target_pairs={{16,0},{17,1},{18,2},{19,3},{20,4},{21,5},{22,6},{23,7},{24,8},{25... | collective-permute-start | bytes 688136 | tf_op jit(solution)/shard_map/ppermute | solution.py:361
  52.6 27.9 %copy-start.2 = (bf16[4,384,72]{2,1,0:T(8,128)(2,1)S(1)}, bf16[4,384,72]{2,1,0:T(8,128)(2,1)}, u32[]{:S(2)}) copy-start(bf16[4,384,72]{2,1,0:T(8,128)(2,1)} %constant.86.clone.refs_4_) | copy-start | bytes 663556
  66.6 12.0 %collective-permute-start.6 = (bf16[72,1024]{1,0:T(8,128)(2,1)S(1)}, bf16[72,1024]{1,0:T(8,128)(2,1)S(1)}, u32[]{:S(2)}, u32[]{:S(2)}) collective-permute-start(bf16[72,1024]{1,0:T(8,128)(2,1)S(1)} %get-tuple-element.26), channel_id=1, source_target_pairs={{15,0},{0,1},{1,2},{2,3},{3,4},{4,5},{5,6},{6,7},{7,8},{8,9},{9,10... | collective-permute-start | bytes 442376 | tf_op jit(solution)/shard_map/ppermute | solution.py:361
  66.7 11.9 %collective-permute-start.7 = (bf16[72,1024]{1,0:T(8,128)(2,1)S(1)}, bf16[72,1024]{1,0:T(8,128)(2,1)S(1)}, u32[]{:S(2)}, u32[]{:S(2)}) collective-permute-start(bf16[72,1024]{1,0:T(8,128)(2,1)S(1)} %get-tuple-element.27), channel_id=1, source_target_pairs={{112,0},{113,1},{114,2},{115,3},{116,4},{117,5},{118,6},{119,7},{1... | collective-permute-start | bytes 442376 | tf_op jit(solution)/shard_map/ppermute | solution.py:361
  68.0 12.6 %collective-permute-start.8 = (bf16[72,1024]{1,0:T(8,128)(2,1)S(1)}, bf16[72,1024]{1,0:T(8,128)(2,1)S(1)}, u32[]{:S(2)}, u32[]{:S(2)}) collective-permute-start(bf16[72,1024]{1,0:T(8,128)(2,1)S(1)} %get-tuple-element.28), channel_id=1, source_target_pairs={{127,0},{112,1},{113,2},{114,3},{115,4},{116,5},{117,6},{118,7},{1... | collective-permute-start | bytes 442376 | tf_op jit(solution)/shard_map/ppermute | solution.py:361

commit v2 on v1

v2 whole, which is shorter than its diff:
```python
import functools
import math

import jax
import jax.numpy as jnp
import numpy as np
from jax import lax
from jax.experimental import pallas as pl
from jax.experimental.pallas import tpu as pltpu
from jax.sharding import PartitionSpec as P

F32 = jnp.float32
BF16 = jnp.bfloat16
HEAD = 32
GROUP = 256
ORDER = (1, 2, 3, 0)
QUADS = ((0, 0), (0, 1), (1, 0), (1, 1))
EXP_SCALE = HEAD ** -0.5 * math.log2(math.e)
MIB = 1024 * 1024


def piece_of(i, j):
    if i >= 3 and j < 6:
        return "lon", (i - 3) * 6 + j
    if i < 3 and j >= 6:
        return "lat", i * 18 + j - 6
    if i < 3 and j < 6:
        return "both", i * 6 + j
    return None, 0


def source_of(i, j):
    i, j = i + 3, j + 6
    if i < 12 and j < 24:
        return "own", (i, j)
    return piece_of(i - 12 if i >= 12 else i, j - 24 if j >= 24 else j)


PIECE_ROWS = {"lon": 56, "lat": 56, "both": 24}


def first_send_tables():
    table, start = np.zeros((136, 288), np.float32), 0
    for name, rows in PIECE_ROWS.items():
        for i in range(12):
            for j in range(24):
                piece, at = piece_of(i, j)
                if piece == name:
                    table[start + at, i * 24 + j] = 1
        start += rows
    return table


OWN_ROWS = {"own0": 64, "own1": 144, "own2": 208}


def window_tables(quad):
    tables = {}
    for r in range(6):
        for c in range(12):
            name, at = source_of(quad[0] * 6 + r, quad[1] * 12 + c)
            if name == "own":
                row = at[0] * 24 + at[1]
                name = "own2" if quad[0] == 1 else "own1" if row >= 144 else "own0"
                at = row - OWN_ROWS[name]
            tables.setdefault(name, np.zeros((80, 80), np.float32))[r * 12 + c, at] = 1
    return tables


def second_send_tables(quad):
    tables = {}
    for r in range(6):
        for c in range(12):
            name, at = piece_of(quad[0] * 6 + r, quad[1] * 12 + c)
            if name is not None:
                tables.setdefault(name, np.zeros((80, 80), np.float32))[at, r * 12 + c] = 1
    return tables


def pair_tables():
    names = list(QUADS) + list(PIECE_ROWS)
    tables = np.zeros((7, 288, 72), np.float32)
    for i in range(12):
        for j in range(24):
            to = ((i % 2) * 2 + j % 2) * 72 + (i // 2) * 12 + j // 2
            name, at = source_of(i, j)
            if name == "own":
                name, at = (at[0] // 6, at[1] // 12), (at[0] % 6) * 12 + at[1] % 12
            tables[names.index(name), to, at] = 1
    return tables


def last_send_table():
    table = np.zeros((3, 288, 96), np.float32)
    for place, level in enumerate(ORDER):
        for i in range(6):
            for j in range(12):
                part = (i // 3) * 2 + j // 6
                to, at = part * 72 + level * 18 + (i % 3) * 6 + j % 6, place * 72 + i * 12 + j
                table[at // 96, to, at % 96] = 1
    return table


def last_tables():
    tables = np.zeros((4, 288, 72), np.float32)
    for part in range(4):
        for level in range(4):
            for i in range(3):
                for j in range(6):
                    row = i + 3 if part // 2 == 0 else i
                    col = j + 6 if part % 2 == 0 else j
                    tables[part, (row * 12 + col) * 4 + level, level * 18 + i * 6 + j] = 1
    return tables


def dot(a, b):
    return jnp.dot(a, b, preferred_element_type=F32)


def normalize(values):
    center = values - jnp.mean(values, -1, keepdims=True)
    spread = jnp.mean(center * center, -1, keepdims=True)
    return center * lax.rsqrt(spread + 1e-05)


def gelu(x):
    return 0.5 * x * (1.0 + lax.erf(x * 0.5**0.5))


def attend(q, k, v, bias):
    nq = q.shape[0]
    lane_head = lax.broadcasted_iota(jnp.int32, (1, GROUP), 1) // HEAD
    stacked = jnp.concatenate(
        [q * (lane_head == h).astype(BF16) for h in range(8)], axis=0
    )
    scores = lax.dot_general(k, stacked, (((1,), (1,)), ((), ())), preferred_element_type=F32)
    if bias is not None:
        scores = scores + bias
    expo = jnp.exp2((scores - jnp.max(scores, 0, keepdims=True)) * EXP_SCALE)
    weights = (expo * (1.0 / jnp.sum(expo, 0, keepdims=True))).astype(BF16)
    full = lax.dot_general(weights, v, (((0,), (0,)), ((), ())), preferred_element_type=F32)
    out = full[:nq]
    for h in range(1, 8):
        out = jnp.where(lane_head == h, full[h * nq : (h + 1) * nq], out)
    return out


def attend_tile(qkv, width, biases):
    both, low, high = biases
    rounded = qkv.astype(BF16)
    groups = []
    for g in range(width // GROUP):
        at = [slice(part * width + g * GROUP, part * width + (g + 1) * GROUP) for part in range(3)]
        pair = attend(*[rounded[:144, s] for s in at], both)
        third = attend(
            rounded[144:224, at[0]],
            qkv[144:216, at[1]].astype(BF16),
            qkv[144:216, at[2]].astype(BF16),
            low,
        )
        fourth = attend(
            rounded[208:288, at[0]],
            qkv[216:288, at[1]].astype(BF16),
            qkv[216:288, at[2]].astype(BF16),
            high,
        )
        groups.append(jnp.concatenate([pair, third[:72], fourth[8:]], axis=0).astype(BF16))
    return jnp.concatenate(groups, axis=1)


def fill_biases(biases):
    edge = lax.axis_index("lat") == lax.axis_size("lat") - 1
    large = jnp.where(edge, 5e29, 0.0).astype(F32)
    for bias, (start, period) in zip(biases, ((0, 144), (0, 80), (8, 80))):
        query = lax.rem(lax.broadcasted_iota(jnp.int32, (1, bias.shape[1]), 1), period) - start
        keys = lax.broadcasted_iota(jnp.int32, (bias.shape[0], 1), 0)
        sides = [
            jnp.where(jnp.where(place >= 72, place - 72, place) < 36, 1.0, -1.0)
            for place in (keys, query)
        ]
        bias[...] = (sides[0] * sides[1] - 1.0) * large


BIAS_SCRATCH = [
    pltpu.VMEM((144, 1152), F32),
    pltpu.VMEM((72, 640), F32),
    pltpu.VMEM((72, 640), F32),
]


def run(body, outs, ins, scratch=(), flops=0, limit=32):
    names, out_names = list(ins), list(outs)

    def kernel(*refs):
        first, last = len(names), len(names) + len(out_names)
        body(dict(zip(names, refs)), dict(zip(out_names, refs[first:last])), refs[last:])

    size = sum(math.prod(array.shape) * 2 for array in ins.values())
    results = pl.pallas_call(
        kernel,
        out_shape=[jax.ShapeDtypeStruct(shape, BF16) for shape in outs.values()],
        in_specs=[pl.BlockSpec(memory_space=pltpu.VMEM)] * len(names),
        out_specs=[pl.BlockSpec(memory_space=pltpu.VMEM)] * len(out_names),
        scratch_shapes=list(scratch),
        compiler_params=pltpu.CompilerParams(vmem_limit_bytes=limit * MIB),
        cost_estimate=pl.CostEstimate(flops=flops, bytes_accessed=size, transcendentals=0),
    )(*ins.values())
    return dict(zip(out_names, results))


def const(table):
    return jnp.asarray(table, BF16)


def split_first(x):
    def body(refs, outs, _):
        for level in range(4):
            rows = dot(refs["table"][...], refs["x"][level])
            start = 0
            for name, count in PIECE_ROWS.items():
                outs[name][level] = rows[start : start + count].astype(BF16)
                start += count

    return run(
        body,
        {name: (4, rows, 512) for name, rows in PIECE_ROWS.items()},
        {"table": const(first_send_tables()), "x": x},
        flops=10_000_000_000,
        limit=8,
    )


CHUNK = 512


def fine_quads(quads, sources, weights, blocks, emit):
    tables = {quad: window_tables(quad) for quad in quads}
    needed = sorted({name for quad in quads for name in tables[quad]})
    ins = {name: sources[name] for name in needed if name in PIECE_ROWS}
    ins |= {"own": sources["own"]} | weights
    stack, place = [], {}
    for quad in quads:
        for name, table in tables[quad].items():
            place[quad, name] = len(stack)
            stack.append(table)
    masked = any(quad[0] == 1 for quad in quads)
    outs = {quad: (4, 72, 512) for quad in quads}
    sends = {}
    if emit:
        for quad in QUADS:
            sends[quad] = second_send_tables(quad)
            for name, table in sends[quad].items():
                place["send", quad, name] = len(stack)
                stack.append(table)
            if quad in blocks and sends[quad]:
                ins["block", quad] = blocks[quad]
        outs |= {name: (4, rows, 512) for name, rows in PIECE_ROWS.items()}
    ins["table"] = const(np.stack(stack))

    def body(refs, outs, biases):
        if masked:
            fill_biases(biases)
        for quad in quads:
            levels = []
            for level in ORDER:
                total = None
                for name in tables[quad]:
                    if name in PIECE_ROWS:
                        source = refs[name][level]
                    else:
                        source = refs["own"][level, OWN_ROWS[name] : OWN_ROWS[name] + 80, :]
                    term = dot(refs["table"][place[quad, name], :72, : source.shape[0]], source)
                    total = term if total is None else total + term
                levels.append(total)
            tokens = jnp.concatenate(levels, axis=0)
            qkv = dot(normalize(tokens).astype(BF16), refs["qkv"][...])
            use = [bias[...] for bias in biases] if quad[0] == 1 else [None] * 3
            mixed = attend_tile(qkv, 512, use)
            hidden = (tokens + dot(mixed, refs["out"][...])).astype(BF16).astype(F32)
            normed = normalize(hidden).astype(BF16)
            total = hidden
            for at in range(0, 2048, CHUNK):
                inner = gelu(dot(normed, refs["up"][:, at : at + CHUNK])).astype(BF16)
                total = total + dot(inner, refs["down"][at : at + CHUNK, :])
            for at, level in enumerate(ORDER):
                outs[quad][level] = total[at * 72 : at * 72 + 72].astype(BF16)
        if emit:
            for name, rows in PIECE_ROWS.items():
                for level in range(4):
                    total = None
                    for quad in QUADS:
                        if name in sends[quad]:
                            block = outs[quad] if quad in outs else refs["block", quad]
                            table = refs["table"][place["send", quad, name], :rows, :72]
                            term = dot(table, block[level])
                            total = term if total is None else total + term
                    outs[name][level] = total.astype(BF16)

    return run(
        body, outs, ins, BIAS_SCRATCH if masked else (), flops=len(quads) * 2_500_000_000
    )


def coarse(blocks, pieces, merge, qkv_weight, out_weight):
    ins = {"table": const(pair_tables())}
    ins |= {"src%d" % at: array for at, array in enumerate([blocks[quad] for quad in QUADS])}
    ins |= {"src%d" % (4 + at): pieces[name] for at, name in enumerate(PIECE_ROWS)}
    ins |= {"merge": merge, "qkv": qkv_weight, "out": out_weight}
    ins |= {"last": const(last_send_table())}

    def body(refs, outs, biases):
        fill_biases(biases)
        rows = []
        for level in ORDER:
            total = None
            for at in range(7):
                source = refs["src%d" % at][level]
                term = dot(refs["table"][at, :, : source.shape[0]], source)
                total = term if total is None else total + term
            pairs = jnp.concatenate([total[72 * at : 72 * at + 72] for at in range(4)], axis=1)
            rows.append(normalize(pairs))
        pairs = jnp.concatenate(rows, axis=0).astype(BF16)
        merged = dot(pairs, refs["merge"][...]).astype(BF16).astype(F32)
        qkv = dot(normalize(merged).astype(BF16), refs["qkv"][...])
        mixed = attend_tile(qkv, 1024, [bias[...] for bias in biases])
        result = (merged + dot(mixed, refs["out"][...])).astype(BF16)
        parts = sum(dot(refs["last"][at], result[96 * at : 96 * at + 96]) for at in range(3))
        for part in range(4):
            outs[part][...] = parts[part * 72 : part * 72 + 72].astype(BF16)

    return run(
        body,
        {part: (72, 1024) for part in range(4)},
        ins,
        BIAS_SCRATCH,
        flops=5_000_000_000,
    )


def assemble(parts):
    def body(refs, outs, _):
        total = None
        for part in range(4):
            term = dot(refs["table"][part], refs[part][...])
            total = term if total is None else total + term
        for row in range(6):
            for col in range(12):
                at = (row * 12 + col) * 4
                outs["out"][row, col] = total[at : at + 4].astype(BF16)

    result = run(
        body,
        {"out": (6, 12, 4, 1024)},
        {"table": const(last_tables())} | dict(enumerate(parts)),
        limit=8,
    )["out"]
    return result.transpose(2, 0, 1, 3)


def receive(array, lat, lon):
    rows, cols = lax.axis_size("lat"), lax.axis_size("lon")
    pairs = [
        (((a + lat) % rows) * cols + (b + lon) % cols, a * cols + b)
        for a in range(rows)
        for b in range(cols)
    ]
    return lax.ppermute(array, ("lat", "lon"), pairs)


def shift(pieces):
    return {
        "lon": receive(pieces["lon"], 0, 1),
        "lat": receive(pieces["lat"], 1, 0),
        "both": receive(pieces["both"], 1, 1),
    }


def shards(fine, fine_qkv, fine_out, fine_up, fine_down, merge_weight, coarse_qkv, coarse_out):
    weights = {"qkv": fine_qkv, "out": fine_out, "up": fine_up, "down": fine_down}
    x = fine.reshape(4, 288, 512)
    sources = {"own": x} | shift(split_first(x))
    blocks = fine_quads(QUADS[:1], sources, weights, {}, False)
    second = fine_quads(QUADS[1:3], sources, weights, blocks, True)
    pieces = shift({name: second[name] for name in PIECE_ROWS})
    blocks |= {quad: second[quad] for quad in QUADS[1:3]}
    blocks |= fine_quads(QUADS[3:], sources, weights, {}, False)
    parts = coarse(blocks, pieces, merge_weight, coarse_qkv, coarse_out)
    moved = [parts[0], receive(parts[1], 0, -1), receive(parts[2], -1, 0), receive(parts[3], -1, -1)]
    return assemble(moved)


def solution(mesh):
    in_specs = (P(None, "lat", "lon", None), P(), P(), P(), P(), P(), P(), P())
    out_specs = P(None, "lat", "lon", None)
    return jax.shard_map(shards, mesh=mesh, in_specs=in_specs, out_specs=out_specs, check_vma=False)
```

time: 83.3 us -> 70.4 us (0.85)
  local copies, waits for them, and re-layouts: 12.7 us -> 2.24 us
  Pallas kernels: 41.8 us -> 33.9 us
  waiting for transfers between devices: 11.9 us -> 15.9 us
  starting transfers between devices: 15.8 us -> 18 us
    unnamed x74 -> x34, local copies, waits for them, and re-layouts: 11.4 us -> 2.24 us
    pallas_call x6, Pallas kernels: 41.8 us -> 33.9 us  [run(): pl.pallas_call(kernel, out_shape=[jax.ShapeDtypeStruct(shape, BF16) for s...]
    ppermute x9, waiting for transfers between devices: 11.9 us -> 15.9 us  [receive(): return lax.ppermute(array, ('lat', 'lon'), pairs)]
    ppermute x9, starting transfers between devices: 15.8 us -> 18 us  [receive(): return lax.ppermute(array, ('lat', 'lon'), pairs)]
    pallas_call x1 -> x0, local copies, waits for them, and re-layouts: 1.27 us -> none  [run(): pl.pallas_call(kernel, out_shape=[jax.ShapeDtypeStruct(shape, BF16) for s...]
  transfers between devices with their start and end apart: 9 -> 9, of which waited for: 3 -> 3; matrix products, arithmetic and copies ran while one was open for 0% -> 0% of each run, Pallas kernels for 32% -> 29%
where the time goes in v2:
time: 70.4 us; the launch traced here: 70.2 us
  Pallas kernels  33.9 us (48%)
  starting transfers between devices  18 us (26%)
  waiting for transfers between devices  15.9 us (23%)
  local copies, waits for them, and re-layouts  2.24 us (3%)
    pallas_call x6, Pallas kernels, run(): pl.pallas_call(kernel, out_shape=[jax.ShapeDtypeStruct(shape, BF16) for s...  33.9 us
    ppermute x9, starting transfers between devices, receive(): return lax.ppermute(array, ('lat', 'lon'), pairs)  18 us
    ppermute x9, waiting for transfers between devices, receive(): return lax.ppermute(array, ('lat', 'lon'), pairs)  15.9 us
    unnamed x34, local copies, waits for them, and re-layouts  2.24 us
  transfers between devices with their start and end apart: 9, of which 3 were waited for; matrix products, arithmetic and copies ran while one was open for 0% of the time, Pallas kernels for 29%

profile of v2, /device:TPU:0, one launch (start us, length us, event | category | flops | bytes accessed | tf_op | source)
XLA Modules:
  0.0 70.2 jit_solution(7299567550369588057)
XLA Ops:
  0.0 1.3 %copy-done.6 = bf16[4,12,24,512]{3,2,1,0:T(8,128)(2,1)S(1)} copy-done((bf16[4,12,24,512]{3,2,1,0:T(8,128)(2,1)S(1)}, bf16[4,12,24,512]{3,2,1,0:T(8,128)(2,1)}, u32[]{:S(2)}) %copy-start.6) | copy-done | bytes 1179672
  1.3 0.9 %copy-done.12 = bf16[136,288]{1,0:T(8,128)(2,1)S(1)} copy-done((bf16[136,288]{1,0:T(8,128)(2,1)S(1)}, bf16[136,288]{1,0:T(8,128)(2,1)}, u32[]{:S(2)}) %copy-start.12) | copy-done | bytes 78360
  2.2 0.0 copy-start.8
  2.2 0.0 copy-start.14
  2.2 0.5 shard_map.146
  2.7 8.3 %collective-permute-start.2 = (bf16[4,24,512]{2,1,0:T(8,128)(2,1)S(1)}, bf16[4,24,512]{2,1,0:T(8,128)(2,1)S(1)}, u32[]{:S(2)}, u32[]{:S(2)}) collective-permute-start(bf16[4,24,512]{2,1,0:T(8,128)(2,1)S(1)} %get-tuple-element.21), channel_id=1, source_target_pairs={{17,0},{18,1},{19,2},{20,3},{21,4},{22,5},{23,6},{24,7},{25,8},{26... | collective-permute-start | bytes 294920 | tf_op jit(solution)/shard_map/ppermute | solution.py:367
  11.0 1.1 %collective-permute-start = (bf16[4,56,512]{2,1,0:T(8,128)(2,1)S(1)}, bf16[4,56,512]{2,1,0:T(8,128)(2,1)S(1)}, u32[]{:S(2)}, u32[]{:S(2)}) collective-permute-start(bf16[4,56,512]{2,1,0:T(8,128)(2,1)S(1)} %get-tuple-element.17), channel_id=1, source_target_pairs={{16,0},{17,1},{18,2},{19,3},{20,4},{21,5},{22,6},{23,7},{24,8},{25... | collective-permute-start | bytes 688136 | tf_op jit(solution)/shard_map/ppermute | solution.py:367
  12.1 1.2 %collective-permute-start.1 = (bf16[4,56,512]{2,1,0:T(8,128)(2,1)S(1)}, bf16[4,56,512]{2,1,0:T(8,128)(2,1)S(1)}, u32[]{:S(2)}, u32[]{:S(2)}) collective-permute-start(bf16[4,56,512]{2,1,0:T(8,128)(2,1)S(1)} %get-tuple-element.18), channel_id=1, source_target_pairs={{1,0},{2,1},{3,2},{4,3},{5,4},{6,5},{7,6},{8,7},{9,8},{10,9},{11,1... | collective-permute-start | bytes 688136 | tf_op jit(solution)/shard_map/ppermute | solution.py:367
  13.2 0.0 copy-done.2
  13.2 0.0 copy-done.3
  13.2 0.0 copy-done.5
  13.2 0.0 copy-done.7
  13.2 0.0 copy-done.8
  13.3 0.0 copy-done.14
  13.3 0.0 slice-start
  13.3 5.0 %shard_map.145.refs_7_.refs_1_ = bf16[4,72,512]{2,1,0:T(8,128)(2,1)S(1)} custom-call(bf16[4,288,512]{2,1,0:T(8,128)(2,1)S(1)} %bitcast.5, bf16[512,1536]{1,0:T(8,128)(2,1)S(1)} %copy-done.5, bf16[512,512]{1,0:T(8,128)(2,1)S(1)} %copy-done.8, bf16[512,2048]{1,0:T(8,128)(2,1)S(1)} %copy-done.2, bf16[2048,512]{1,0:T(8,128)(2,1)S(1)} %copy-done.3, ...), custom_call_target="tpu_custom_call" | custom-call | flops 2500000000 | bytes 7496704 | tf_op jit(solution)/shard_map/pallas_call | solution.py:199
  18.3 0.0 copy-start.13
  18.3 0.0 slice-start.1
  18.3 0.0 collective-permute-done.refs_0_.refs_1_
  18.3 0.0 collective-permute-done.1.refs_1_.refs_2_
  18.3 0.0 copy-done.11
  18.3 10.5 %shard_map.147 = (bf16[4,72,512]{2,1,0:T(8,128)(2,1)S(1)}, bf16[4,72,512]{2,1,0:T(8,128)(2,1)S(1)}, bf16[4,56,512]{2,1,0:T(8,128)(2,1)S(1)}, bf16[4,56,512]{2,1,0:T(8,128)(2,1)S(1)}, bf16[4,24,512]{2,1,0:T(8,128)(2,1)S(1)}) custom-call(bf16[4,56,512]{2,1,0:T(8,128)(2,1)S(1)} %collective-permute-done.refs_0_.refs_1_, ...), custom_call_target="tpu_custom_call" | custom-call | flops 5000000000 | bytes 8352768 | tf_op jit(solution)/shard_map/pallas_call | solution.py:199
  28.8 6.2 %collective-permute-start.5 = (bf16[4,24,512]{2,1,0:T(8,128)(2,1)S(1)}, bf16[4,24,512]{2,1,0:T(8,128)(2,1)S(1)}, u32[]{:S(2)}, u32[]{:S(2)}) collective-permute-start(bf16[4,24,512]{2,1,0:T(8,128)(2,1)S(1)} %get-tuple-element.24), channel_id=1, source_target_pairs={{17,0},{18,1},{19,2},{20,3},{21,4},{22,5},{23,6},{24,7},{25,8},{26... | collective-permute-start | bytes 294920 | tf_op jit(solution)/shard_map/ppermute | solution.py:367
  35.0 0.0 collective-permute-start.3
  35.0 0.0 copy-start.10
  35.0 1.0 %collective-permute-start.4 = (bf16[4,56,512]{2,1,0:T(8,128)(2,1)S(1)}, bf16[4,56,512]{2,1,0:T(8,128)(2,1)S(1)}, u32[]{:S(2)}, u32[]{:S(2)}) collective-permute-start(bf16[4,56,512]{2,1,0:T(8,128)(2,1)S(1)} %get-tuple-element.23), channel_id=1, source_target_pairs={{16,0},{17,1},{18,2},{19,3},{20,4},{21,5},{22,6},{23,7},{24,8},{25... | collective-permute-start | bytes 688136 | tf_op jit(solution)/shard_map/ppermute | solution.py:367
  36.0 0.0 collective-permute-done.2.refs_0_
  36.0 0.0 copy-done.13
  36.0 5.2 %shard_map.148.refs_4_ = bf16[4,72,512]{2,1,0:T(8,128)(2,1)S(1)} custom-call(bf16[4,24,512]{2,1,0:T(8,128)(2,1)S(1)} %collective-permute-done.2.refs_0_, bf16[4,56,512]{2,1,0:T(8,128)(2,1)S(1)} %collective-permute-done.refs_0_.refs_1_, bf16[4,56,512]{2,1,0:T(8,128)(2,1)S(1)} %collective-permute-done.1.refs_1_.refs_2_, bf16[4,288,512]{2,1,0:T(8,128)(2,1)S(1)} %bitcast.7, ...), custom_call_target="tpu_custom_call" | custom-call | flops 2500000000 | bytes 8079360 | tf_op jit(solution)/shard_map/pallas_call | solution.py:199
  41.2 0.0 collective-permute-done.5.refs_7_
  41.2 0.0 collective-permute-done.3.refs_5_
  41.2 1.9 %collective-permute-done.4.refs_6_ = bf16[4,56,512]{2,1,0:T(8,128)(2,1)S(1)} collective-permute-done((bf16[4,56,512]{2,1,0:T(8,128)(2,1)S(1)}, bf16[4,56,512]{2,1,0:T(8,128)(2,1)S(1)}, u32[]{:S(2)}, u32[]{:S(2)}) %collective-permute-start.4) | collective-permute-done | bytes 229408 | tf_op jit(solution)/shard_map/ppermute | solution.py:367
  43.1 0.0 slice-done
  43.1 0.0 slice-done.1
  43.1 0.0 copy-done.1
  43.1 0.0 copy-done.4
  43.1 0.0 copy-done.9
  43.1 0.0 copy-done.10
  43.1 0.0 copy-start
  43.2 11.2 %shard_map.149 = (bf16[72,1024]{1,0:T(8,128)(2,1)S(1)}, bf16[72,1024]{1,0:T(8,128)(2,1)S(1)}, bf16[72,1024]{1,0:T(8,128)(2,1)S(1)}, bf16[72,1024]{1,0:T(8,128)(2,1)S(1)}) custom-call(bf16[7,288,72]{2,1,0:T(8,128)(2,1)S(1)} %copy-done.9, bf16[4,72,512]{2,1,0:T(8,128)(2,1)S(1)} %shard_map.145.refs_7_.refs_1_, ...), custom_call_target="tpu_custom_call" | custom-call | flops 5000000000 | bytes 14775808 | tf_op jit(solution)/shard_map/pallas_call | solution.py:199
  54.4 0.1 collective-permute-start.6
  54.5 0.2 collective-permute-start.7
  54.6 0.0 collective-permute-start.8
  54.6 12.6 %collective-permute-done.6.refs_2_ = bf16[72,1024]{1,0:T(8,128)(2,1)S(1)} collective-permute-done((bf16[72,1024]{1,0:T(8,128)(2,1)S(1)}, bf16[72,1024]{1,0:T(8,128)(2,1)S(1)}, u32[]{:S(2)}, u32[]{:S(2)}) %collective-permute-start.6) | collective-permute-done | bytes 147488 | tf_op jit(solution)/shard_map/ppermute | solution.py:367
  67.3 0.0 collective-permute-done.7.refs_3_
  67.3 1.4 %collective-permute-done.8.refs_4_ = bf16[72,1024]{1,0:T(8,128)(2,1)S(1)} collective-permute-done((bf16[72,1024]{1,0:T(8,128)(2,1)S(1)}, bf16[72,1024]{1,0:T(8,128)(2,1)S(1)}, u32[]{:S(2)}, u32[]{:S(2)}) %collective-permute-start.8) | collective-permute-done | bytes 147488 | tf_op jit(solution)/shard_map/ppermute | solution.py:367
  68.7 0.0 copy-done
  68.7 1.6 %shard_map.150 = bf16[6,12,4,1024]{3,2,1,0:T(4,128)(2,1)} custom-call(bf16[4,288,72]{2,1,0:T(8,128)(2,1)S(1)} %copy-done, bf16[72,1024]{1,0:T(8,128)(2,1)S(1)} %get-tuple-element.25.refs_1_, bf16[72,1024]{1,0:T(8,128)(2,1)S(1)} %collective-permute-done.6.refs_2_, bf16[72,1024]{1,0:T(8,128)(2,1)S(1)} %collective-permute-done.7.refs_3_, ...), custom_call_target="tpu_custom_call" | custom-call | bytes 755712 | tf_op jit(solution)/shard_map/pallas_call | solution.py:199
  (11 shorter events, 0.0 us)
Async XLA Ops:
  0.0 1.3 %copy-start.6 = (bf16[4,12,24,512]{3,2,1,0:T(8,128)(2,1)S(1)}, bf16[4,12,24,512]{3,2,1,0:T(8,128)(2,1)}, u32[]{:S(2)}) copy-start(bf16[4,12,24,512]{3,2,1,0:T(8,128)(2,1)} %param.15) | copy-start | bytes 3538948
  1.3 0.9 %copy-start.12 = (bf16[136,288]{1,0:T(8,128)(2,1)S(1)}, bf16[136,288]{1,0:T(8,128)(2,1)}, u32[]{:S(2)}) copy-start(bf16[136,288]{1,0:T(8,128)(2,1)} %constant.14.clone.refs_0_) | copy-start | bytes 235012
  2.2 11.1 %copy-start.2 = (bf16[512,2048]{1,0:T(8,128)(2,1)S(1)}, bf16[512,2048]{1,0:T(8,128)(2,1)}, u32[]{:S(2)}) copy-start(bf16[512,2048]{1,0:T(8,128)(2,1)} %refs_6_.3) | copy-start | bytes 6291460
  2.2 11.1 %copy-start.3 = (bf16[2048,512]{1,0:T(8,128)(2,1)S(1)}, bf16[2048,512]{1,0:T(8,128)(2,1)}, u32[]{:S(2)}) copy-start(bf16[2048,512]{1,0:T(8,128)(2,1)} %refs_7_.1) | copy-start | bytes 6291460
  2.2 11.1 %copy-start.5 = (bf16[512,1536]{1,0:T(8,128)(2,1)S(1)}, bf16[512,1536]{1,0:T(8,128)(2,1)}, u32[]{:S(2)}) copy-start(bf16[512,1536]{1,0:T(8,128)(2,1)} %refs_4_.5) | copy-start | bytes 4718596
  2.2 11.1 %copy-start.7 = (bf16[4,12,24,512]{3,2,1,0:T(8,128)(2,1)S(1)}, bf16[4,12,24,512]{3,2,1,0:T(8,128)(2,1)}, u32[]{:S(2)}) copy-start(bf16[4,12,24,512]{3,2,1,0:T(8,128)(2,1)} %param.15) | copy-start | bytes 3538948
  2.2 11.1 %copy-start.8 = (bf16[512,512]{1,0:T(8,128)(2,1)S(1)}, bf16[512,512]{1,0:T(8,128)(2,1)}, u32[]{:S(2)}) copy-start(bf16[512,512]{1,0:T(8,128)(2,1)} %refs_5_.4) | copy-start | bytes 1572868
  2.2 11.1 %copy-start.14 = (bf16[2,80,80]{2,1,0:T(8,128)(2,1)S(1)}, bf16[2,80,80]{2,1,0:T(8,128)(2,1)}, u32[]{:S(2)}) copy-start(bf16[2,80,80]{2,1,0:T(8,128)(2,1)} %constant.15.clone.refs_5_) | copy-start | bytes 76804
  2.7 33.3 %collective-permute-start.2 = (bf16[4,24,512]{2,1,0:T(8,128)(2,1)S(1)}, bf16[4,24,512]{2,1,0:T(8,128)(2,1)S(1)}, u32[]{:S(2)}, u32[]{:S(2)}) collective-permute-start(bf16[4,24,512]{2,1,0:T(8,128)(2,1)S(1)} %get-tuple-element.21), channel_id=1, source_target_pairs={{17,0},{18,1},{19,2},{20,3},{21,4},{22,5},{23,6},{24,7},{25,8},{26... | collective-permute-start | bytes 294920 | tf_op jit(solution)/shard_map/ppermute | solution.py:367
  11.0 7.4 %collective-permute-start = (bf16[4,56,512]{2,1,0:T(8,128)(2,1)S(1)}, bf16[4,56,512]{2,1,0:T(8,128)(2,1)S(1)}, u32[]{:S(2)}, u32[]{:S(2)}) collective-permute-start(bf16[4,56,512]{2,1,0:T(8,128)(2,1)S(1)} %get-tuple-element.17), channel_id=1, source_target_pairs={{16,0},{17,1},{18,2},{19,3},{20,4},{21,5},{22,6},{23,7},{24,8},{25... | collective-permute-start | bytes 688136 | tf_op jit(solution)/shard_map/ppermute | solution.py:367
  12.1 6.3 %copy-start.11 = (bf16[10,80,80]{2,1,0:T(8,128)(2,1)S(1)}, bf16[10,80,80]{2,1,0:T(8,128)(2,1)}, u32[]{:S(2)}) copy-start(bf16[10,80,80]{2,1,0:T(8,128)(2,1)} %constant.16.clone.refs_8_) | copy-start | bytes 384004
  12.1 6.3 %collective-permute-start.1 = (bf16[4,56,512]{2,1,0:T(8,128)(2,1)S(1)}, bf16[4,56,512]{2,1,0:T(8,128)(2,1)S(1)}, u32[]{:S(2)}, u32[]{:S(2)}) collective-permute-start(bf16[4,56,512]{2,1,0:T(8,128)(2,1)S(1)} %get-tuple-element.18), channel_id=1, source_target_pairs={{1,0},{2,1},{3,2},{4,3},{5,4},{6,5},{7,6},{8,7},{9,8},{10,9},{11,1... | collective-permute-start | bytes 688136 | tf_op jit(solution)/shard_map/ppermute | solution.py:367
  13.3 29.8 %slice-start = ((s8[6291456]{0:T(1024)(128)(4,1)}), s8[4194304]{0:T(1024)(128)(4,1)S(1)}, s32[]{:S(2)}) async-start(s8[6291456]{0:T(1024)(128)(4,1)} %bitcast.2), calls=%async_computation | async-start | bytes 8388608
  18.3 17.7 %copy-start.13 = (bf16[4,80,80]{2,1,0:T(8,128)(2,1)S(1)}, bf16[4,80,80]{2,1,0:T(8,128)(2,1)}, u32[]{:S(2)}) copy-start(bf16[4,80,80]{2,1,0:T(8,128)(2,1)} %constant.17.clone.refs_8_) | copy-start | bytes 153604
  18.3 24.8 %slice-start.1 = ((s8[6291456]{0:T(1024)(128)(4,1)}), s8[2097152]{0:T(1024)(128)(4,1)S(1)}, s32[]{:S(2)}) async-start(s8[6291456]{0:T(1024)(128)(4,1)} %bitcast.2), calls=%async_computation.1 | async-start | bytes 4194304
  28.8 12.4 %collective-permute-start.5 = (bf16[4,24,512]{2,1,0:T(8,128)(2,1)S(1)}, bf16[4,24,512]{2,1,0:T(8,128)(2,1)S(1)}, u32[]{:S(2)}, u32[]{:S(2)}) collective-permute-start(bf16[4,24,512]{2,1,0:T(8,128)(2,1)S(1)} %get-tuple-element.24), channel_id=1, source_target_pairs={{17,0},{18,1},{19,2},{20,3},{21,4},{22,5},{23,6},{24,7},{25,8},{26... | collective-permute-start | bytes 294920 | tf_op jit(solution)/shard_map/ppermute | solution.py:367
  35.0 6.2 %collective-permute-start.3 = (bf16[4,56,512]{2,1,0:T(8,128)(2,1)S(1)}, bf16[4,56,512]{2,1,0:T(8,128)(2,1)S(1)}, u32[]{:S(2)}, u32[]{:S(2)}) collective-permute-start(bf16[4,56,512]{2,1,0:T(8,128)(2,1)S(1)} %get-tuple-element.22), channel_id=1, source_target_pairs={{1,0},{2,1},{3,2},{4,3},{5,4},{6,5},{7,6},{8,7},{9,8},{10,9},{11,1... | collective-permute-start | bytes 688136 | tf_op jit(solution)/shard_map/ppermute | solution.py:367
  35.0 8.1 %copy-start.1 = (bf16[2048,1024]{1,0:T(8,128)(2,1)S(1)}, bf16[2048,1024]{1,0:T(8,128)(2,1)}, u32[]{:S(2)}) copy-start(bf16[2048,1024]{1,0:T(8,128)(2,1)} %refs_8_.3) | copy-start | bytes 12582916
  35.0 8.1 %copy-start.4 = (bf16[1024,1024]{1,0:T(8,128)(2,1)S(1)}, bf16[1024,1024]{1,0:T(8,128)(2,1)}, u32[]{:S(2)}) copy-start(bf16[1024,1024]{1,0:T(8,128)(2,1)} %refs_10_.1) | copy-start | bytes 6291460
  35.0 8.1 %copy-start.9 = (bf16[7,288,72]{2,1,0:T(8,128)(2,1)S(1)}, bf16[7,288,72]{2,1,0:T(8,128)(2,1)}, u32[]{:S(2)}) copy-start(bf16[7,288,72]{2,1,0:T(8,128)(2,1)} %constant.18.clone.refs_0_) | copy-start | bytes 870916
  35.0 8.1 %copy-start.10 = (bf16[3,288,96]{2,1,0:T(8,128)(2,1)S(1)}, bf16[3,288,96]{2,1,0:T(8,128)(2,1)}, u32[]{:S(2)}) copy-start(bf16[3,288,96]{2,1,0:T(8,128)(2,1)} %constant.19.clone.refs_11_) | copy-start | bytes 497668
  35.0 8.1 %collective-permute-start.4 = (bf16[4,56,512]{2,1,0:T(8,128)(2,1)S(1)}, bf16[4,56,512]{2,1,0:T(8,128)(2,1)S(1)}, u32[]{:S(2)}, u32[]{:S(2)}) collective-permute-start(bf16[4,56,512]{2,1,0:T(8,128)(2,1)S(1)} %get-tuple-element.23), channel_id=1, source_target_pairs={{16,0},{17,1},{18,2},{19,3},{20,4},{21,5},{22,6},{23,7},{24,8},{25... | collective-permute-start | bytes 688136 | tf_op jit(solution)/shard_map/ppermute | solution.py:367
  43.1 25.5 %copy-start = (bf16[4,288,72]{2,1,0:T(8,128)(2,1)S(1)}, bf16[4,288,72]{2,1,0:T(8,128)(2,1)}, u32[]{:S(2)}) copy-start(bf16[4,288,72]{2,1,0:T(8,128)(2,1)} %constant.20.clone.refs_0_) | copy-start | bytes 497668
  54.4 12.9 %collective-permute-start.6 = (bf16[72,1024]{1,0:T(8,128)(2,1)S(1)}, bf16[72,1024]{1,0:T(8,128)(2,1)S(1)}, u32[]{:S(2)}, u32[]{:S(2)}) collective-permute-start(bf16[72,1024]{1,0:T(8,128)(2,1)S(1)} %get-tuple-element.26), channel_id=1, source_target_pairs={{15,0},{0,1},{1,2},{2,3},{3,4},{4,5},{5,6},{6,7},{7,8},{8,9},{9,10... | collective-permute-start | bytes 442376 | tf_op jit(solution)/shard_map/ppermute | solution.py:367
  54.5 12.8 %collective-permute-start.7 = (bf16[72,1024]{1,0:T(8,128)(2,1)S(1)}, bf16[72,1024]{1,0:T(8,128)(2,1)S(1)}, u32[]{:S(2)}, u32[]{:S(2)}) collective-permute-start(bf16[72,1024]{1,0:T(8,128)(2,1)S(1)} %get-tuple-element.27), channel_id=1, source_target_pairs={{112,0},{113,1},{114,2},{115,3},{116,4},{117,5},{118,6},{119,7},{1... | collective-permute-start | bytes 442376 | tf_op jit(solution)/shard_map/ppermute | solution.py:367
  54.6 14.0 %collective-permute-start.8 = (bf16[72,1024]{1,0:T(8,128)(2,1)S(1)}, bf16[72,1024]{1,0:T(8,128)(2,1)S(1)}, u32[]{:S(2)}, u32[]{:S(2)}) collective-permute-start(bf16[72,1024]{1,0:T(8,128)(2,1)S(1)} %get-tuple-element.28), channel_id=1, source_target_pairs={{127,0},{112,1},{113,2},{114,3},{115,4},{116,5},{117,6},{118,7},{1... | collective-permute-start | bytes 442376 | tf_op jit(solution)/shard_map/ppermute | solution.py:367

commit v3 on v2

v3 whole, which is shorter than its diff:
```python
import functools
import math

import jax
import jax.numpy as jnp
import numpy as np
from jax import lax
from jax.experimental import pallas as pl
from jax.experimental.pallas import tpu as pltpu
from jax.sharding import PartitionSpec as P

F32 = jnp.float32
BF16 = jnp.bfloat16
HEAD = 32
GROUP = 256
ORDER = (1, 2, 3, 0)
QUADS = ((0, 0), (0, 1), (1, 0), (1, 1))
EXP_SCALE = HEAD ** -0.5 * math.log2(math.e)
MIB = 1024 * 1024


def piece_of(i, j):
    if i >= 3 and j < 6:
        return "lon", (i - 3) * 6 + j
    if i < 3 and j >= 6:
        return "lat", i * 18 + j - 6
    if i < 3 and j < 6:
        return "both", i * 6 + j
    return None, 0


def source_of(i, j):
    i, j = i + 3, j + 6
    if i < 12 and j < 24:
        return "own", (i, j)
    return piece_of(i - 12 if i >= 12 else i, j - 24 if j >= 24 else j)


PIECE_ROWS = {"lon": 56, "lat": 56, "both": 24}


def first_send_table():
    row = lax.broadcasted_iota(jnp.int32, (136, 1), 0).astype(F32)

    def at(start, width, first_row, first_col):
        place = row - start
        line = jnp.floor((place + 0.5) / width)
        return (line + first_row) * 24 + (place - line * width) + first_col

    source = jnp.where(row < 56, at(0, 6, 3, 0), jnp.where(row < 112, at(56, 18, 0, 6), at(112, 6, 0, 0)))
    lane = lax.broadcasted_iota(jnp.int32, (136, 288), 1).astype(F32)
    return (lane == source).astype(F32).astype(BF16)


OWN_ROWS = ((64, 224), (208, 288))
GATHER = (
    {"own": 0, "lon": 160},
    {"own": 0, "lon": 80, "lat": 144, "both": 208},
)


def window_table(quad):
    table, used = np.zeros((2, 80, 128), np.float32), set()
    for r in range(6):
        for c in range(12):
            name, at = source_of(quad[0] * 6 + r, quad[1] * 12 + c)
            used.add(name)
            if name == "own":
                at = at[0] * 24 + at[1] - OWN_ROWS[quad[0]][0]
            at += GATHER[quad[0]][name]
            table[at // 128, r * 12 + c, at % 128] = 1
    return table, sorted(used)


def second_send_tables(quad):
    tables = {}
    for r in range(6):
        for c in range(12):
            name, at = piece_of(quad[0] * 6 + r, quad[1] * 12 + c)
            if name is not None:
                tables.setdefault(name, np.zeros((80, 128), np.float32))[at, r * 12 + c] = 1
    return tables


PAIR_GATHER = {quad: 80 * at for at, quad in enumerate(QUADS)}
PAIR_GATHER |= {"lon": 320, "lat": 384, "both": 448}


def pair_tables():
    table = np.zeros((4, 288, 128), np.float32)
    for i in range(12):
        for j in range(24):
            to = ((i % 2) * 2 + j % 2) * 72 + (i // 2) * 12 + j // 2
            name, at = source_of(i, j)
            if name == "own":
                name, at = (at[0] // 6, at[1] // 12), (at[0] % 6) * 12 + at[1] % 12
            at += PAIR_GATHER[name]
            table[at // 128, to, at % 128] = 1
    return table


def last_send_table():
    table = np.zeros((3, 288, 96), np.float32)
    for place, level in enumerate(ORDER):
        for i in range(6):
            for j in range(12):
                part = (i // 3) * 2 + j // 6
                to, at = part * 72 + ((i % 3) * 6 + j % 6) * 4 + level, place * 72 + i * 12 + j
                table[at // 96, to, at % 96] = 1
    return table


def dot(a, b):
    return jnp.dot(a, b, preferred_element_type=F32)


def normalize(values):
    center = values - jnp.mean(values, -1, keepdims=True)
    spread = jnp.mean(center * center, -1, keepdims=True)
    return center * lax.rsqrt(spread + 1e-05)


def gelu(x):
    return 0.5 * x * (1.0 + lax.erf(x * 0.5**0.5))


def attend(q, k, v, bias, first):
    lane_head = lax.broadcasted_iota(jnp.int32, (1, GROUP), 1) // HEAD
    stacked = jnp.concatenate(
        [q * (lane_head == h).astype(BF16) for h in range(8)], axis=0
    )
    scores = lax.dot_general(k, stacked, (((1,), (1,)), ((), ())), preferred_element_type=F32)
    if first is not None:
        scores = jnp.where(first, scores[:72], scores[72:])
    if bias is not None:
        scores = scores + bias[: scores.shape[0]]
    expo = jnp.exp2((scores - jnp.max(scores, 0, keepdims=True)) * EXP_SCALE)
    weights = expo * (1.0 / jnp.sum(expo, 0, keepdims=True))
    if first is not None:
        parts = [jnp.where(first, weights, 0.0), jnp.where(first, 0.0, weights)]
        weights = jnp.concatenate(parts, axis=0)
    full = lax.dot_general(
        weights.astype(BF16), v, (((0,), (0,)), ((), ())), preferred_element_type=F32
    )
    out = full[:144]
    for h in range(1, 8):
        out = jnp.where(lane_head == h, full[h * 144 : h * 144 + 144], out)
    return out


def attend_tile(qkv, width, bias):
    lane = lax.broadcasted_iota(jnp.int32, (1, 1152), 1)
    first = lax.rem(lane, 144) < 72
    groups = []
    for g in range(width // GROUP):
        at = [slice(part * width + g * GROUP, part * width + (g + 1) * GROUP) for part in range(3)]
        pair = attend(*[qkv[:144, s] for s in at], bias, None)
        alone = attend(*[qkv[144:, s] for s in at], bias, first)
        groups.append(jnp.concatenate([pair, alone], axis=0).astype(BF16))
    return jnp.concatenate(groups, axis=1)


def fill_bias(bias):
    edge = lax.axis_index("lat") == lax.axis_size("lat") - 1
    large = jnp.where(edge, 5e29, 0.0).astype(F32)
    query = lax.rem(lax.broadcasted_iota(jnp.int32, (1, 1152), 1), 144)
    keys = lax.broadcasted_iota(jnp.int32, (144, 1), 0)
    sides = [
        jnp.where(jnp.where(place >= 72, place - 72, place) < 36, 1.0, -1.0)
        for place in (keys, query)
    ]
    bias[...] = (sides[0] * sides[1] - 1.0) * large


BIAS = pltpu.VMEM((144, 1152), F32)


def run(body, outs, ins, scratch=(), flops=0, limit=32):
    names, out_names = list(ins), list(outs)

    def kernel(*refs):
        first, last = len(names), len(names) + len(out_names)
        body(dict(zip(names, refs)), dict(zip(out_names, refs[first:last])), refs[last:])

    size = sum(math.prod(array.shape) * 2 for array in ins.values())
    results = pl.pallas_call(
        kernel,
        out_shape=[jax.ShapeDtypeStruct(shape, BF16) for shape in outs.values()],
        in_specs=[pl.BlockSpec(memory_space=pltpu.VMEM)] * len(names),
        out_specs=[pl.BlockSpec(memory_space=pltpu.VMEM)] * len(out_names),
        scratch_shapes=list(scratch),
        compiler_params=pltpu.CompilerParams(vmem_limit_bytes=limit * MIB),
        cost_estimate=pl.CostEstimate(flops=flops, bytes_accessed=size, transcendentals=0),
    )(*ins.values())
    return dict(zip(out_names, results))


def const(table):
    return jnp.asarray(table, BF16)


def split_first(x):
    def body(refs, outs, _):
        table = first_send_table()
        for level in range(4):
            rows = dot(table, refs["x"][level])
            start = 0
            for name, count in PIECE_ROWS.items():
                outs[name][level] = rows[start : start + count].astype(BF16)
                start += count

    return run(
        body,
        {name: (4, rows, 512) for name, rows in PIECE_ROWS.items()},
        {"x": x},
        flops=10_000_000_000,
        limit=8,
    )


CHUNK = 1024


def fine_quads(quads, sources, weights, blocks, emit):
    tables = {quad: window_table(quad) for quad in quads}
    needed = sorted({name for quad in quads for name in tables[quad][1]})
    ins = {name: sources[name] for name in needed} | weights
    stack, place = [], {}
    for quad in quads:
        place[quad] = len(stack)
        stack += list(tables[quad][0])
    masked = any(quad[0] == 1 for quad in quads)
    outs = {quad: (4, 72, 512) for quad in quads}
    sends = {}
    if emit:
        for quad in QUADS:
            sends[quad] = second_send_tables(quad)
            for name, table in sends[quad].items():
                place["send", quad, name] = len(stack)
                stack.append(table)
            if quad in blocks and sends[quad]:
                ins["block", quad] = blocks[quad]
        outs |= {name: (4, rows, 512) for name, rows in PIECE_ROWS.items()}
    ins["table"] = const(np.stack(stack))

    def body(refs, outs, scratch):
        gathered = scratch[0]
        gathered[...] = jnp.zeros_like(gathered)
        if masked:
            fill_bias(scratch[1])
        for at, quad in enumerate(quads):
            table = [refs["table"][place[quad] + part, :72, :] for part in range(2)]
            table = jnp.concatenate(table, axis=1)
            levels = []
            for level in ORDER:
                for name in tables[quad][1]:
                    rows = slice(*OWN_ROWS[quad[0]]) if name == "own" else slice(None)
                    source = refs[name][level, rows, :]
                    start = GATHER[quad[0]][name]
                    gathered[at * 4 + level, start : start + source.shape[0], :] = source
                levels.append(dot(table, gathered[at * 4 + level]))
            tokens = jnp.concatenate(levels, axis=0)
            qkv = dot(normalize(tokens).astype(BF16), refs["qkv"][...]).astype(BF16)
            mixed = attend_tile(qkv, 512, scratch[1] if quad[0] == 1 else None)
            hidden = (tokens + dot(mixed, refs["out"][...])).astype(BF16).astype(F32)
            normed = normalize(hidden).astype(BF16)
            total = hidden
            for at in range(0, 2048, CHUNK):
                inner = gelu(dot(normed, refs["up"][:, at : at + CHUNK])).astype(BF16)
                total = total + dot(inner, refs["down"][at : at + CHUNK, :])
            for at, level in enumerate(ORDER):
                outs[quad][level] = total[at * 72 : at * 72 + 72].astype(BF16)
        if emit:
            for name, rows in PIECE_ROWS.items():
                for level in range(4):
                    total = None
                    for quad in QUADS:
                        if name in sends[quad]:
                            block = outs[quad] if quad in outs else refs["block", quad]
                            table = refs["table"][place["send", quad, name], :rows, :72]
                            term = dot(table, block[level])
                            total = term if total is None else total + term
                    outs[name][level] = total.astype(BF16)

    return run(
        body,
        outs,
        ins,
        [pltpu.VMEM((4 * len(quads), 256, 512), BF16)] + ([BIAS] if masked else []),
        flops=len(quads) * 2_500_000_000,
    )


def coarse(blocks, pieces, merge, qkv_weight, out_weight):
    sources = {("from", quad): blocks[quad] for quad in QUADS}
    sources |= {("from", name): pieces[name] for name in PIECE_ROWS}
    ins = sources | {"table": const(pair_tables()), "last": const(last_send_table())}
    ins |= {"merge": merge, "qkv": qkv_weight, "out": out_weight}

    def body(refs, outs, scratch):
        gathered, bias = scratch
        gathered[...] = jnp.zeros_like(gathered)
        fill_bias(bias)
        table = jnp.concatenate([refs["table"][at] for at in range(4)], axis=1)
        rows = []
        for level in ORDER:
            for name, start in PAIR_GATHER.items():
                source = refs["from", name][level]
                gathered[level, start : start + source.shape[0], :] = source
            total = dot(table, gathered[level])
            pairs = jnp.concatenate([total[72 * at : 72 * at + 72] for at in range(4)], axis=1)
            rows.append(normalize(pairs))
        pairs = jnp.concatenate(rows, axis=0).astype(BF16)
        merged = dot(pairs, refs["merge"][...]).astype(BF16).astype(F32)
        qkv = dot(normalize(merged).astype(BF16), refs["qkv"][...]).astype(BF16)
        mixed = attend_tile(qkv, 1024, bias)
        result = (merged + dot(mixed, refs["out"][...])).astype(BF16)
        parts = sum(dot(refs["last"][at], result[96 * at : 96 * at + 96]) for at in range(3))
        for part in range(4):
            for at in range(18):
                start = part * 72 + at * 4
                outs[part][at // 6, at % 6] = parts[start : start + 4].astype(BF16)

    return run(
        body,
        {part: (3, 6, 4, 1024) for part in range(4)},
        ins,
        [pltpu.VMEM((4, 512, 512), BF16), BIAS],
        flops=5_000_000_000,
    )


def assemble(parts):
    def body(refs, outs, _):
        for at in range(4):
            row, col = (3, 0)[at // 2], (6, 0)[at % 2]
            outs["out"][row : row + 3, col : col + 6] = refs[at][...]

    result = run(body, {"out": (6, 12, 4, 1024)}, dict(enumerate(parts)), limit=8)["out"]
    return result.transpose(2, 0, 1, 3)


def receive(array, lat, lon):
    rows, cols = lax.axis_size("lat"), lax.axis_size("lon")
    pairs = [
        (((a + lat) % rows) * cols + (b + lon) % cols, a * cols + b)
        for a in range(rows)
        for b in range(cols)
    ]
    return lax.ppermute(array, ("lat", "lon"), pairs)


def shift(pieces):
    return {
        "lon": receive(pieces["lon"], 0, 1),
        "lat": receive(pieces["lat"], 1, 0),
        "both": receive(pieces["both"], 1, 1),
    }


def shards(fine, fine_qkv, fine_out, fine_up, fine_down, merge_weight, coarse_qkv, coarse_out):
    weights = {"qkv": fine_qkv, "out": fine_out, "up": fine_up, "down": fine_down}
    x = fine.reshape(4, 288, 512)
    sources = {"own": x} | shift(split_first(x))
    blocks = fine_quads(QUADS[:1], sources, weights, {}, False)
    second = fine_quads(QUADS[1:3], sources, weights, blocks, True)
    pieces = shift({name: second[name] for name in PIECE_ROWS})
    blocks |= {quad: second[quad] for quad in QUADS[1:3]}
    blocks |= fine_quads(QUADS[3:], sources, weights, {}, False)
    parts = coarse(blocks, pieces, merge_weight, coarse_qkv, coarse_out)
    moved = [parts[0], receive(parts[1], 0, -1), receive(parts[2], -1, 0), receive(parts[3], -1, -1)]
    return assemble(moved)


def solution(mesh):
    in_specs = (P(None, "lat", "lon", None), P(), P(), P(), P(), P(), P(), P())
    out_specs = P(None, "lat", "lon", None)
    return jax.shard_map(shards, mesh=mesh, in_specs=in_specs, out_specs=out_specs, check_vma=False)
```

time: 70.4 us -> 65.7 us (0.933)
  Pallas kernels: 33.9 us -> 28.9 us
  local copies, waits for them, and re-layouts: 2.24 us -> 1.34 us
    pallas_call x6, Pallas kernels: 33.9 us -> 28.9 us  [run(): pl.pallas_call(kernel, out_shape=[jax.ShapeDtypeStruct(shape, BF16) for s...]
    unnamed x34 -> x30, local copies, waits for them, and re-layouts: 2.24 us -> 1.34 us
  transfers between devices with their start and end apart: 9 -> 9, of which waited for: 3 -> 3; matrix products, arithmetic and copies ran while one was open for 0% -> 0% of each run, Pallas kernels for 29% -> 28%
where the time goes in v3:
time: 65.7 us; the launch traced here: 65.6 us
  Pallas kernels  28.9 us (44%)
  starting transfers between devices  18.5 us (28%)
  waiting for transfers between devices  16.6 us (25%)
  local copies, waits for them, and re-layouts  1.34 us (2%)
    pallas_call x6, Pallas kernels, run(): pl.pallas_call(kernel, out_shape=[jax.ShapeDtypeStruct(shape, BF16) for s...  28.9 us
    ppermute x9, starting transfers between devices, receive(): return lax.ppermute(array, ('lat', 'lon'), pairs)  18.5 us
    ppermute x9, waiting for transfers between devices, receive(): return lax.ppermute(array, ('lat', 'lon'), pairs)  16.6 us
    unnamed x30, local copies, waits for them, and re-layouts  1.34 us
  transfers between devices with their start and end apart: 9, of which 3 were waited for; matrix products, arithmetic and copies ran while one was open for 0% of the time, Pallas kernels for 28%

profile of v3, /device:TPU:0, one launch (start us, length us, event | category | flops | bytes accessed | tf_op | source)
XLA Modules:
  0.0 65.6 jit_solution(17160533770856243624)
XLA Ops:
  0.0 0.0 copy-start.5
  0.0 1.3 %copy-done.5 = bf16[4,12,24,512]{3,2,1,0:T(8,128)(2,1)S(1)} copy-done((bf16[4,12,24,512]{3,2,1,0:T(8,128)(2,1)S(1)}, bf16[4,12,24,512]{3,2,1,0:T(8,128)(2,1)}, u32[]{:S(2)}) %copy-start.5) | copy-done | bytes 1179672
  1.3 0.0 copy-start.1
  1.3 0.0 copy-start.2
  1.3 0.0 copy-start.7
  1.3 0.0 copy-start.12
  1.3 0.5 shard_map.128
  1.8 8.3 %collective-permute-start.2 = (bf16[4,24,512]{2,1,0:T(8,128)(2,1)S(1)}, bf16[4,24,512]{2,1,0:T(8,128)(2,1)S(1)}, u32[]{:S(2)}, u32[]{:S(2)}) collective-permute-start(bf16[4,24,512]{2,1,0:T(8,128)(2,1)S(1)} %get-tuple-element.21), channel_id=1, source_target_pairs={{17,0},{18,1},{19,2},{20,3},{21,4},{22,5},{23,6},{24,7},{25,8},{26... | collective-permute-start | bytes 294920 | tf_op jit(solution)/shard_map/ppermute | solution.py:350
  10.1 1.1 %collective-permute-start = (bf16[4,56,512]{2,1,0:T(8,128)(2,1)S(1)}, bf16[4,56,512]{2,1,0:T(8,128)(2,1)S(1)}, u32[]{:S(2)}, u32[]{:S(2)}) collective-permute-start(bf16[4,56,512]{2,1,0:T(8,128)(2,1)S(1)} %get-tuple-element.17), channel_id=1, source_target_pairs={{16,0},{17,1},{18,2},{19,3},{20,4},{21,5},{22,6},{23,7},{24,8},{25... | collective-permute-start | bytes 688136 | tf_op jit(solution)/shard_map/ppermute | solution.py:350
  11.2 1.2 %collective-permute-start.1 = (bf16[4,56,512]{2,1,0:T(8,128)(2,1)S(1)}, bf16[4,56,512]{2,1,0:T(8,128)(2,1)S(1)}, u32[]{:S(2)}, u32[]{:S(2)}) collective-permute-start(bf16[4,56,512]{2,1,0:T(8,128)(2,1)S(1)} %get-tuple-element.18), channel_id=1, source_target_pairs={{1,0},{2,1},{3,2},{4,3},{5,4},{6,5},{7,6},{8,7},{9,8},{10,9},{11,1... | collective-permute-start | bytes 688136 | tf_op jit(solution)/shard_map/ppermute | solution.py:350
  12.4 0.0 copy-done.1
  12.4 0.0 copy-done.2
  12.4 0.0 copy-done.4
  12.4 0.0 copy-done.6
  12.4 0.0 copy-done.7
  12.4 0.0 copy-done.12
  12.4 0.0 slice-start
  12.4 4.5 %shard_map.127.refs_7_.refs_0_ = bf16[4,72,512]{2,1,0:T(8,128)(2,1)S(1)} custom-call(bf16[4,288,512]{2,1,0:T(8,128)(2,1)S(1)} %bitcast.5, bf16[512,1536]{1,0:T(8,128)(2,1)S(1)} %copy-done.4, bf16[512,512]{1,0:T(8,128)(2,1)S(1)} %copy-done.7, bf16[512,2048]{1,0:T(8,128)(2,1)S(1)} %copy-done.1, bf16[2048,512]{1,0:T(8,128)(2,1)S(1)} %copy-done.2, ...), custom_call_target="tpu_custom_call" | custom-call | flops 2500000000 | bytes 7512064 | tf_op jit(solution)/shard_map/pallas_call | solution.py:186
  16.9 0.0 copy-start.11
  16.9 0.0 slice-start.1
  16.9 0.0 collective-permute-done.refs_0_.refs_1_
  17.0 0.0 collective-permute-done.1.refs_1_.refs_2_
  17.0 0.0 copy-done.10
  17.0 9.3 %shard_map.129 = (bf16[4,72,512]{2,1,0:T(8,128)(2,1)S(1)}, bf16[4,72,512]{2,1,0:T(8,128)(2,1)S(1)}, bf16[4,56,512]{2,1,0:T(8,128)(2,1)S(1)}, bf16[4,56,512]{2,1,0:T(8,128)(2,1)S(1)}, bf16[4,24,512]{2,1,0:T(8,128)(2,1)S(1)}) custom-call(bf16[4,56,512]{2,1,0:T(8,128)(2,1)S(1)} %collective-permute-done.refs_0_.refs_1_, ...), custom_call_target="tpu_custom_call" | custom-call | flops 5000000000 | bytes 8409088 | tf_op jit(solution)/shard_map/pallas_call | solution.py:186
  26.2 6.5 %collective-permute-start.5 = (bf16[4,24,512]{2,1,0:T(8,128)(2,1)S(1)}, bf16[4,24,512]{2,1,0:T(8,128)(2,1)S(1)}, u32[]{:S(2)}, u32[]{:S(2)}) collective-permute-start(bf16[4,24,512]{2,1,0:T(8,128)(2,1)S(1)} %get-tuple-element.24), channel_id=1, source_target_pairs={{17,0},{18,1},{19,2},{20,3},{21,4},{22,5},{23,6},{24,7},{25,8},{26... | collective-permute-start | bytes 294920 | tf_op jit(solution)/shard_map/ppermute | solution.py:350
  32.7 0.0 collective-permute-start.3
  32.8 0.0 copy-start.9
  32.8 1.2 %collective-permute-start.4 = (bf16[4,56,512]{2,1,0:T(8,128)(2,1)S(1)}, bf16[4,56,512]{2,1,0:T(8,128)(2,1)S(1)}, u32[]{:S(2)}, u32[]{:S(2)}) collective-permute-start(bf16[4,56,512]{2,1,0:T(8,128)(2,1)S(1)} %get-tuple-element.23), channel_id=1, source_target_pairs={{16,0},{17,1},{18,2},{19,3},{20,4},{21,5},{22,6},{23,7},{24,8},{25... | collective-permute-start | bytes 688136 | tf_op jit(solution)/shard_map/ppermute | solution.py:350
  33.9 0.0 collective-permute-done.2.refs_0_
  33.9 0.0 copy-done.11
  33.9 4.5 %shard_map.130.refs_3_ = bf16[4,72,512]{2,1,0:T(8,128)(2,1)S(1)} custom-call(bf16[4,24,512]{2,1,0:T(8,128)(2,1)S(1)} %collective-permute-done.2.refs_0_, bf16[4,56,512]{2,1,0:T(8,128)(2,1)S(1)} %collective-permute-done.refs_0_.refs_1_, bf16[4,56,512]{2,1,0:T(8,128)(2,1)S(1)} %collective-permute-done.1.refs_1_.refs_2_, bf16[4,288,512]{2,1,0:T(8,128)(2,1)S(1)} %bitcast.7, ...), custom_call_target="tpu_custom_call" | custom-call | flops 2500000000 | bytes 8069120 | tf_op jit(solution)/shard_map/pallas_call | solution.py:186
  38.4 0.0 collective-permute-done.5.refs_6_
  38.5 0.0 collective-permute-done.3.refs_4_
  38.5 2.4 %collective-permute-done.4.refs_5_ = bf16[4,56,512]{2,1,0:T(8,128)(2,1)S(1)} collective-permute-done((bf16[4,56,512]{2,1,0:T(8,128)(2,1)S(1)}, bf16[4,56,512]{2,1,0:T(8,128)(2,1)S(1)}, u32[]{:S(2)}, u32[]{:S(2)}) %collective-permute-start.4) | collective-permute-done | bytes 229408 | tf_op jit(solution)/shard_map/ppermute | solution.py:350
  40.8 0.0 slice-done
  40.8 0.0 slice-done.1
  40.8 0.0 copy-done
  40.9 0.0 copy-done.3
  40.9 0.0 copy-done.8
  40.9 0.0 copy-done.9
  40.9 9.3 %shard_map.131 = (bf16[3,6,4,1024]{3,2,1,0:T(4,128)(2,1)S(1)}, bf16[3,6,4,1024]{3,2,1,0:T(4,128)(2,1)S(1)}, bf16[3,6,4,1024]{3,2,1,0:T(4,128)(2,1)S(1)}, bf16[3,6,4,1024]{3,2,1,0:T(4,128)(2,1)S(1)}) custom-call(bf16[4,72,512]{2,1,0:T(8,128)(2,1)S(1)} %shard_map.127.refs_7_.refs_0_, bf16[4,72,512]{2,1,0:T(8,128)(2,1)S(1)} %get-tuple-element.19.refs_1_, ...), custom_call_target="tpu_custom_call" | custom-call | flops 5000000000 | bytes 14780416 | tf_op jit(solution)/shard_map/pallas_call | solution.py:186
  50.2 0.1 collective-permute-start.6
  50.3 0.2 collective-permute-start.7
  50.5 0.0 collective-permute-start.8
  50.5 12.6 %collective-permute-done.6.refs_1_ = bf16[3,6,4,1024]{3,2,1,0:T(4,128)(2,1)S(1)} collective-permute-done((bf16[3,6,4,1024]{3,2,1,0:T(4,128)(2,1)S(1)}, bf16[3,6,4,1024]{3,2,1,0:T(4,128)(2,1)S(1)}, u32[]{:S(2)}, u32[]{:S(2)}) %collective-permute-start.6) | collective-permute-done | bytes 147488 | tf_op jit(solution)/shard_map/ppermute | solution.py:350
  63.1 0.0 collective-permute-done.7.refs_2_
  63.1 1.6 %collective-permute-done.8.refs_3_ = bf16[3,6,4,1024]{3,2,1,0:T(4,128)(2,1)S(1)} collective-permute-done((bf16[3,6,4,1024]{3,2,1,0:T(4,128)(2,1)S(1)}, bf16[3,6,4,1024]{3,2,1,0:T(4,128)(2,1)S(1)}, u32[]{:S(2)}, u32[]{:S(2)}) %collective-permute-start.8) | collective-permute-done | bytes 147488 | tf_op jit(solution)/shard_map/ppermute | solution.py:350
  64.7 0.9 %shard_map.132 = bf16[6,12,4,1024]{3,2,1,0:T(4,128)(2,1)} custom-call(bf16[3,6,4,1024]{3,2,1,0:T(4,128)(2,1)S(1)} %get-tuple-element.25.refs_0_, bf16[3,6,4,1024]{3,2,1,0:T(4,128)(2,1)S(1)} %collective-permute-done.6.refs_1_, bf16[3,6,4,1024]{3,2,1,0:T(4,128)(2,1)S(1)} %collective-permute-done.7.refs_2_, ...), custom_call_target="tpu_custom_call" | custom-call | bytes 589824 | tf_op jit(solution)/shard_map/pallas_call | solution.py:186
  (7 shorter events, 0.0 us)
Async XLA Ops:
  0.0 1.3 %copy-start.5 = (bf16[4,12,24,512]{3,2,1,0:T(8,128)(2,1)S(1)}, bf16[4,12,24,512]{3,2,1,0:T(8,128)(2,1)}, u32[]{:S(2)}) copy-start(bf16[4,12,24,512]{3,2,1,0:T(8,128)(2,1)} %param.13) | copy-start | bytes 3538948
  1.3 11.1 %copy-start.1 = (bf16[512,2048]{1,0:T(8,128)(2,1)S(1)}, bf16[512,2048]{1,0:T(8,128)(2,1)}, u32[]{:S(2)}) copy-start(bf16[512,2048]{1,0:T(8,128)(2,1)} %refs_6_.3) | copy-start | bytes 6291460
  1.3 11.1 %copy-start.2 = (bf16[2048,512]{1,0:T(8,128)(2,1)S(1)}, bf16[2048,512]{1,0:T(8,128)(2,1)}, u32[]{:S(2)}) copy-start(bf16[2048,512]{1,0:T(8,128)(2,1)} %refs_7_.2) | copy-start | bytes 6291460
  1.3 11.1 %copy-start.4 = (bf16[512,1536]{1,0:T(8,128)(2,1)S(1)}, bf16[512,1536]{1,0:T(8,128)(2,1)}, u32[]{:S(2)}) copy-start(bf16[512,1536]{1,0:T(8,128)(2,1)} %refs_4_.5) | copy-start | bytes 4718596
  1.3 11.1 %copy-start.6 = (bf16[4,12,24,512]{3,2,1,0:T(8,128)(2,1)S(1)}, bf16[4,12,24,512]{3,2,1,0:T(8,128)(2,1)}, u32[]{:S(2)}) copy-start(bf16[4,12,24,512]{3,2,1,0:T(8,128)(2,1)} %param.13) | copy-start | bytes 3538948
  1.3 11.1 %copy-start.7 = (bf16[512,512]{1,0:T(8,128)(2,1)S(1)}, bf16[512,512]{1,0:T(8,128)(2,1)}, u32[]{:S(2)}) copy-start(bf16[512,512]{1,0:T(8,128)(2,1)} %refs_5_.4) | copy-start | bytes 1572868
  1.3 11.1 %copy-start.12 = (bf16[2,80,128]{2,1,0:T(8,128)(2,1)S(1)}, bf16[2,80,128]{2,1,0:T(8,128)(2,1)}, u32[]{:S(2)}) copy-start(bf16[2,80,128]{2,1,0:T(8,128)(2,1)} %constant.10.clone.refs_5_) | copy-start | bytes 122884
  1.8 32.1 %collective-permute-start.2 = (bf16[4,24,512]{2,1,0:T(8,128)(2,1)S(1)}, bf16[4,24,512]{2,1,0:T(8,128)(2,1)S(1)}, u32[]{:S(2)}, u32[]{:S(2)}) collective-permute-start(bf16[4,24,512]{2,1,0:T(8,128)(2,1)S(1)} %get-tuple-element.21), channel_id=1, source_target_pairs={{17,0},{18,1},{19,2},{20,3},{21,4},{22,5},{23,6},{24,7},{25,8},{26... | collective-permute-start | bytes 294920 | tf_op jit(solution)/shard_map/ppermute | solution.py:350
  10.1 6.9 %collective-permute-start = (bf16[4,56,512]{2,1,0:T(8,128)(2,1)S(1)}, bf16[4,56,512]{2,1,0:T(8,128)(2,1)S(1)}, u32[]{:S(2)}, u32[]{:S(2)}) collective-permute-start(bf16[4,56,512]{2,1,0:T(8,128)(2,1)S(1)} %get-tuple-element.17), channel_id=1, source_target_pairs={{16,0},{17,1},{18,2},{19,3},{20,4},{21,5},{22,6},{23,7},{24,8},{25... | collective-permute-start | bytes 688136 | tf_op jit(solution)/shard_map/ppermute | solution.py:350
  11.2 5.8 %copy-start.10 = (bf16[9,80,128]{2,1,0:T(8,128)(2,1)S(1)}, bf16[9,80,128]{2,1,0:T(8,128)(2,1)}, u32[]{:S(2)}) copy-start(bf16[9,80,128]{2,1,0:T(8,128)(2,1)} %constant.11.clone.refs_8_) | copy-start | bytes 552964
  11.2 5.8 %collective-permute-start.1 = (bf16[4,56,512]{2,1,0:T(8,128)(2,1)S(1)}, bf16[4,56,512]{2,1,0:T(8,128)(2,1)S(1)}, u32[]{:S(2)}, u32[]{:S(2)}) collective-permute-start(bf16[4,56,512]{2,1,0:T(8,128)(2,1)S(1)} %get-tuple-element.18), channel_id=1, source_target_pairs={{1,0},{2,1},{3,2},{4,3},{5,4},{6,5},{7,6},{8,7},{9,8},{10,9},{11,1... | collective-permute-start | bytes 688136 | tf_op jit(solution)/shard_map/ppermute | solution.py:350
  12.4 28.4 %slice-start = ((s8[6291456]{0:T(1024)(128)(4,1)}), s8[4194304]{0:T(1024)(128)(4,1)S(1)}, s32[]{:S(2)}) async-start(s8[6291456]{0:T(1024)(128)(4,1)} %bitcast.2), calls=%async_computation | async-start | bytes 8388608
  16.9 17.0 %copy-start.11 = (bf16[2,80,128]{2,1,0:T(8,128)(2,1)S(1)}, bf16[2,80,128]{2,1,0:T(8,128)(2,1)}, u32[]{:S(2)}) copy-start(bf16[2,80,128]{2,1,0:T(8,128)(2,1)} %constant.12.clone.refs_8_) | copy-start | bytes 122884
  16.9 23.9 %slice-start.1 = ((s8[6291456]{0:T(1024)(128)(4,1)}), s8[2097152]{0:T(1024)(128)(4,1)S(1)}, s32[]{:S(2)}) async-start(s8[6291456]{0:T(1024)(128)(4,1)} %bitcast.2), calls=%async_computation.1 | async-start | bytes 4194304
  26.2 12.2 %collective-permute-start.5 = (bf16[4,24,512]{2,1,0:T(8,128)(2,1)S(1)}, bf16[4,24,512]{2,1,0:T(8,128)(2,1)S(1)}, u32[]{:S(2)}, u32[]{:S(2)}) collective-permute-start(bf16[4,24,512]{2,1,0:T(8,128)(2,1)S(1)} %get-tuple-element.24), channel_id=1, source_target_pairs={{17,0},{18,1},{19,2},{20,3},{21,4},{22,5},{23,6},{24,7},{25,8},{26... | collective-permute-start | bytes 294920 | tf_op jit(solution)/shard_map/ppermute | solution.py:350
  32.7 5.7 %collective-permute-start.3 = (bf16[4,56,512]{2,1,0:T(8,128)(2,1)S(1)}, bf16[4,56,512]{2,1,0:T(8,128)(2,1)S(1)}, u32[]{:S(2)}, u32[]{:S(2)}) collective-permute-start(bf16[4,56,512]{2,1,0:T(8,128)(2,1)S(1)} %get-tuple-element.22), channel_id=1, source_target_pairs={{1,0},{2,1},{3,2},{4,3},{5,4},{6,5},{7,6},{8,7},{9,8},{10,9},{11,1... | collective-permute-start | bytes 688136 | tf_op jit(solution)/shard_map/ppermute | solution.py:350
  32.7 8.1 %copy-start = (bf16[2048,1024]{1,0:T(8,128)(2,1)S(1)}, bf16[2048,1024]{1,0:T(8,128)(2,1)}, u32[]{:S(2)}) copy-start(bf16[2048,1024]{1,0:T(8,128)(2,1)} %refs_9_.1) | copy-start | bytes 12582916
  32.7 8.1 %copy-start.3 = (bf16[1024,1024]{1,0:T(8,128)(2,1)S(1)}, bf16[1024,1024]{1,0:T(8,128)(2,1)}, u32[]{:S(2)}) copy-start(bf16[1024,1024]{1,0:T(8,128)(2,1)} %refs_11_.1) | copy-start | bytes 6291460
  32.8 8.1 %copy-start.8 = (bf16[4,288,128]{2,1,0:T(8,128)(2,1)S(1)}, bf16[4,288,128]{2,1,0:T(8,128)(2,1)}, u32[]{:S(2)}) copy-start(bf16[4,288,128]{2,1,0:T(8,128)(2,1)} %constant.13.clone.refs_7_) | copy-start | bytes 884740
  32.8 8.1 %copy-start.9 = (bf16[3,288,96]{2,1,0:T(8,128)(2,1)S(1)}, bf16[3,288,96]{2,1,0:T(8,128)(2,1)}, u32[]{:S(2)}) copy-start(bf16[3,288,96]{2,1,0:T(8,128)(2,1)} %constant.14.clone.refs_8_) | copy-start | bytes 497668
  32.8 8.1 %collective-permute-start.4 = (bf16[4,56,512]{2,1,0:T(8,128)(2,1)S(1)}, bf16[4,56,512]{2,1,0:T(8,128)(2,1)S(1)}, u32[]{:S(2)}, u32[]{:S(2)}) collective-permute-start(bf16[4,56,512]{2,1,0:T(8,128)(2,1)S(1)} %get-tuple-element.23), channel_id=1, source_target_pairs={{16,0},{17,1},{18,2},{19,3},{20,4},{21,5},{22,6},{23,7},{24,8},{25... | collective-permute-start | bytes 688136 | tf_op jit(solution)/shard_map/ppermute | solution.py:350
  50.2 12.9 %collective-permute-start.6 = (bf16[3,6,4,1024]{3,2,1,0:T(4,128)(2,1)S(1)}, bf16[3,6,4,1024]{3,2,1,0:T(4,128)(2,1)S(1)}, u32[]{:S(2)}, u32[]{:S(2)}) collective-permute-start(bf16[3,6,4,1024]{3,2,1,0:T(4,128)(2,1)S(1)} %get-tuple-element.26), channel_id=1, source_target_pairs={{15,0},{0,1},{1,2},{2,3},{3,4},{4,5},{5,6},{6,7},{7,8},{8,9},{9,10... | collective-permute-start | bytes 442376 | tf_op jit(solution)/shard_map/ppermute | solution.py:350
  50.3 12.8 %collective-permute-start.7 = (bf16[3,6,4,1024]{3,2,1,0:T(4,128)(2,1)S(1)}, bf16[3,6,4,1024]{3,2,1,0:T(4,128)(2,1)S(1)}, u32[]{:S(2)}, u32[]{:S(2)}) collective-permute-start(bf16[3,6,4,1024]{3,2,1,0:T(4,128)(2,1)S(1)} %get-tuple-element.27), channel_id=1, source_target_pairs={{112,0},{113,1},{114,2},{115,3},{116,4},{117,5},{118,6},{119,7},{1... | collective-permute-start | bytes 442376 | tf_op jit(solution)/shard_map/ppermute | solution.py:350
  50.5 14.2 %collective-permute-start.8 = (bf16[3,6,4,1024]{3,2,1,0:T(4,128)(2,1)S(1)}, bf16[3,6,4,1024]{3,2,1,0:T(4,128)(2,1)S(1)}, u32[]{:S(2)}, u32[]{:S(2)}) collective-permute-start(bf16[3,6,4,1024]{3,2,1,0:T(4,128)(2,1)S(1)} %get-tuple-element.28), channel_id=1, source_target_pairs={{127,0},{112,1},{113,2},{114,3},{115,4},{116,5},{117,6},{118,7},{1... | collective-permute-start | bytes 442376 | tf_op jit(solution)/shard_map/ppermute | solution.py:350

commit v4 on v3

--- a/solution.py
+++ b/solution.py
@@ -40,15 +40,15 @@
 
 
 def first_send_table():
-    row = lax.broadcasted_iota(jnp.int32, (136, 1), 0).astype(F32)
+    row = lax.broadcasted_iota(jnp.int32, (112, 1), 0).astype(F32)
 
     def at(start, width, first_row, first_col):
         place = row - start
         line = jnp.floor((place + 0.5) / width)
         return (line + first_row) * 24 + (place - line * width) + first_col
 
-    source = jnp.where(row < 56, at(0, 6, 3, 0), jnp.where(row < 112, at(56, 18, 0, 6), at(112, 6, 0, 0)))
-    lane = lax.broadcasted_iota(jnp.int32, (136, 288), 1).astype(F32)
+    source = jnp.where(row < 56, at(0, 6, 3, 0), at(56, 18, 0, 6))
+    lane = lax.broadcasted_iota(jnp.int32, (112, 288), 1).astype(F32)
     return (lane == source).astype(F32).astype(BF16)
 
 
@@ -124,12 +124,15 @@
     return 0.5 * x * (1.0 + lax.erf(x * 0.5**0.5))
 
 
-def attend(q, k, v, bias, first):
+def score(q, k):
     lane_head = lax.broadcasted_iota(jnp.int32, (1, GROUP), 1) // HEAD
     stacked = jnp.concatenate(
         [q * (lane_head == h).astype(BF16) for h in range(8)], axis=0
     )
-    scores = lax.dot_general(k, stacked, (((1,), (1,)), ((), ())), preferred_element_type=F32)
+    return lax.dot_general(k, stacked, (((1,), (1,)), ((), ())), preferred_element_type=F32)
+
+
+def mix(scores, v, bias, first):
     if first is not None:
         scores = jnp.where(first, scores[:72], scores[72:])
     if bias is not None:
@@ -142,22 +145,39 @@
     full = lax.dot_general(
         weights.astype(BF16), v, (((0,), (0,)), ((), ())), preferred_element_type=F32
     )
+    lane_head = lax.broadcasted_iota(jnp.int32, (1, GROUP), 1) // HEAD
     out = full[:144]
     for h in range(1, 8):
         out = jnp.where(lane_head == h, full[h * 144 : h * 144 + 144], out)
-    return out
-
-
-def attend_tile(qkv, width, bias):
+    return out.astype(BF16)
+
+
+def attend(qkv, width, biases):
     lane = lax.broadcasted_iota(jnp.int32, (1, 1152), 1)
     first = lax.rem(lane, 144) < 72
-    groups = []
-    for g in range(width // GROUP):
-        at = [slice(part * width + g * GROUP, part * width + (g + 1) * GROUP) for part in range(3)]
-        pair = attend(*[qkv[:144, s] for s in at], bias, None)
-        alone = attend(*[qkv[144:, s] for s in at], bias, first)
-        groups.append(jnp.concatenate([pair, alone], axis=0).astype(BF16))
-    return jnp.concatenate(groups, axis=1)
+    units = []
+    for at, bias in enumerate(biases):
+        for g in range(width // GROUP):
+            for half in range(2):
+                rows = slice(at * 288 + half * 144, at * 288 + half * 144 + 144)
+                lanes = [
+                    slice(part * width + g * GROUP, part * width + (g + 1) * GROUP)
+                    for part in range(3)
+                ]
+                operands = [qkv[rows, s] for s in lanes]
+                units.append((at, g, half, operands, bias, first if half else None))
+    outs = {}
+    ready = score(*units[0][3][:2])
+    for at, (tile, g, half, operands, bias, alone) in enumerate(units):
+        ahead = score(*units[at + 1][3][:2]) if at + 1 < len(units) else None
+        outs[tile, half, g] = mix(ready, operands[2], bias, alone)
+        ready = ahead
+    rows = []
+    for tile in range(len(biases)):
+        for half in range(2):
+            row = [outs[tile, half, g] for g in range(width // GROUP)]
+            rows.append(jnp.concatenate(row, axis=1))
+    return jnp.concatenate(rows, axis=0)
 
 
 def fill_bias(bias):
@@ -204,18 +224,24 @@
         table = first_send_table()
         for level in range(4):
             rows = dot(table, refs["x"][level])
-            start = 0
-            for name, count in PIECE_ROWS.items():
-                outs[name][level] = rows[start : start + count].astype(BF16)
-                start += count
+            outs["lon"][level] = rows[:56].astype(BF16)
+            outs["lat"][level] = rows[56:].astype(BF16)
 
     return run(
         body,
-        {name: (4, rows, 512) for name, rows in PIECE_ROWS.items()},
+        {name: (4, PIECE_ROWS[name], 512) for name in ("lon", "lat")},
         {"x": x},
         flops=10_000_000_000,
         limit=8,
     )
+
+
+def corner_table():
+    table = np.zeros((80, 128), np.float32)
+    for i in range(3):
+        for j in range(6):
+            table[i * 6 + j, i * 24 + j] = 1
+    return table
 
 
 CHUNK = 1024
@@ -235,12 +261,16 @@
     if emit:
         for quad in QUADS:
             sends[quad] = second_send_tables(quad)
+            sends[quad] = {name: sends[quad][name] for name in emit if name in sends[quad]}
             for name, table in sends[quad].items():
                 place["send", quad, name] = len(stack)
                 stack.append(table)
             if quad in blocks and sends[quad]:
                 ins["block", quad] = blocks[quad]
-        outs |= {name: (4, rows, 512) for name, rows in PIECE_ROWS.items()}
+        outs |= {name: (8 if name == "both" else 4, PIECE_ROWS[name], 512) for name in emit}
+    if "both" in emit:
+        place["corner"] = len(stack)
+        stack.append(corner_table())
     ins["table"] = const(np.stack(stack))
 
     def body(refs, outs, scratch):
@@ -248,10 +278,10 @@
         gathered[...] = jnp.zeros_like(gathered)
         if masked:
             fill_bias(scratch[1])
+        levels = []
         for at, quad in enumerate(quads):
             table = [refs["table"][place[quad] + part, :72, :] for part in range(2)]
             table = jnp.concatenate(table, axis=1)
-            levels = []
             for level in ORDER:
                 for name in tables[quad][1]:
                     rows = slice(*OWN_ROWS[quad[0]]) if name == "own" else slice(None)
@@ -259,28 +289,33 @@
                     start = GATHER[quad[0]][name]
                     gathered[at * 4 + level, start : start + source.shape[0], :] = source
                 levels.append(dot(table, gathered[at * 4 + level]))
-            tokens = jnp.concatenate(levels, axis=0)
-            qkv = dot(normalize(tokens).astype(BF16), refs["qkv"][...]).astype(BF16)
-            mixed = attend_tile(qkv, 512, scratch[1] if quad[0] == 1 else None)
-            hidden = (tokens + dot(mixed, refs["out"][...])).astype(BF16).astype(F32)
-            normed = normalize(hidden).astype(BF16)
-            total = hidden
-            for at in range(0, 2048, CHUNK):
-                inner = gelu(dot(normed, refs["up"][:, at : at + CHUNK])).astype(BF16)
-                total = total + dot(inner, refs["down"][at : at + CHUNK, :])
-            for at, level in enumerate(ORDER):
-                outs[quad][level] = total[at * 72 : at * 72 + 72].astype(BF16)
-        if emit:
-            for name, rows in PIECE_ROWS.items():
-                for level in range(4):
-                    total = None
-                    for quad in QUADS:
-                        if name in sends[quad]:
-                            block = outs[quad] if quad in outs else refs["block", quad]
-                            table = refs["table"][place["send", quad, name], :rows, :72]
-                            term = dot(table, block[level])
-                            total = term if total is None else total + term
-                    outs[name][level] = total.astype(BF16)
+        tokens = jnp.concatenate(levels, axis=0)
+        qkv = dot(normalize(tokens).astype(BF16), refs["qkv"][...]).astype(BF16)
+        mixed = attend(qkv, 512, [scratch[1] if quad[0] == 1 else None for quad in quads])
+        hidden = (tokens + dot(mixed, refs["out"][...])).astype(BF16).astype(F32)
+        normed = normalize(hidden).astype(BF16)
+        total = hidden
+        for at in range(0, 2048, CHUNK):
+            inner = gelu(dot(normed, refs["up"][:, at : at + CHUNK])).astype(BF16)
+            total = total + dot(inner, refs["down"][at : at + CHUNK, :])
+        for at, quad in enumerate(quads):
+            for place_at, level in enumerate(ORDER):
+                start = at * 288 + place_at * 72
+                outs[quad][level] = total[start : start + 72].astype(BF16)
+        for name in emit:
+            rows = PIECE_ROWS[name]
+            for level in range(4):
+                total = None
+                for quad in QUADS:
+                    if name in sends[quad]:
+                        block = outs[quad] if quad in outs else refs["block", quad]
+                        table = refs["table"][place["send", quad, name], :rows, :72]
+                        term = dot(table, block[level])
+                        total = term if total is None else total + term
+                if name == "both":
+                    corner = dot(refs["table"][place["corner"], :24, :80], refs["own"][level, :80, :])
+                    outs[name][level] = corner.astype(BF16)
+                outs[name][level + (4 if name == "both" else 0)] = total.astype(BF16)
 
     return run(
         body,
@@ -305,7 +340,7 @@
         rows = []
         for level in ORDER:
             for name, start in PAIR_GATHER.items():
-                source = refs["from", name][level]
+                source = refs["from", name][level + (4 if name == "both" else 0)]
                 gathered[level, start : start + source.shape[0], :] = source
             total = dot(table, gathered[level])
             pairs = jnp.concatenate([total[72 * at : 72 * at + 72] for at in range(4)], axis=1)
@@ -313,7 +348,7 @@
         pairs = jnp.concatenate(rows, axis=0).astype(BF16)
         merged = dot(pairs, refs["merge"][...]).astype(BF16).astype(F32)
         qkv = dot(normalize(merged).astype(BF16), refs["qkv"][...]).astype(BF16)
-        mixed = attend_tile(qkv, 1024, bias)
+        mixed = attend(qkv, 1024, [bias])
         result = (merged + dot(mixed, refs["out"][...])).astype(BF16)
         parts = sum(dot(refs["last"][at], result[96 * at : 96 * at + 96]) for at in range(3))
         for part in range(4):
@@ -350,23 +385,24 @@
     return lax.ppermute(array, ("lat", "lon"), pairs)
 
 
+AHEAD = {"lon": (0, 1), "lat": (1, 0), "both": (1, 1)}
+
+
 def shift(pieces):
-    return {
-        "lon": receive(pieces["lon"], 0, 1),
-        "lat": receive(pieces["lat"], 1, 0),
-        "both": receive(pieces["both"], 1, 1),
-    }
+    return {name: receive(piece, *AHEAD[name]) for name, piece in pieces.items()}
 
 
 def shards(fine, fine_qkv, fine_out, fine_up, fine_down, merge_weight, coarse_qkv, coarse_out):
     weights = {"qkv": fine_qkv, "out": fine_out, "up": fine_up, "down": fine_down}
     x = fine.reshape(4, 288, 512)
     sources = {"own": x} | shift(split_first(x))
-    blocks = fine_quads(QUADS[:1], sources, weights, {}, False)
-    second = fine_quads(QUADS[1:3], sources, weights, blocks, True)
-    pieces = shift({name: second[name] for name in PIECE_ROWS})
-    blocks |= {quad: second[quad] for quad in QUADS[1:3]}
-    blocks |= fine_quads(QUADS[3:], sources, weights, {}, False)
+    blocks = fine_quads(QUADS[:1], sources, weights, {}, ("both",))
+    corners = shift({"both": blocks.pop("both")})["both"]
+    sources["both"] = corners
+    second = fine_quads(QUADS[1:3], sources, weights, blocks, ("lon", "lat"))
+    pieces = shift({name: second.pop(name) for name in ("lon", "lat")}) | {"both": corners}
+    blocks |= second
+    blocks |= fine_quads(QUADS[3:], sources, weights, {}, ())
     parts = coarse(blocks, pieces, merge_weight, coarse_qkv, coarse_out)
     moved = [parts[0], receive(parts[1], 0, -1), receive(parts[2], -1, 0), receive(parts[3], -1, -1)]
     return assemble(moved)

time: 65.7 us -> 59.4 us (0.904)
  waiting for transfers between devices: 16.6 us -> 14.3 us
  Pallas kernels: 28.9 us -> 26.7 us
  starting transfers between devices: 18.5 us -> 16.8 us
    ppermute x9 -> x8, waiting for transfers between devices: 16.6 us -> 14.3 us  [receive(): return lax.ppermute(array, ('lat', 'lon'), pairs)]
    pallas_call x6, Pallas kernels: 28.9 us -> 26.7 us  [run(): pl.pallas_call(kernel, out_shape=[jax.ShapeDtypeStruct(shape, BF16) for s...]
    ppermute x9 -> x8, starting transfers between devices: 18.5 us -> 16.8 us  [receive(): return lax.ppermute(array, ('lat', 'lon'), pairs)]
  transfers between devices with their start and end apart: 9 -> 8, of which waited for: 3 -> 4; matrix products, arithmetic and copies ran while one was open for 0% -> 0% of each run, Pallas kernels for 28% -> 28%
where the time goes in v4:
time: 59.4 us; the launch traced here: 59.3 us
  Pallas kernels  26.7 us (45%)
  starting transfers between devices  16.8 us (28%)
  waiting for transfers between devices  14.3 us (24%)
  local copies, waits for them, and re-layouts  1.34 us (2%)
    pallas_call x6, Pallas kernels, run(): pl.pallas_call(kernel, out_shape=[jax.ShapeDtypeStruct(shape, BF16) for s...  26.7 us
    ppermute x8, starting transfers between devices, receive(): return lax.ppermute(array, ('lat', 'lon'), pairs)  16.8 us
    ppermute x8, waiting for transfers between devices, receive(): return lax.ppermute(array, ('lat', 'lon'), pairs)  14.3 us
    unnamed x30, local copies, waits for them, and re-layouts  1.34 us
  transfers between devices with their start and end apart: 8, of which 4 were waited for; matrix products, arithmetic and copies ran while one was open for 0% of the time, Pallas kernels for 28%

profile of v4, /device:TPU:0, one launch (start us, length us, event | category | flops | bytes accessed | tf_op | source)
XLA Modules:
  0.0 59.3 jit_solution(4330128320865345304)
XLA Ops:
  0.0 0.0 copy-start.5
  0.0 1.3 %copy-done.5 = bf16[4,12,24,512]{3,2,1,0:T(8,128)(2,1)S(1)} copy-done((bf16[4,12,24,512]{3,2,1,0:T(8,128)(2,1)S(1)}, bf16[4,12,24,512]{3,2,1,0:T(8,128)(2,1)}, u32[]{:S(2)}) %copy-start.5) | copy-done | bytes 1179672
  1.3 0.0 copy-start.1
  1.3 0.0 copy-start.2
  1.3 0.0 copy-start.4
  1.3 0.0 copy-start.6
  1.3 0.0 copy-start.7
  1.3 0.0 copy-start.11
  1.3 0.4 shard_map.128
  1.7 3.9 %collective-permute-start = (bf16[4,56,512]{2,1,0:T(8,128)(2,1)S(1)}, bf16[4,56,512]{2,1,0:T(8,128)(2,1)S(1)}, u32[]{:S(2)}, u32[]{:S(2)}) collective-permute-start(bf16[4,56,512]{2,1,0:T(8,128)(2,1)S(1)} %get-tuple-element.18), channel_id=1, source_target_pairs={{16,0},{17,1},{18,2},{19,3},{20,4},{21,5},{22,6},{23,7},{24,8},{25... | collective-permute-start | bytes 688136 | tf_op jit(solution)/shard_map/ppermute | solution.py:385
  5.7 0.0 copy-start.10
  5.7 5.5 %collective-permute-start.1 = (bf16[4,56,512]{2,1,0:T(8,128)(2,1)S(1)}, bf16[4,56,512]{2,1,0:T(8,128)(2,1)S(1)}, u32[]{:S(2)}, u32[]{:S(2)}) collective-permute-start(bf16[4,56,512]{2,1,0:T(8,128)(2,1)S(1)} %get-tuple-element.19), channel_id=1, source_target_pairs={{1,0},{2,1},{3,2},{4,3},{5,4},{6,5},{7,6},{8,7},{9,8},{10,9},{11,1... | collective-permute-start | bytes 688136 | tf_op jit(solution)/shard_map/ppermute | solution.py:385
  11.2 0.0 copy-done.1
  11.2 0.0 copy-done.2
  11.2 0.0 copy-done.4
  11.2 0.0 copy-done.6
  11.2 0.0 copy-done.7
  11.2 0.0 copy-done.11
  11.2 0.0 slice-start
  11.2 4.3 %shard_map.127 = (bf16[4,72,512]{2,1,0:T(8,128)(2,1)S(1)}, bf16[8,24,512]{2,1,0:T(8,128)(2,1)S(1)}) custom-call(bf16[4,288,512]{2,1,0:T(8,128)(2,1)S(1)} %bitcast.5, bf16[512,1536]{1,0:T(8,128)(2,1)S(1)} %copy-done.4, bf16[512,512]{1,0:T(8,128)(2,1)S(1)} %copy-done.7, bf16[512,2048]{1,0:T(8,128)(2,1)S(1)} %copy-done.1, bf16[2048,512]{1,0:T(8,128)(2,1)S(1)} %copy-done.2, ...), custom_call_target="tpu_custom_call" | custom-call | flops 2500000000 | bytes 7553024 | tf_op jit(solution)/shard_map/pallas_call | solution.py:206
  15.6 1.4 %collective-permute-start.2 = (bf16[8,24,512]{2,1,0:T(8,128)(2,1)S(1)}, bf16[8,24,512]{2,1,0:T(8,128)(2,1)S(1)}, u32[]{:S(2)}, u32[]{:S(2)}) collective-permute-start(bf16[8,24,512]{2,1,0:T(8,128)(2,1)S(1)} %get-tuple-element.22), channel_id=1, source_target_pairs={{17,0},{18,1},{19,2},{20,3},{21,4},{22,5},{23,6},{24,7},{25,8},{26... | collective-permute-start | bytes 589832 | tf_op jit(solution)/shard_map/ppermute | solution.py:385
  17.0 0.0 collective-permute-done.refs_0_.refs_1_
  17.0 0.0 collective-permute-done.1.refs_1_.refs_2_
  17.0 0.0 copy-done.10
  17.0 0.0 copy-start.12
  17.0 0.0 slice-start.1
  17.0 8.0 %shard_map.129 = (bf16[4,72,512]{2,1,0:T(8,128)(2,1)S(1)}, bf16[4,72,512]{2,1,0:T(8,128)(2,1)S(1)}, bf16[4,56,512]{2,1,0:T(8,128)(2,1)S(1)}, bf16[4,56,512]{2,1,0:T(8,128)(2,1)S(1)}) custom-call(bf16[4,56,512]{2,1,0:T(8,128)(2,1)S(1)} %collective-permute-done.refs_0_.refs_1_, bf16[4,56,512]{2,1,0:T(8,128)(2,1)S(1)} %collective-permute-done.1.refs_1_.refs_2_, ...), custom_call_target="tpu_custom_call" | custom-call | flops 5000000000 | bytes 8388608 | tf_op jit(solution)/shard_map/pallas_call | solution.py:206
  25.0 3.5 %collective-permute-start.3 = (bf16[4,56,512]{2,1,0:T(8,128)(2,1)S(1)}, bf16[4,56,512]{2,1,0:T(8,128)(2,1)S(1)}, u32[]{:S(2)}, u32[]{:S(2)}) collective-permute-start(bf16[4,56,512]{2,1,0:T(8,128)(2,1)S(1)} %get-tuple-element.23), channel_id=1, source_target_pairs={{1,0},{2,1},{3,2},{4,3},{5,4},{6,5},{7,6},{8,7},{9,8},{10,9},{11,1... | collective-permute-start | bytes 688136 | tf_op jit(solution)/shard_map/ppermute | solution.py:385
  28.5 0.9 %collective-permute-start.4 = (bf16[4,56,512]{2,1,0:T(8,128)(2,1)S(1)}, bf16[4,56,512]{2,1,0:T(8,128)(2,1)S(1)}, u32[]{:S(2)}, u32[]{:S(2)}) collective-permute-start(bf16[4,56,512]{2,1,0:T(8,128)(2,1)S(1)} %get-tuple-element.24), channel_id=1, source_target_pairs={{16,0},{17,1},{18,2},{19,3},{20,4},{21,5},{22,6},{23,7},{24,8},{25... | collective-permute-start | bytes 688136 | tf_op jit(solution)/shard_map/ppermute | solution.py:385
  29.4 0.0 collective-permute-done.2.refs_0_.refs_6_
  29.4 0.0 copy-done.12
  29.4 4.3 %shard_map.130.refs_3_ = bf16[4,72,512]{2,1,0:T(8,128)(2,1)S(1)} custom-call(bf16[8,24,512]{2,1,0:T(8,128)(2,1)S(1)} %collective-permute-done.2.refs_0_.refs_6_, bf16[4,56,512]{2,1,0:T(8,128)(2,1)S(1)} %collective-permute-done.refs_0_.refs_1_, bf16[4,56,512]{2,1,0:T(8,128)(2,1)S(1)} %collective-permute-done.1.refs_1_.refs_2_, ...), custom_call_target="tpu_custom_call" | custom-call | flops 2500000000 | bytes 8167424 | tf_op jit(solution)/shard_map/pallas_call | solution.py:206
  33.7 0.0 collective-permute-done.3.refs_4_
  33.7 0.9 %collective-permute-done.4.refs_5_ = bf16[4,56,512]{2,1,0:T(8,128)(2,1)S(1)} collective-permute-done((bf16[4,56,512]{2,1,0:T(8,128)(2,1)S(1)}, bf16[4,56,512]{2,1,0:T(8,128)(2,1)S(1)}, u32[]{:S(2)}, u32[]{:S(2)}) %collective-permute-start.4) | collective-permute-done | bytes 229408 | tf_op jit(solution)/shard_map/ppermute | solution.py:385
  34.6 0.0 slice-done
  34.6 0.0 slice-done.1
  34.6 0.0 copy-done
  34.6 0.0 copy-done.3
  34.6 0.0 copy-done.8
  34.6 0.0 copy-done.9
  34.7 8.8 %shard_map.131 = (bf16[3,6,4,1024]{3,2,1,0:T(4,128)(2,1)S(1)}, bf16[3,6,4,1024]{3,2,1,0:T(4,128)(2,1)S(1)}, bf16[3,6,4,1024]{3,2,1,0:T(4,128)(2,1)S(1)}, bf16[3,6,4,1024]{3,2,1,0:T(4,128)(2,1)S(1)}) custom-call(bf16[4,72,512]{2,1,0:T(8,128)(2,1)S(1)} %get-tuple-element.17.refs_7_.refs_0_, bf16[4,72,512]{2,1,0:T(8,128)(2,1)S(1)} %get-tuple-element.20.refs_1_, ...), custom_call_target="tpu_custom_call" | custom-call | flops 5000000000 | bytes 14878720 | tf_op jit(solution)/shard_map/pallas_call | solution.py:206
  43.5 0.1 collective-permute-start.5
  43.6 0.4 collective-permute-start.6
  44.0 1.1 %collective-permute-start.7 = (bf16[3,6,4,1024]{3,2,1,0:T(4,128)(2,1)S(1)}, bf16[3,6,4,1024]{3,2,1,0:T(4,128)(2,1)S(1)}, u32[]{:S(2)}, u32[]{:S(2)}) collective-permute-start(bf16[3,6,4,1024]{3,2,1,0:T(4,128)(2,1)S(1)} %get-tuple-element.28), channel_id=1, source_target_pairs={{127,0},{112,1},{113,2},{114,3},{115,4},{116,5},{117,6},{118,7},{1... | collective-permute-start | bytes 442376 | tf_op jit(solution)/shard_map/ppermute | solution.py:385
  45.1 6.7 %collective-permute-done.5.refs_1_ = bf16[3,6,4,1024]{3,2,1,0:T(4,128)(2,1)S(1)} collective-permute-done((bf16[3,6,4,1024]{3,2,1,0:T(4,128)(2,1)S(1)}, bf16[3,6,4,1024]{3,2,1,0:T(4,128)(2,1)S(1)}, u32[]{:S(2)}, u32[]{:S(2)}) %collective-permute-start.5) | collective-permute-done | bytes 147488 | tf_op jit(solution)/shard_map/ppermute | solution.py:385
  51.7 0.7 %collective-permute-done.6.refs_2_ = bf16[3,6,4,1024]{3,2,1,0:T(4,128)(2,1)S(1)} collective-permute-done((bf16[3,6,4,1024]{3,2,1,0:T(4,128)(2,1)S(1)}, bf16[3,6,4,1024]{3,2,1,0:T(4,128)(2,1)S(1)}, u32[]{:S(2)}, u32[]{:S(2)}) %collective-permute-start.6) | collective-permute-done | bytes 147488 | tf_op jit(solution)/shard_map/ppermute | solution.py:385
  52.4 6.1 %collective-permute-done.7.refs_3_ = bf16[3,6,4,1024]{3,2,1,0:T(4,128)(2,1)S(1)} collective-permute-done((bf16[3,6,4,1024]{3,2,1,0:T(4,128)(2,1)S(1)}, bf16[3,6,4,1024]{3,2,1,0:T(4,128)(2,1)S(1)}, u32[]{:S(2)}, u32[]{:S(2)}) %collective-permute-start.7) | collective-permute-done | bytes 147488 | tf_op jit(solution)/shard_map/ppermute | solution.py:385
  58.5 0.9 %shard_map.132 = bf16[6,12,4,1024]{3,2,1,0:T(4,128)(2,1)} custom-call(bf16[3,6,4,1024]{3,2,1,0:T(4,128)(2,1)S(1)} %get-tuple-element.25.refs_0_, bf16[3,6,4,1024]{3,2,1,0:T(4,128)(2,1)S(1)} %collective-permute-done.5.refs_1_, bf16[3,6,4,1024]{3,2,1,0:T(4,128)(2,1)S(1)} %collective-permute-done.6.refs_2_, ...), custom_call_target="tpu_custom_call" | custom-call | bytes 589824 | tf_op jit(solution)/shard_map/pallas_call | solution.py:206
  (5 shorter events, 0.0 us)
Async XLA Ops:
  0.0 1.3 %copy-start.5 = (bf16[4,12,24,512]{3,2,1,0:T(8,128)(2,1)S(1)}, bf16[4,12,24,512]{3,2,1,0:T(8,128)(2,1)}, u32[]{:S(2)}) copy-start(bf16[4,12,24,512]{3,2,1,0:T(8,128)(2,1)} %param.13) | copy-start | bytes 3538948
  1.3 9.9 %copy-start.1 = (bf16[512,2048]{1,0:T(8,128)(2,1)S(1)}, bf16[512,2048]{1,0:T(8,128)(2,1)}, u32[]{:S(2)}) copy-start(bf16[512,2048]{1,0:T(8,128)(2,1)} %refs_6_.3) | copy-start | bytes 6291460
  1.3 9.9 %copy-start.2 = (bf16[2048,512]{1,0:T(8,128)(2,1)S(1)}, bf16[2048,512]{1,0:T(8,128)(2,1)}, u32[]{:S(2)}) copy-start(bf16[2048,512]{1,0:T(8,128)(2,1)} %refs_7_.2) | copy-start | bytes 6291460
  1.3 9.9 %copy-start.4 = (bf16[512,1536]{1,0:T(8,128)(2,1)S(1)}, bf16[512,1536]{1,0:T(8,128)(2,1)}, u32[]{:S(2)}) copy-start(bf16[512,1536]{1,0:T(8,128)(2,1)} %refs_4_.5) | copy-start | bytes 4718596
  1.3 9.9 %copy-start.6 = (bf16[4,12,24,512]{3,2,1,0:T(8,128)(2,1)S(1)}, bf16[4,12,24,512]{3,2,1,0:T(8,128)(2,1)}, u32[]{:S(2)}) copy-start(bf16[4,12,24,512]{3,2,1,0:T(8,128)(2,1)} %param.13) | copy-start | bytes 3538948
  1.3 9.9 %copy-start.7 = (bf16[512,512]{1,0:T(8,128)(2,1)S(1)}, bf16[512,512]{1,0:T(8,128)(2,1)}, u32[]{:S(2)}) copy-start(bf16[512,512]{1,0:T(8,128)(2,1)} %refs_5_.4) | copy-start | bytes 1572868
  1.3 9.9 %copy-start.11 = (bf16[4,80,128]{2,1,0:T(8,128)(2,1)S(1)}, bf16[4,80,128]{2,1,0:T(8,128)(2,1)}, u32[]{:S(2)}) copy-start(bf16[4,80,128]{2,1,0:T(8,128)(2,1)} %constant.10.clone.refs_5_) | copy-start | bytes 245764
  1.7 15.2 %collective-permute-start = (bf16[4,56,512]{2,1,0:T(8,128)(2,1)S(1)}, bf16[4,56,512]{2,1,0:T(8,128)(2,1)S(1)}, u32[]{:S(2)}, u32[]{:S(2)}) collective-permute-start(bf16[4,56,512]{2,1,0:T(8,128)(2,1)S(1)} %get-tuple-element.18), channel_id=1, source_target_pairs={{16,0},{17,1},{18,2},{19,3},{20,4},{21,5},{22,6},{23,7},{24,8},{25... | collective-permute-start | bytes 688136 | tf_op jit(solution)/shard_map/ppermute | solution.py:385
  5.7 11.3 %copy-start.10 = (bf16[8,80,128]{2,1,0:T(8,128)(2,1)S(1)}, bf16[8,80,128]{2,1,0:T(8,128)(2,1)}, u32[]{:S(2)}) copy-start(bf16[8,80,128]{2,1,0:T(8,128)(2,1)} %constant.11.clone.refs_8_) | copy-start | bytes 491524
  5.7 11.3 %collective-permute-start.1 = (bf16[4,56,512]{2,1,0:T(8,128)(2,1)S(1)}, bf16[4,56,512]{2,1,0:T(8,128)(2,1)S(1)}, u32[]{:S(2)}, u32[]{:S(2)}) collective-permute-start(bf16[4,56,512]{2,1,0:T(8,128)(2,1)S(1)} %get-tuple-element.19), channel_id=1, source_target_pairs={{1,0},{2,1},{3,2},{4,3},{5,4},{6,5},{7,6},{8,7},{9,8},{10,9},{11,1... | collective-permute-start | bytes 688136 | tf_op jit(solution)/shard_map/ppermute | solution.py:385
  11.2 23.4 %slice-start = ((s8[6291456]{0:T(1024)(128)(4,1)}), s8[4194304]{0:T(1024)(128)(4,1)S(1)}, s32[]{:S(2)}) async-start(s8[6291456]{0:T(1024)(128)(4,1)} %bitcast.2), calls=%async_computation | async-start | bytes 8388608
  15.6 13.8 %collective-permute-start.2 = (bf16[8,24,512]{2,1,0:T(8,128)(2,1)S(1)}, bf16[8,24,512]{2,1,0:T(8,128)(2,1)S(1)}, u32[]{:S(2)}, u32[]{:S(2)}) collective-permute-start(bf16[8,24,512]{2,1,0:T(8,128)(2,1)S(1)} %get-tuple-element.22), channel_id=1, source_target_pairs={{17,0},{18,1},{19,2},{20,3},{21,4},{22,5},{23,6},{24,7},{25,8},{26... | collective-permute-start | bytes 589832 | tf_op jit(solution)/shard_map/ppermute | solution.py:385
  17.0 12.4 %copy-start.12 = (bf16[2,80,128]{2,1,0:T(8,128)(2,1)S(1)}, bf16[2,80,128]{2,1,0:T(8,128)(2,1)}, u32[]{:S(2)}) copy-start(bf16[2,80,128]{2,1,0:T(8,128)(2,1)} %constant.12.clone.refs_8_) | copy-start | bytes 122884
  17.0 17.6 %slice-start.1 = ((s8[6291456]{0:T(1024)(128)(4,1)}), s8[2097152]{0:T(1024)(128)(4,1)S(1)}, s32[]{:S(2)}) async-start(s8[6291456]{0:T(1024)(128)(4,1)} %bitcast.2), calls=%async_computation.1 | async-start | bytes 4194304
  25.0 8.7 %collective-permute-start.3 = (bf16[4,56,512]{2,1,0:T(8,128)(2,1)S(1)}, bf16[4,56,512]{2,1,0:T(8,128)(2,1)S(1)}, u32[]{:S(2)}, u32[]{:S(2)}) collective-permute-start(bf16[4,56,512]{2,1,0:T(8,128)(2,1)S(1)} %get-tuple-element.23), channel_id=1, source_target_pairs={{1,0},{2,1},{3,2},{4,3},{5,4},{6,5},{7,6},{8,7},{9,8},{10,9},{11,1... | collective-permute-start | bytes 688136 | tf_op jit(solution)/shard_map/ppermute | solution.py:385
  28.5 6.1 %copy-start = (bf16[2048,1024]{1,0:T(8,128)(2,1)S(1)}, bf16[2048,1024]{1,0:T(8,128)(2,1)}, u32[]{:S(2)}) copy-start(bf16[2048,1024]{1,0:T(8,128)(2,1)} %refs_9_.1) | copy-start | bytes 12582916
  28.5 6.1 %copy-start.3 = (bf16[1024,1024]{1,0:T(8,128)(2,1)S(1)}, bf16[1024,1024]{1,0:T(8,128)(2,1)}, u32[]{:S(2)}) copy-start(bf16[1024,1024]{1,0:T(8,128)(2,1)} %refs_11_.1) | copy-start | bytes 6291460
  28.5 6.1 %copy-start.8 = (bf16[4,288,128]{2,1,0:T(8,128)(2,1)S(1)}, bf16[4,288,128]{2,1,0:T(8,128)(2,1)}, u32[]{:S(2)}) copy-start(bf16[4,288,128]{2,1,0:T(8,128)(2,1)} %constant.13.clone.refs_7_) | copy-start | bytes 884740
  28.5 6.1 %copy-start.9 = (bf16[3,288,96]{2,1,0:T(8,128)(2,1)S(1)}, bf16[3,288,96]{2,1,0:T(8,128)(2,1)}, u32[]{:S(2)}) copy-start(bf16[3,288,96]{2,1,0:T(8,128)(2,1)} %constant.14.clone.refs_8_) | copy-start | bytes 497668
  28.5 6.1 %collective-permute-start.4 = (bf16[4,56,512]{2,1,0:T(8,128)(2,1)S(1)}, bf16[4,56,512]{2,1,0:T(8,128)(2,1)S(1)}, u32[]{:S(2)}, u32[]{:S(2)}) collective-permute-start(bf16[4,56,512]{2,1,0:T(8,128)(2,1)S(1)} %get-tuple-element.24), channel_id=1, source_target_pairs={{16,0},{17,1},{18,2},{19,3},{20,4},{21,5},{22,6},{23,7},{24,8},{25... | collective-permute-start | bytes 688136 | tf_op jit(solution)/shard_map/ppermute | solution.py:385
  43.5 8.3 %collective-permute-start.5 = (bf16[3,6,4,1024]{3,2,1,0:T(4,128)(2,1)S(1)}, bf16[3,6,4,1024]{3,2,1,0:T(4,128)(2,1)S(1)}, u32[]{:S(2)}, u32[]{:S(2)}) collective-permute-start(bf16[3,6,4,1024]{3,2,1,0:T(4,128)(2,1)S(1)} %get-tuple-element.26), channel_id=1, source_target_pairs={{15,0},{0,1},{1,2},{2,3},{3,4},{4,5},{5,6},{6,7},{7,8},{8,9},{9,10... | collective-permute-start | bytes 442376 | tf_op jit(solution)/shard_map/ppermute | solution.py:385
  43.6 8.9 %collective-permute-start.6 = (bf16[3,6,4,1024]{3,2,1,0:T(4,128)(2,1)S(1)}, bf16[3,6,4,1024]{3,2,1,0:T(4,128)(2,1)S(1)}, u32[]{:S(2)}, u32[]{:S(2)}) collective-permute-start(bf16[3,6,4,1024]{3,2,1,0:T(4,128)(2,1)S(1)} %get-tuple-element.27), channel_id=1, source_target_pairs={{112,0},{113,1},{114,2},{115,3},{116,4},{117,5},{118,6},{119,7},{1... | collective-permute-start | bytes 442376 | tf_op jit(solution)/shard_map/ppermute | solution.py:385
  44.0 14.5 %collective-permute-start.7 = (bf16[3,6,4,1024]{3,2,1,0:T(4,128)(2,1)S(1)}, bf16[3,6,4,1024]{3,2,1,0:T(4,128)(2,1)S(1)}, u32[]{:S(2)}, u32[]{:S(2)}) collective-permute-start(bf16[3,6,4,1024]{3,2,1,0:T(4,128)(2,1)S(1)} %get-tuple-element.28), channel_id=1, source_target_pairs={{127,0},{112,1},{113,2},{114,3},{115,4},{116,5},{117,6},{118,7},{1... | collective-permute-start | bytes 442376 | tf_op jit(solution)/shard_map/ppermute | solution.py:385

commit v5 on v4

--- a/solution.py
+++ b/solution.py
@@ -399,12 +399,15 @@
     blocks = fine_quads(QUADS[:1], sources, weights, {}, ("both",))
     corners = shift({"both": blocks.pop("both")})["both"]
     sources["both"] = corners
-    second = fine_quads(QUADS[1:3], sources, weights, blocks, ("lon", "lat"))
-    pieces = shift({name: second.pop(name) for name in ("lon", "lat")}) | {"both": corners}
-    blocks |= second
+    second = fine_quads(QUADS[1:2], sources, weights, blocks, ("lat",))
+    pieces = {"both": corners} | shift({"lat": second.pop("lat")})
+    third = fine_quads(QUADS[2:3], sources, weights, blocks, ("lon",))
+    pieces |= shift({"lon": third.pop("lon")})
+    blocks |= second | third
     blocks |= fine_quads(QUADS[3:], sources, weights, {}, ())
     parts = coarse(blocks, pieces, merge_weight, coarse_qkv, coarse_out)
-    moved = [parts[0], receive(parts[1], 0, -1), receive(parts[2], -1, 0), receive(parts[3], -1, -1)]
+    corner, lat = receive(parts[3], -1, -1), receive(parts[2], -1, 0)
+    moved = [parts[0], receive(parts[1], 0, -1), lat, corner]
     return assemble(moved)
 
 

time: 59.4 us -> 58.8 us (0.990)
  Pallas kernels: 26.7 us -> 27.6 us
  starting transfers between devices: 16.8 us -> 16 us
  waiting for transfers between devices: 14.3 us -> 13.5 us
    pallas_call x6 -> x7, Pallas kernels: 26.7 us -> 27.6 us  [run(): pl.pallas_call(kernel, out_shape=[jax.ShapeDtypeStruct(shape, BF16) for s...]
    ppermute x8, waiting for transfers between devices: 14.3 us -> 13.5 us  [receive(): return lax.ppermute(array, ('lat', 'lon'), pairs)]
    ppermute x8, starting transfers between devices: 16.8 us -> 16 us  [receive(): return lax.ppermute(array, ('lat', 'lon'), pairs)]
    unnamed x30 -> x32, local copies, waits for them, and re-layouts: 1.34 us -> 1.35 us
  transfers between devices with their start and end apart: 8 -> 8, of which waited for: 4 -> 3; matrix products, arithmetic and copies ran while one was open for 0% -> 0% of each run, Pallas kernels for 28% -> 30%
where the time goes in v5:
time: 58.8 us; the launch traced here: 58.7 us
  Pallas kernels  27.6 us (47%)
  starting transfers between devices  16 us (27%)
  waiting for transfers between devices  13.5 us (23%)
  local copies, waits for them, and re-layouts  1.35 us (2%)
    pallas_call x7, Pallas kernels, run(): pl.pallas_call(kernel, out_shape=[jax.ShapeDtypeStruct(shape, BF16) for s...  27.6 us
    ppermute x8, starting transfers between devices, receive(): return lax.ppermute(array, ('lat', 'lon'), pairs)  16 us
    ppermute x8, waiting for transfers between devices, receive(): return lax.ppermute(array, ('lat', 'lon'), pairs)  13.5 us
    unnamed x32, local copies, waits for them, and re-layouts  1.35 us
  transfers between devices with their start and end apart: 8, of which 3 were waited for; matrix products, arithmetic and copies ran while one was open for 0% of the time, Pallas kernels for 30%

profile of v5, /device:TPU:0, one launch (start us, length us, event | category | flops | bytes accessed | tf_op | source)
XLA Modules:
  0.0 58.7 jit_solution(9917090149399125745)
XLA Ops:
  0.0 0.0 copy-start.5
  0.0 1.3 %copy-done.5 = bf16[4,12,24,512]{3,2,1,0:T(8,128)(2,1)S(1)} copy-done((bf16[4,12,24,512]{3,2,1,0:T(8,128)(2,1)S(1)}, bf16[4,12,24,512]{3,2,1,0:T(8,128)(2,1)}, u32[]{:S(2)}) %copy-start.5) | copy-done | bytes 1179672
  1.3 0.0 copy-start.7
  1.3 0.0 copy-start.12
  1.3 0.4 shard_map.137
  1.7 6.2 %collective-permute-start = (bf16[4,56,512]{2,1,0:T(8,128)(2,1)S(1)}, bf16[4,56,512]{2,1,0:T(8,128)(2,1)S(1)}, u32[]{:S(2)}, u32[]{:S(2)}) collective-permute-start(bf16[4,56,512]{2,1,0:T(8,128)(2,1)S(1)} %get-tuple-element.18), channel_id=1, source_target_pairs={{1,0},{2,1},{3,2},{4,3},{5,4},{6,5},{7,6},{8,7},{9,8},{10,9},{11,1... | collective-permute-start | bytes 688136 | tf_op jit(solution)/shard_map/ppermute | solution.py:385
  8.0 2.9 %collective-permute-start.1 = (bf16[4,56,512]{2,1,0:T(8,128)(2,1)S(1)}, bf16[4,56,512]{2,1,0:T(8,128)(2,1)S(1)}, u32[]{:S(2)}, u32[]{:S(2)}) collective-permute-start(bf16[4,56,512]{2,1,0:T(8,128)(2,1)S(1)} %get-tuple-element.20), channel_id=1, source_target_pairs={{16,0},{17,1},{18,2},{19,3},{20,4},{21,5},{22,6},{23,7},{24,8},{25... | collective-permute-start | bytes 688136 | tf_op jit(solution)/shard_map/ppermute | solution.py:385
  10.9 0.0 copy-done.1
  10.9 0.0 copy-done.2
  10.9 0.0 copy-done.4
  10.9 0.0 copy-done.6
  10.9 0.0 copy-done.7
  10.9 0.0 copy-done.12
  10.9 4.3 %shard_map.136 = (bf16[4,72,512]{2,1,0:T(8,128)(2,1)S(1)}, bf16[8,24,512]{2,1,0:T(8,128)(2,1)S(1)}) custom-call(bf16[4,288,512]{2,1,0:T(8,128)(2,1)S(1)} %bitcast.5, bf16[512,1536]{1,0:T(8,128)(2,1)S(1)} %copy-done.4, bf16[512,512]{1,0:T(8,128)(2,1)S(1)} %copy-done.7, bf16[512,2048]{1,0:T(8,128)(2,1)S(1)} %copy-done.1, bf16[2048,512]{1,0:T(8,128)(2,1)S(1)} %copy-done.2, ...), custom_call_target="tpu_custom_call" | custom-call | flops 2500000000 | bytes 7553024 | tf_op jit(solution)/shard_map/pallas_call | solution.py:206
  15.2 1.8 %collective-permute-start.2 = (bf16[8,24,512]{2,1,0:T(8,128)(2,1)S(1)}, bf16[8,24,512]{2,1,0:T(8,128)(2,1)S(1)}, u32[]{:S(2)}, u32[]{:S(2)}) collective-permute-start(bf16[8,24,512]{2,1,0:T(8,128)(2,1)S(1)} %get-tuple-element.22), channel_id=1, source_target_pairs={{17,0},{18,1},{19,2},{20,3},{21,4},{22,5},{23,6},{24,7},{25,8},{26... | collective-permute-start | bytes 589832 | tf_op jit(solution)/shard_map/ppermute | solution.py:385
  17.0 0.0 collective-permute-done.refs_0_.refs_2_
  17.0 0.0 copy-done.11
  17.0 4.4 %shard_map.138 = (bf16[4,72,512]{2,1,0:T(8,128)(2,1)S(1)}, bf16[4,56,512]{2,1,0:T(8,128)(2,1)S(1)}) custom-call(bf16[4,56,512]{2,1,0:T(8,128)(2,1)S(1)} %collective-permute-done.refs_0_.refs_2_, bf16[4,288,512]{2,1,0:T(8,128)(2,1)S(1)} %bitcast.6, bf16[512,1536]{1,0:T(8,128)(2,1)S(1)} %copy-done.4, bf16[512,512]{1,0:T(8,128)(2,1)S(1)} %copy-done.7, ...), custom_call_target="tpu_custom_call" | custom-call | flops 2500000000 | bytes 8077312 | tf_op jit(solution)/shard_map/pallas_call | solution.py:206
  21.3 0.0 copy-start.13
  21.3 1.4 %collective-permute-start.4 = (bf16[4,56,512]{2,1,0:T(8,128)(2,1)S(1)}, bf16[4,56,512]{2,1,0:T(8,128)(2,1)S(1)}, u32[]{:S(2)}, u32[]{:S(2)}) collective-permute-start(bf16[4,56,512]{2,1,0:T(8,128)(2,1)S(1)} %get-tuple-element.24), channel_id=1, source_target_pairs={{16,0},{17,1},{18,2},{19,3},{20,4},{21,5},{22,6},{23,7},{24,8},{25... | collective-permute-start | bytes 688136 | tf_op jit(solution)/shard_map/ppermute | solution.py:385
  22.7 0.0 collective-permute-done.1.refs_0_.refs_1_
  22.7 0.0 copy-done.10
  22.7 4.6 %shard_map.139 = (bf16[4,72,512]{2,1,0:T(8,128)(2,1)S(1)}, bf16[4,56,512]{2,1,0:T(8,128)(2,1)S(1)}) custom-call(bf16[4,56,512]{2,1,0:T(8,128)(2,1)S(1)} %collective-permute-done.1.refs_0_.refs_1_, bf16[4,288,512]{2,1,0:T(8,128)(2,1)S(1)} %bitcast.7, bf16[512,1536]{1,0:T(8,128)(2,1)S(1)} %copy-done.4, bf16[512,512]{1,0:T(8,128)(2,1)S(1)} %copy-done.7, ...), custom_call_target="tpu_custom_call" | custom-call | flops 2500000000 | bytes 8077312 | tf_op jit(solution)/shard_map/pallas_call | solution.py:206
  27.3 0.0 slice-start.1
  27.3 0.0 copy-start
  27.3 0.0 copy-start.3
  27.3 0.0 copy-start.8
  27.3 0.0 copy-start.9
  27.3 2.2 %collective-permute-start.3 = (bf16[4,56,512]{2,1,0:T(8,128)(2,1)S(1)}, bf16[4,56,512]{2,1,0:T(8,128)(2,1)S(1)}, u32[]{:S(2)}, u32[]{:S(2)}) collective-permute-start(bf16[4,56,512]{2,1,0:T(8,128)(2,1)S(1)} %get-tuple-element.23), channel_id=1, source_target_pairs={{1,0},{2,1},{3,2},{4,3},{5,4},{6,5},{7,6},{8,7},{9,8},{10,9},{11,1... | collective-permute-start | bytes 688136 | tf_op jit(solution)/shard_map/ppermute | solution.py:385
  29.6 0.0 collective-permute-done.2.refs_0_.refs_6_
  29.6 0.0 copy-done.13
  29.6 4.3 %shard_map.140.refs_3_ = bf16[4,72,512]{2,1,0:T(8,128)(2,1)S(1)} custom-call(bf16[8,24,512]{2,1,0:T(8,128)(2,1)S(1)} %collective-permute-done.2.refs_0_.refs_6_, bf16[4,56,512]{2,1,0:T(8,128)(2,1)S(1)} %collective-permute-done.1.refs_0_.refs_1_, bf16[4,56,512]{2,1,0:T(8,128)(2,1)S(1)} %collective-permute-done.refs_0_.refs_2_, ...), custom_call_target="tpu_custom_call" | custom-call | flops 2500000000 | bytes 8167424 | tf_op jit(solution)/shard_map/pallas_call | solution.py:206
  33.8 0.0 collective-permute-done.4.refs_5_
  33.9 0.0 collective-permute-done.3.refs_4_
  33.9 0.0 slice-done
  33.9 0.0 slice-done.1
  33.9 0.0 copy-done
  33.9 0.0 copy-done.3
  33.9 0.0 copy-done.8
  33.9 0.0 copy-done.9
  33.9 8.8 %shard_map.141 = (bf16[3,6,4,1024]{3,2,1,0:T(4,128)(2,1)S(1)}, bf16[3,6,4,1024]{3,2,1,0:T(4,128)(2,1)S(1)}, bf16[3,6,4,1024]{3,2,1,0:T(4,128)(2,1)S(1)}, bf16[3,6,4,1024]{3,2,1,0:T(4,128)(2,1)S(1)}) custom-call(bf16[4,72,512]{2,1,0:T(8,128)(2,1)S(1)} %get-tuple-element.17.refs_6_.refs_0_, bf16[4,72,512]{2,1,0:T(8,128)(2,1)S(1)} %get-tuple-element.19.refs_1_, ...), custom_call_target="tpu_custom_call" | custom-call | flops 5000000000 | bytes 14878720 | tf_op jit(solution)/shard_map/pallas_call | solution.py:206
  42.7 0.1 collective-permute-start.5
  42.8 0.4 collective-permute-start.6
  43.2 1.1 %collective-permute-start.7 = (bf16[3,6,4,1024]{3,2,1,0:T(4,128)(2,1)S(1)}, bf16[3,6,4,1024]{3,2,1,0:T(4,128)(2,1)S(1)}, u32[]{:S(2)}, u32[]{:S(2)}) collective-permute-start(bf16[3,6,4,1024]{3,2,1,0:T(4,128)(2,1)S(1)} %get-tuple-element.28), channel_id=1, source_target_pairs={{127,0},{112,1},{113,2},{114,3},{115,4},{116,5},{117,6},{118,7},{1... | collective-permute-start | bytes 442376 | tf_op jit(solution)/shard_map/ppermute | solution.py:385
  44.3 6.7 %collective-permute-done.5.refs_1_ = bf16[3,6,4,1024]{3,2,1,0:T(4,128)(2,1)S(1)} collective-permute-done((bf16[3,6,4,1024]{3,2,1,0:T(4,128)(2,1)S(1)}, bf16[3,6,4,1024]{3,2,1,0:T(4,128)(2,1)S(1)}, u32[]{:S(2)}, u32[]{:S(2)}) %collective-permute-start.5) | collective-permute-done | bytes 147488 | tf_op jit(solution)/shard_map/ppermute | solution.py:385
  51.0 0.7 %collective-permute-done.6.refs_2_ = bf16[3,6,4,1024]{3,2,1,0:T(4,128)(2,1)S(1)} collective-permute-done((bf16[3,6,4,1024]{3,2,1,0:T(4,128)(2,1)S(1)}, bf16[3,6,4,1024]{3,2,1,0:T(4,128)(2,1)S(1)}, u32[]{:S(2)}, u32[]{:S(2)}) %collective-permute-start.6) | collective-permute-done | bytes 147488 | tf_op jit(solution)/shard_map/ppermute | solution.py:385
  51.7 6.2 %collective-permute-done.7.refs_3_ = bf16[3,6,4,1024]{3,2,1,0:T(4,128)(2,1)S(1)} collective-permute-done((bf16[3,6,4,1024]{3,2,1,0:T(4,128)(2,1)S(1)}, bf16[3,6,4,1024]{3,2,1,0:T(4,128)(2,1)S(1)}, u32[]{:S(2)}, u32[]{:S(2)}) %collective-permute-start.7) | collective-permute-done | bytes 147488 | tf_op jit(solution)/shard_map/ppermute | solution.py:385
  57.8 0.9 %shard_map.142 = bf16[6,12,4,1024]{3,2,1,0:T(4,128)(2,1)} custom-call(bf16[3,6,4,1024]{3,2,1,0:T(4,128)(2,1)S(1)} %get-tuple-element.25.refs_0_, bf16[3,6,4,1024]{3,2,1,0:T(4,128)(2,1)S(1)} %collective-permute-done.5.refs_1_, bf16[3,6,4,1024]{3,2,1,0:T(4,128)(2,1)S(1)} %collective-permute-done.6.refs_2_, ...), custom_call_target="tpu_custom_call" | custom-call | bytes 589824 | tf_op jit(solution)/shard_map/pallas_call | solution.py:206
  (8 shorter events, 0.0 us)
Async XLA Ops:
  0.0 1.3 %copy-start.5 = (bf16[4,12,24,512]{3,2,1,0:T(8,128)(2,1)S(1)}, bf16[4,12,24,512]{3,2,1,0:T(8,128)(2,1)}, u32[]{:S(2)}) copy-start(bf16[4,12,24,512]{3,2,1,0:T(8,128)(2,1)} %param.14) | copy-start | bytes 3538948
  1.3 9.6 %copy-start.1 = (bf16[512,2048]{1,0:T(8,128)(2,1)S(1)}, bf16[512,2048]{1,0:T(8,128)(2,1)}, u32[]{:S(2)}) copy-start(bf16[512,2048]{1,0:T(8,128)(2,1)} %refs_6_.1) | copy-start | bytes 6291460
  1.3 9.6 %copy-start.2 = (bf16[2048,512]{1,0:T(8,128)(2,1)S(1)}, bf16[2048,512]{1,0:T(8,128)(2,1)}, u32[]{:S(2)}) copy-start(bf16[2048,512]{1,0:T(8,128)(2,1)} %refs_7_.4) | copy-start | bytes 6291460
  1.3 9.6 %copy-start.4 = (bf16[512,1536]{1,0:T(8,128)(2,1)S(1)}, bf16[512,1536]{1,0:T(8,128)(2,1)}, u32[]{:S(2)}) copy-start(bf16[512,1536]{1,0:T(8,128)(2,1)} %refs_4_.7) | copy-start | bytes 4718596
  1.3 9.6 %copy-start.6 = (bf16[4,12,24,512]{3,2,1,0:T(8,128)(2,1)S(1)}, bf16[4,12,24,512]{3,2,1,0:T(8,128)(2,1)}, u32[]{:S(2)}) copy-start(bf16[4,12,24,512]{3,2,1,0:T(8,128)(2,1)} %param.14) | copy-start | bytes 3538948
  1.3 9.6 %copy-start.7 = (bf16[512,512]{1,0:T(8,128)(2,1)S(1)}, bf16[512,512]{1,0:T(8,128)(2,1)}, u32[]{:S(2)}) copy-start(bf16[512,512]{1,0:T(8,128)(2,1)} %refs_5_.6) | copy-start | bytes 1572868
  1.3 9.6 %copy-start.12 = (bf16[4,80,128]{2,1,0:T(8,128)(2,1)S(1)}, bf16[4,80,128]{2,1,0:T(8,128)(2,1)}, u32[]{:S(2)}) copy-start(bf16[4,80,128]{2,1,0:T(8,128)(2,1)} %constant.12.clone.refs_5_) | copy-start | bytes 245764
  1.7 15.2 %collective-permute-start = (bf16[4,56,512]{2,1,0:T(8,128)(2,1)S(1)}, bf16[4,56,512]{2,1,0:T(8,128)(2,1)S(1)}, u32[]{:S(2)}, u32[]{:S(2)}) collective-permute-start(bf16[4,56,512]{2,1,0:T(8,128)(2,1)S(1)} %get-tuple-element.18), channel_id=1, source_target_pairs={{1,0},{2,1},{3,2},{4,3},{5,4},{6,5},{7,6},{8,7},{9,8},{10,9},{11,1... | collective-permute-start | bytes 688136 | tf_op jit(solution)/shard_map/ppermute | solution.py:385
  8.0 9.0 %copy-start.11 = (bf16[4,80,128]{2,1,0:T(8,128)(2,1)S(1)}, bf16[4,80,128]{2,1,0:T(8,128)(2,1)}, u32[]{:S(2)}) copy-start(bf16[4,80,128]{2,1,0:T(8,128)(2,1)} %constant.13.clone.refs_7_) | copy-start | bytes 245764
  8.0 14.7 %collective-permute-start.1 = (bf16[4,56,512]{2,1,0:T(8,128)(2,1)S(1)}, bf16[4,56,512]{2,1,0:T(8,128)(2,1)S(1)}, u32[]{:S(2)}, u32[]{:S(2)}) collective-permute-start(bf16[4,56,512]{2,1,0:T(8,128)(2,1)S(1)} %get-tuple-element.20), channel_id=1, source_target_pairs={{16,0},{17,1},{18,2},{19,3},{20,4},{21,5},{22,6},{23,7},{24,8},{25... | collective-permute-start | bytes 688136 | tf_op jit(solution)/shard_map/ppermute | solution.py:385
  15.2 14.4 %collective-permute-start.2 = (bf16[8,24,512]{2,1,0:T(8,128)(2,1)S(1)}, bf16[8,24,512]{2,1,0:T(8,128)(2,1)S(1)}, u32[]{:S(2)}, u32[]{:S(2)}) collective-permute-start(bf16[8,24,512]{2,1,0:T(8,128)(2,1)S(1)} %get-tuple-element.22), channel_id=1, source_target_pairs={{17,0},{18,1},{19,2},{20,3},{21,4},{22,5},{23,6},{24,7},{25,8},{26... | collective-permute-start | bytes 589832 | tf_op jit(solution)/shard_map/ppermute | solution.py:385
  17.0 5.7 %copy-start.10 = (bf16[4,80,128]{2,1,0:T(8,128)(2,1)S(1)}, bf16[4,80,128]{2,1,0:T(8,128)(2,1)}, u32[]{:S(2)}) copy-start(bf16[4,80,128]{2,1,0:T(8,128)(2,1)} %constant.14.clone.refs_7_) | copy-start | bytes 245764
  21.3 8.2 %copy-start.13 = (bf16[2,80,128]{2,1,0:T(8,128)(2,1)S(1)}, bf16[2,80,128]{2,1,0:T(8,128)(2,1)}, u32[]{:S(2)}) copy-start(bf16[2,80,128]{2,1,0:T(8,128)(2,1)} %constant.15.clone.refs_8_) | copy-start | bytes 122884
  21.3 12.5 %collective-permute-start.4 = (bf16[4,56,512]{2,1,0:T(8,128)(2,1)S(1)}, bf16[4,56,512]{2,1,0:T(8,128)(2,1)S(1)}, u32[]{:S(2)}, u32[]{:S(2)}) collective-permute-start(bf16[4,56,512]{2,1,0:T(8,128)(2,1)S(1)} %get-tuple-element.24), channel_id=1, source_target_pairs={{16,0},{17,1},{18,2},{19,3},{20,4},{21,5},{22,6},{23,7},{24,8},{25... | collective-permute-start | bytes 688136 | tf_op jit(solution)/shard_map/ppermute | solution.py:385
  22.7 11.2 %slice-start = ((s8[6291456]{0:T(1024)(128)(4,1)}), s8[4194304]{0:T(1024)(128)(4,1)S(1)}, s32[]{:S(2)}) async-start(s8[6291456]{0:T(1024)(128)(4,1)} %bitcast.2), calls=%async_computation | async-start | bytes 8388608
  27.3 6.6 %slice-start.1 = ((s8[6291456]{0:T(1024)(128)(4,1)}), s8[2097152]{0:T(1024)(128)(4,1)S(1)}, s32[]{:S(2)}) async-start(s8[6291456]{0:T(1024)(128)(4,1)} %bitcast.2), calls=%async_computation.1 | async-start | bytes 4194304
  27.3 6.6 %copy-start = (bf16[2048,1024]{1,0:T(8,128)(2,1)S(1)}, bf16[2048,1024]{1,0:T(8,128)(2,1)}, u32[]{:S(2)}) copy-start(bf16[2048,1024]{1,0:T(8,128)(2,1)} %refs_9_.1) | copy-start | bytes 12582916
  27.3 6.6 %copy-start.3 = (bf16[1024,1024]{1,0:T(8,128)(2,1)S(1)}, bf16[1024,1024]{1,0:T(8,128)(2,1)}, u32[]{:S(2)}) copy-start(bf16[1024,1024]{1,0:T(8,128)(2,1)} %refs_11_.1) | copy-start | bytes 6291460
  27.3 6.6 %copy-start.8 = (bf16[4,288,128]{2,1,0:T(8,128)(2,1)S(1)}, bf16[4,288,128]{2,1,0:T(8,128)(2,1)}, u32[]{:S(2)}) copy-start(bf16[4,288,128]{2,1,0:T(8,128)(2,1)} %constant.16.clone.refs_7_) | copy-start | bytes 884740
  27.3 6.6 %copy-start.9 = (bf16[3,288,96]{2,1,0:T(8,128)(2,1)S(1)}, bf16[3,288,96]{2,1,0:T(8,128)(2,1)}, u32[]{:S(2)}) copy-start(bf16[3,288,96]{2,1,0:T(8,128)(2,1)} %constant.17.clone.refs_8_) | copy-start | bytes 497668
  27.3 6.5 %collective-permute-start.3 = (bf16[4,56,512]{2,1,0:T(8,128)(2,1)S(1)}, bf16[4,56,512]{2,1,0:T(8,128)(2,1)S(1)}, u32[]{:S(2)}, u32[]{:S(2)}) collective-permute-start(bf16[4,56,512]{2,1,0:T(8,128)(2,1)S(1)} %get-tuple-element.23), channel_id=1, source_target_pairs={{1,0},{2,1},{3,2},{4,3},{5,4},{6,5},{7,6},{8,7},{9,8},{10,9},{11,1... | collective-permute-start | bytes 688136 | tf_op jit(solution)/shard_map/ppermute | solution.py:385
  42.7 8.3 %collective-permute-start.5 = (bf16[3,6,4,1024]{3,2,1,0:T(4,128)(2,1)S(1)}, bf16[3,6,4,1024]{3,2,1,0:T(4,128)(2,1)S(1)}, u32[]{:S(2)}, u32[]{:S(2)}) collective-permute-start(bf16[3,6,4,1024]{3,2,1,0:T(4,128)(2,1)S(1)} %get-tuple-element.26), channel_id=1, source_target_pairs={{15,0},{0,1},{1,2},{2,3},{3,4},{4,5},{5,6},{6,7},{7,8},{8,9},{9,10... | collective-permute-start | bytes 442376 | tf_op jit(solution)/shard_map/ppermute | solution.py:385
  42.8 8.9 %collective-permute-start.6 = (bf16[3,6,4,1024]{3,2,1,0:T(4,128)(2,1)S(1)}, bf16[3,6,4,1024]{3,2,1,0:T(4,128)(2,1)S(1)}, u32[]{:S(2)}, u32[]{:S(2)}) collective-permute-start(bf16[3,6,4,1024]{3,2,1,0:T(4,128)(2,1)S(1)} %get-tuple-element.27), channel_id=1, source_target_pairs={{112,0},{113,1},{114,2},{115,3},{116,4},{117,5},{118,6},{119,7},{1... | collective-permute-start | bytes 442376 | tf_op jit(solution)/shard_map/ppermute | solution.py:385
  43.2 14.7 %collective-permute-start.7 = (bf16[3,6,4,1024]{3,2,1,0:T(4,128)(2,1)S(1)}, bf16[3,6,4,1024]{3,2,1,0:T(4,128)(2,1)S(1)}, u32[]{:S(2)}, u32[]{:S(2)}) collective-permute-start(bf16[3,6,4,1024]{3,2,1,0:T(4,128)(2,1)S(1)} %get-tuple-element.28), channel_id=1, source_target_pairs={{127,0},{112,1},{113,2},{114,3},{115,4},{116,5},{117,6},{118,7},{1... | collective-permute-start | bytes 442376 | tf_op jit(solution)/shard_map/ppermute | solution.py:385

commit v6 on v5

--- a/solution.py
+++ b/solution.py
@@ -100,13 +100,13 @@
 
 
 def last_send_table():
-    table = np.zeros((3, 288, 96), np.float32)
+    table = np.zeros((3, 288, 128), np.float32)
     for place, level in enumerate(ORDER):
         for i in range(6):
             for j in range(12):
                 part = (i // 3) * 2 + j // 6
                 to, at = part * 72 + ((i % 3) * 6 + j % 6) * 4 + level, place * 72 + i * 12 + j
-                table[at // 96, to, at % 96] = 1
+                table[at // 128, to, at % 128] = 1
     return table
 
 
@@ -145,11 +145,16 @@
     full = lax.dot_general(
         weights.astype(BF16), v, (((0,), (0,)), ((), ())), preferred_element_type=F32
     )
-    lane_head = lax.broadcasted_iota(jnp.int32, (1, GROUP), 1) // HEAD
-    out = full[:144]
-    for h in range(1, 8):
-        out = jnp.where(lane_head == h, full[h * 144 : h * 144 + 144], out)
-    return out.astype(BF16)
+    lane_head = lax.broadcasted_iota(jnp.int32, (1, 128), 1) // HEAD
+    halves = []
+    for side in range(2):
+        lanes = slice(side * 128, side * 128 + 128)
+        out = full[side * 576 : side * 576 + 144, lanes]
+        for h in range(1, 4):
+            start = (side * 4 + h) * 144
+            out = jnp.where(lane_head == h, full[start : start + 144, lanes], out)
+        halves.append(out)
+    return jnp.concatenate(halves, axis=1).astype(BF16)
 
 
 def attend(qkv, width, biases):
@@ -350,7 +355,8 @@
         qkv = dot(normalize(merged).astype(BF16), refs["qkv"][...]).astype(BF16)
         mixed = attend(qkv, 1024, [bias])
         result = (merged + dot(mixed, refs["out"][...])).astype(BF16)
-        parts = sum(dot(refs["last"][at], result[96 * at : 96 * at + 96]) for at in range(3))
+        last = jnp.concatenate([refs["last"][at] for at in range(3)], axis=1)
+        parts = dot(last[:, :288], result)
         for part in range(4):
             for at in range(18):
                 start = part * 72 + at * 4

time: 58.8 us -> 58.6 us (level)
  no operation moved by 1% of the time
where the time goes in v6:
time: 58.6 us; the launch traced here: 58.5 us
  Pallas kernels  27.3 us (47%)
  starting transfers between devices  16 us (27%)
  waiting for transfers between devices  13.6 us (23%)
  local copies, waits for them, and re-layouts  1.35 us (2%)
    pallas_call x7, Pallas kernels, run(): pl.pallas_call(kernel, out_shape=[jax.ShapeDtypeStruct(shape, BF16) for s...  27.3 us
    ppermute x8, starting transfers between devices, receive(): return lax.ppermute(array, ('lat', 'lon'), pairs)  16 us
    ppermute x8, waiting for transfers between devices, receive(): return lax.ppermute(array, ('lat', 'lon'), pairs)  13.6 us
    unnamed x32, local copies, waits for them, and re-layouts  1.35 us
  transfers between devices with their start and end apart: 8, of which 3 were waited for; matrix products, arithmetic and copies ran while one was open for 0% of the time, Pallas kernels for 30%

profile of v6, /device:TPU:0, one launch (start us, length us, event | category | flops | bytes accessed | tf_op | source)
XLA Modules:
  0.0 58.5 jit_solution(7696329805337328841)
XLA Ops:
  0.0 0.0 copy-start.5
  0.0 1.3 %copy-done.5 = bf16[4,12,24,512]{3,2,1,0:T(8,128)(2,1)S(1)} copy-done((bf16[4,12,24,512]{3,2,1,0:T(8,128)(2,1)S(1)}, bf16[4,12,24,512]{3,2,1,0:T(8,128)(2,1)}, u32[]{:S(2)}) %copy-start.5) | copy-done | bytes 1179672
  1.3 0.0 copy-start.7
  1.3 0.0 copy-start.12
  1.3 0.4 shard_map.137
  1.7 6.2 %collective-permute-start = (bf16[4,56,512]{2,1,0:T(8,128)(2,1)S(1)}, bf16[4,56,512]{2,1,0:T(8,128)(2,1)S(1)}, u32[]{:S(2)}, u32[]{:S(2)}) collective-permute-start(bf16[4,56,512]{2,1,0:T(8,128)(2,1)S(1)} %get-tuple-element.18), channel_id=1, source_target_pairs={{1,0},{2,1},{3,2},{4,3},{5,4},{6,5},{7,6},{8,7},{9,8},{10,9},{11,1... | collective-permute-start | bytes 688136 | tf_op jit(solution)/shard_map/ppermute | solution.py:391
  8.0 2.9 %collective-permute-start.1 = (bf16[4,56,512]{2,1,0:T(8,128)(2,1)S(1)}, bf16[4,56,512]{2,1,0:T(8,128)(2,1)S(1)}, u32[]{:S(2)}, u32[]{:S(2)}) collective-permute-start(bf16[4,56,512]{2,1,0:T(8,128)(2,1)S(1)} %get-tuple-element.20), channel_id=1, source_target_pairs={{16,0},{17,1},{18,2},{19,3},{20,4},{21,5},{22,6},{23,7},{24,8},{25... | collective-permute-start | bytes 688136 | tf_op jit(solution)/shard_map/ppermute | solution.py:391
  10.9 0.0 copy-done.1
  10.9 0.0 copy-done.2
  10.9 0.0 copy-done.4
  10.9 0.0 copy-done.6
  10.9 0.0 copy-done.7
  10.9 0.0 copy-done.12
  10.9 4.3 %shard_map.136 = (bf16[4,72,512]{2,1,0:T(8,128)(2,1)S(1)}, bf16[8,24,512]{2,1,0:T(8,128)(2,1)S(1)}) custom-call(bf16[4,288,512]{2,1,0:T(8,128)(2,1)S(1)} %bitcast.5, bf16[512,1536]{1,0:T(8,128)(2,1)S(1)} %copy-done.4, bf16[512,512]{1,0:T(8,128)(2,1)S(1)} %copy-done.7, bf16[512,2048]{1,0:T(8,128)(2,1)S(1)} %copy-done.1, bf16[2048,512]{1,0:T(8,128)(2,1)S(1)} %copy-done.2, ...), custom_call_target="tpu_custom_call" | custom-call | flops 2500000000 | bytes 7553024 | tf_op jit(solution)/shard_map/pallas_call | solution.py:211
  15.2 1.8 %collective-permute-start.2 = (bf16[8,24,512]{2,1,0:T(8,128)(2,1)S(1)}, bf16[8,24,512]{2,1,0:T(8,128)(2,1)S(1)}, u32[]{:S(2)}, u32[]{:S(2)}) collective-permute-start(bf16[8,24,512]{2,1,0:T(8,128)(2,1)S(1)} %get-tuple-element.22), channel_id=1, source_target_pairs={{17,0},{18,1},{19,2},{20,3},{21,4},{22,5},{23,6},{24,7},{25,8},{26... | collective-permute-start | bytes 589832 | tf_op jit(solution)/shard_map/ppermute | solution.py:391
  16.9 0.0 collective-permute-done.refs_0_.refs_2_
  16.9 0.0 copy-done.11
  16.9 4.3 %shard_map.138 = (bf16[4,72,512]{2,1,0:T(8,128)(2,1)S(1)}, bf16[4,56,512]{2,1,0:T(8,128)(2,1)S(1)}) custom-call(bf16[4,56,512]{2,1,0:T(8,128)(2,1)S(1)} %collective-permute-done.refs_0_.refs_2_, bf16[4,288,512]{2,1,0:T(8,128)(2,1)S(1)} %bitcast.6, bf16[512,1536]{1,0:T(8,128)(2,1)S(1)} %copy-done.4, bf16[512,512]{1,0:T(8,128)(2,1)S(1)} %copy-done.7, ...), custom_call_target="tpu_custom_call" | custom-call | flops 2500000000 | bytes 8077312 | tf_op jit(solution)/shard_map/pallas_call | solution.py:211
  21.3 0.0 copy-start.13
  21.3 1.4 %collective-permute-start.4 = (bf16[4,56,512]{2,1,0:T(8,128)(2,1)S(1)}, bf16[4,56,512]{2,1,0:T(8,128)(2,1)S(1)}, u32[]{:S(2)}, u32[]{:S(2)}) collective-permute-start(bf16[4,56,512]{2,1,0:T(8,128)(2,1)S(1)} %get-tuple-element.24), channel_id=1, source_target_pairs={{16,0},{17,1},{18,2},{19,3},{20,4},{21,5},{22,6},{23,7},{24,8},{25... | collective-permute-start | bytes 688136 | tf_op jit(solution)/shard_map/ppermute | solution.py:391
  22.7 0.0 collective-permute-done.1.refs_0_.refs_1_
  22.7 0.0 copy-done.10
  22.7 4.5 %shard_map.139 = (bf16[4,72,512]{2,1,0:T(8,128)(2,1)S(1)}, bf16[4,56,512]{2,1,0:T(8,128)(2,1)S(1)}) custom-call(bf16[4,56,512]{2,1,0:T(8,128)(2,1)S(1)} %collective-permute-done.1.refs_0_.refs_1_, bf16[4,288,512]{2,1,0:T(8,128)(2,1)S(1)} %bitcast.7, bf16[512,1536]{1,0:T(8,128)(2,1)S(1)} %copy-done.4, bf16[512,512]{1,0:T(8,128)(2,1)S(1)} %copy-done.7, ...), custom_call_target="tpu_custom_call" | custom-call | flops 2500000000 | bytes 8077312 | tf_op jit(solution)/shard_map/pallas_call | solution.py:211
  27.2 0.0 slice-start.1
  27.2 0.0 copy-start
  27.2 0.0 copy-start.3
  27.3 0.0 copy-start.8
  27.3 0.0 copy-start.9
  27.3 2.3 %collective-permute-start.3 = (bf16[4,56,512]{2,1,0:T(8,128)(2,1)S(1)}, bf16[4,56,512]{2,1,0:T(8,128)(2,1)S(1)}, u32[]{:S(2)}, u32[]{:S(2)}) collective-permute-start(bf16[4,56,512]{2,1,0:T(8,128)(2,1)S(1)} %get-tuple-element.23), channel_id=1, source_target_pairs={{1,0},{2,1},{3,2},{4,3},{5,4},{6,5},{7,6},{8,7},{9,8},{10,9},{11,1... | collective-permute-start | bytes 688136 | tf_op jit(solution)/shard_map/ppermute | solution.py:391
  29.5 0.0 collective-permute-done.2.refs_0_.refs_6_
  29.5 0.0 copy-done.13
  29.5 4.3 %shard_map.140.refs_3_ = bf16[4,72,512]{2,1,0:T(8,128)(2,1)S(1)} custom-call(bf16[8,24,512]{2,1,0:T(8,128)(2,1)S(1)} %collective-permute-done.2.refs_0_.refs_6_, bf16[4,56,512]{2,1,0:T(8,128)(2,1)S(1)} %collective-permute-done.1.refs_0_.refs_1_, bf16[4,56,512]{2,1,0:T(8,128)(2,1)S(1)} %collective-permute-done.refs_0_.refs_2_, ...), custom_call_target="tpu_custom_call" | custom-call | flops 2500000000 | bytes 8167424 | tf_op jit(solution)/shard_map/pallas_call | solution.py:211
  33.8 0.0 collective-permute-done.4.refs_5_
  33.8 0.0 collective-permute-done.3.refs_4_
  33.8 0.0 slice-done
  33.8 0.0 slice-done.1
  33.9 0.0 copy-done
  33.9 0.0 copy-done.3
  33.9 0.0 copy-done.8
  33.9 0.0 copy-done.9
  33.9 8.6 %shard_map.141 = (bf16[3,6,4,1024]{3,2,1,0:T(4,128)(2,1)S(1)}, bf16[3,6,4,1024]{3,2,1,0:T(4,128)(2,1)S(1)}, bf16[3,6,4,1024]{3,2,1,0:T(4,128)(2,1)S(1)}, bf16[3,6,4,1024]{3,2,1,0:T(4,128)(2,1)S(1)}) custom-call(bf16[4,72,512]{2,1,0:T(8,128)(2,1)S(1)} %get-tuple-element.17.refs_6_.refs_0_, bf16[4,72,512]{2,1,0:T(8,128)(2,1)S(1)} %get-tuple-element.19.refs_1_, ...), custom_call_target="tpu_custom_call" | custom-call | flops 5000000000 | bytes 14934016 | tf_op jit(solution)/shard_map/pallas_call | solution.py:211
  42.5 0.1 collective-permute-start.5
  42.6 0.3 collective-permute-start.6
  42.9 1.1 %collective-permute-start.7 = (bf16[3,6,4,1024]{3,2,1,0:T(4,128)(2,1)S(1)}, bf16[3,6,4,1024]{3,2,1,0:T(4,128)(2,1)S(1)}, u32[]{:S(2)}, u32[]{:S(2)}) collective-permute-start(bf16[3,6,4,1024]{3,2,1,0:T(4,128)(2,1)S(1)} %get-tuple-element.28), channel_id=1, source_target_pairs={{127,0},{112,1},{113,2},{114,3},{115,4},{116,5},{117,6},{118,7},{1... | collective-permute-start | bytes 442376 | tf_op jit(solution)/shard_map/ppermute | solution.py:391
  44.0 6.7 %collective-permute-done.5.refs_1_ = bf16[3,6,4,1024]{3,2,1,0:T(4,128)(2,1)S(1)} collective-permute-done((bf16[3,6,4,1024]{3,2,1,0:T(4,128)(2,1)S(1)}, bf16[3,6,4,1024]{3,2,1,0:T(4,128)(2,1)S(1)}, u32[]{:S(2)}, u32[]{:S(2)}) %collective-permute-start.5) | collective-permute-done | bytes 147488 | tf_op jit(solution)/shard_map/ppermute | solution.py:391
  50.8 0.7 %collective-permute-done.6.refs_2_ = bf16[3,6,4,1024]{3,2,1,0:T(4,128)(2,1)S(1)} collective-permute-done((bf16[3,6,4,1024]{3,2,1,0:T(4,128)(2,1)S(1)}, bf16[3,6,4,1024]{3,2,1,0:T(4,128)(2,1)S(1)}, u32[]{:S(2)}, u32[]{:S(2)}) %collective-permute-start.6) | collective-permute-done | bytes 147488 | tf_op jit(solution)/shard_map/ppermute | solution.py:391
  51.4 6.2 %collective-permute-done.7.refs_3_ = bf16[3,6,4,1024]{3,2,1,0:T(4,128)(2,1)S(1)} collective-permute-done((bf16[3,6,4,1024]{3,2,1,0:T(4,128)(2,1)S(1)}, bf16[3,6,4,1024]{3,2,1,0:T(4,128)(2,1)S(1)}, u32[]{:S(2)}, u32[]{:S(2)}) %collective-permute-start.7) | collective-permute-done | bytes 147488 | tf_op jit(solution)/shard_map/ppermute | solution.py:391
  57.6 0.9 %shard_map.142 = bf16[6,12,4,1024]{3,2,1,0:T(4,128)(2,1)} custom-call(bf16[3,6,4,1024]{3,2,1,0:T(4,128)(2,1)S(1)} %get-tuple-element.25.refs_0_, bf16[3,6,4,1024]{3,2,1,0:T(4,128)(2,1)S(1)} %collective-permute-done.5.refs_1_, bf16[3,6,4,1024]{3,2,1,0:T(4,128)(2,1)S(1)} %collective-permute-done.6.refs_2_, ...), custom_call_target="tpu_custom_call" | custom-call | bytes 589824 | tf_op jit(solution)/shard_map/pallas_call | solution.py:211
  (8 shorter events, 0.0 us)
Async XLA Ops:
  0.0 1.3 %copy-start.5 = (bf16[4,12,24,512]{3,2,1,0:T(8,128)(2,1)S(1)}, bf16[4,12,24,512]{3,2,1,0:T(8,128)(2,1)}, u32[]{:S(2)}) copy-start(bf16[4,12,24,512]{3,2,1,0:T(8,128)(2,1)} %param.14) | copy-start | bytes 3538948
  1.3 9.6 %copy-start.1 = (bf16[512,2048]{1,0:T(8,128)(2,1)S(1)}, bf16[512,2048]{1,0:T(8,128)(2,1)}, u32[]{:S(2)}) copy-start(bf16[512,2048]{1,0:T(8,128)(2,1)} %refs_6_.1) | copy-start | bytes 6291460
  1.3 9.6 %copy-start.2 = (bf16[2048,512]{1,0:T(8,128)(2,1)S(1)}, bf16[2048,512]{1,0:T(8,128)(2,1)}, u32[]{:S(2)}) copy-start(bf16[2048,512]{1,0:T(8,128)(2,1)} %refs_7_.4) | copy-start | bytes 6291460
  1.3 9.6 %copy-start.4 = (bf16[512,1536]{1,0:T(8,128)(2,1)S(1)}, bf16[512,1536]{1,0:T(8,128)(2,1)}, u32[]{:S(2)}) copy-start(bf16[512,1536]{1,0:T(8,128)(2,1)} %refs_4_.7) | copy-start | bytes 4718596
  1.3 9.6 %copy-start.6 = (bf16[4,12,24,512]{3,2,1,0:T(8,128)(2,1)S(1)}, bf16[4,12,24,512]{3,2,1,0:T(8,128)(2,1)}, u32[]{:S(2)}) copy-start(bf16[4,12,24,512]{3,2,1,0:T(8,128)(2,1)} %param.14) | copy-start | bytes 3538948
  1.3 9.6 %copy-start.7 = (bf16[512,512]{1,0:T(8,128)(2,1)S(1)}, bf16[512,512]{1,0:T(8,128)(2,1)}, u32[]{:S(2)}) copy-start(bf16[512,512]{1,0:T(8,128)(2,1)} %refs_5_.6) | copy-start | bytes 1572868
  1.3 9.6 %copy-start.12 = (bf16[4,80,128]{2,1,0:T(8,128)(2,1)S(1)}, bf16[4,80,128]{2,1,0:T(8,128)(2,1)}, u32[]{:S(2)}) copy-start(bf16[4,80,128]{2,1,0:T(8,128)(2,1)} %constant.12.clone.refs_5_) | copy-start | bytes 245764
  1.7 15.2 %collective-permute-start = (bf16[4,56,512]{2,1,0:T(8,128)(2,1)S(1)}, bf16[4,56,512]{2,1,0:T(8,128)(2,1)S(1)}, u32[]{:S(2)}, u32[]{:S(2)}) collective-permute-start(bf16[4,56,512]{2,1,0:T(8,128)(2,1)S(1)} %get-tuple-element.18), channel_id=1, source_target_pairs={{1,0},{2,1},{3,2},{4,3},{5,4},{6,5},{7,6},{8,7},{9,8},{10,9},{11,1... | collective-permute-start | bytes 688136 | tf_op jit(solution)/shard_map/ppermute | solution.py:391
  8.0 9.0 %copy-start.11 = (bf16[4,80,128]{2,1,0:T(8,128)(2,1)S(1)}, bf16[4,80,128]{2,1,0:T(8,128)(2,1)}, u32[]{:S(2)}) copy-start(bf16[4,80,128]{2,1,0:T(8,128)(2,1)} %constant.13.clone.refs_7_) | copy-start | bytes 245764
  8.0 14.7 %collective-permute-start.1 = (bf16[4,56,512]{2,1,0:T(8,128)(2,1)S(1)}, bf16[4,56,512]{2,1,0:T(8,128)(2,1)S(1)}, u32[]{:S(2)}, u32[]{:S(2)}) collective-permute-start(bf16[4,56,512]{2,1,0:T(8,128)(2,1)S(1)} %get-tuple-element.20), channel_id=1, source_target_pairs={{16,0},{17,1},{18,2},{19,3},{20,4},{21,5},{22,6},{23,7},{24,8},{25... | collective-permute-start | bytes 688136 | tf_op jit(solution)/shard_map/ppermute | solution.py:391
  15.2 14.4 %collective-permute-start.2 = (bf16[8,24,512]{2,1,0:T(8,128)(2,1)S(1)}, bf16[8,24,512]{2,1,0:T(8,128)(2,1)S(1)}, u32[]{:S(2)}, u32[]{:S(2)}) collective-permute-start(bf16[8,24,512]{2,1,0:T(8,128)(2,1)S(1)} %get-tuple-element.22), channel_id=1, source_target_pairs={{17,0},{18,1},{19,2},{20,3},{21,4},{22,5},{23,6},{24,7},{25,8},{26... | collective-permute-start | bytes 589832 | tf_op jit(solution)/shard_map/ppermute | solution.py:391
  16.9 5.7 %copy-start.10 = (bf16[4,80,128]{2,1,0:T(8,128)(2,1)S(1)}, bf16[4,80,128]{2,1,0:T(8,128)(2,1)}, u32[]{:S(2)}) copy-start(bf16[4,80,128]{2,1,0:T(8,128)(2,1)} %constant.14.clone.refs_7_) | copy-start | bytes 245764
  21.3 8.3 %copy-start.13 = (bf16[2,80,128]{2,1,0:T(8,128)(2,1)S(1)}, bf16[2,80,128]{2,1,0:T(8,128)(2,1)}, u32[]{:S(2)}) copy-start(bf16[2,80,128]{2,1,0:T(8,128)(2,1)} %constant.15.clone.refs_8_) | copy-start | bytes 122884
  21.3 12.5 %collective-permute-start.4 = (bf16[4,56,512]{2,1,0:T(8,128)(2,1)S(1)}, bf16[4,56,512]{2,1,0:T(8,128)(2,1)S(1)}, u32[]{:S(2)}, u32[]{:S(2)}) collective-permute-start(bf16[4,56,512]{2,1,0:T(8,128)(2,1)S(1)} %get-tuple-element.24), channel_id=1, source_target_pairs={{16,0},{17,1},{18,2},{19,3},{20,4},{21,5},{22,6},{23,7},{24,8},{25... | collective-permute-start | bytes 688136 | tf_op jit(solution)/shard_map/ppermute | solution.py:391
  22.7 11.2 %slice-start = ((s8[6291456]{0:T(1024)(128)(4,1)}), s8[4194304]{0:T(1024)(128)(4,1)S(1)}, s32[]{:S(2)}) async-start(s8[6291456]{0:T(1024)(128)(4,1)} %bitcast.2), calls=%async_computation | async-start | bytes 8388608
  27.2 6.6 %slice-start.1 = ((s8[6291456]{0:T(1024)(128)(4,1)}), s8[2097152]{0:T(1024)(128)(4,1)S(1)}, s32[]{:S(2)}) async-start(s8[6291456]{0:T(1024)(128)(4,1)} %bitcast.2), calls=%async_computation.1 | async-start | bytes 4194304
  27.2 6.6 %copy-start = (bf16[2048,1024]{1,0:T(8,128)(2,1)S(1)}, bf16[2048,1024]{1,0:T(8,128)(2,1)}, u32[]{:S(2)}) copy-start(bf16[2048,1024]{1,0:T(8,128)(2,1)} %refs_9_.1) | copy-start | bytes 12582916
  27.2 6.6 %copy-start.3 = (bf16[1024,1024]{1,0:T(8,128)(2,1)S(1)}, bf16[1024,1024]{1,0:T(8,128)(2,1)}, u32[]{:S(2)}) copy-start(bf16[1024,1024]{1,0:T(8,128)(2,1)} %refs_11_.1) | copy-start | bytes 6291460
  27.3 6.6 %copy-start.8 = (bf16[4,288,128]{2,1,0:T(8,128)(2,1)S(1)}, bf16[4,288,128]{2,1,0:T(8,128)(2,1)}, u32[]{:S(2)}) copy-start(bf16[4,288,128]{2,1,0:T(8,128)(2,1)} %constant.16.clone.refs_7_) | copy-start | bytes 884740
  27.3 6.6 %copy-start.9 = (bf16[3,288,128]{2,1,0:T(8,128)(2,1)S(1)}, bf16[3,288,128]{2,1,0:T(8,128)(2,1)}, u32[]{:S(2)}) copy-start(bf16[3,288,128]{2,1,0:T(8,128)(2,1)} %constant.17.clone.refs_8_) | copy-start | bytes 663556
  27.3 6.5 %collective-permute-start.3 = (bf16[4,56,512]{2,1,0:T(8,128)(2,1)S(1)}, bf16[4,56,512]{2,1,0:T(8,128)(2,1)S(1)}, u32[]{:S(2)}, u32[]{:S(2)}) collective-permute-start(bf16[4,56,512]{2,1,0:T(8,128)(2,1)S(1)} %get-tuple-element.23), channel_id=1, source_target_pairs={{1,0},{2,1},{3,2},{4,3},{5,4},{6,5},{7,6},{8,7},{9,8},{10,9},{11,1... | collective-permute-start | bytes 688136 | tf_op jit(solution)/shard_map/ppermute | solution.py:391
  42.5 8.3 %collective-permute-start.5 = (bf16[3,6,4,1024]{3,2,1,0:T(4,128)(2,1)S(1)}, bf16[3,6,4,1024]{3,2,1,0:T(4,128)(2,1)S(1)}, u32[]{:S(2)}, u32[]{:S(2)}) collective-permute-start(bf16[3,6,4,1024]{3,2,1,0:T(4,128)(2,1)S(1)} %get-tuple-element.26), channel_id=1, source_target_pairs={{15,0},{0,1},{1,2},{2,3},{3,4},{4,5},{5,6},{6,7},{7,8},{8,9},{9,10... | collective-permute-start | bytes 442376 | tf_op jit(solution)/shard_map/ppermute | solution.py:391
  42.6 8.9 %collective-permute-start.6 = (bf16[3,6,4,1024]{3,2,1,0:T(4,128)(2,1)S(1)}, bf16[3,6,4,1024]{3,2,1,0:T(4,128)(2,1)S(1)}, u32[]{:S(2)}, u32[]{:S(2)}) collective-permute-start(bf16[3,6,4,1024]{3,2,1,0:T(4,128)(2,1)S(1)} %get-tuple-element.27), channel_id=1, source_target_pairs={{112,0},{113,1},{114,2},{115,3},{116,4},{117,5},{118,6},{119,7},{1... | collective-permute-start | bytes 442376 | tf_op jit(solution)/shard_map/ppermute | solution.py:391
  42.9 14.7 %collective-permute-start.7 = (bf16[3,6,4,1024]{3,2,1,0:T(4,128)(2,1)S(1)}, bf16[3,6,4,1024]{3,2,1,0:T(4,128)(2,1)S(1)}, u32[]{:S(2)}, u32[]{:S(2)}) collective-permute-start(bf16[3,6,4,1024]{3,2,1,0:T(4,128)(2,1)S(1)} %get-tuple-element.28), channel_id=1, source_target_pairs={{127,0},{112,1},{113,2},{114,3},{115,4},{116,5},{117,6},{118,7},{1... | collective-permute-start | bytes 442376 | tf_op jit(solution)/shard_map/ppermute | solution.py:391

commit v7 on v6

--- a/solution.py
+++ b/solution.py
@@ -405,10 +405,10 @@
     blocks = fine_quads(QUADS[:1], sources, weights, {}, ("both",))
     corners = shift({"both": blocks.pop("both")})["both"]
     sources["both"] = corners
-    second = fine_quads(QUADS[1:2], sources, weights, blocks, ("lat",))
-    pieces = {"both": corners} | shift({"lat": second.pop("lat")})
-    third = fine_quads(QUADS[2:3], sources, weights, blocks, ("lon",))
-    pieces |= shift({"lon": third.pop("lon")})
+    second = fine_quads(QUADS[2:3], sources, weights, blocks, ("lon",))
+    pieces = {"both": corners} | shift({"lon": second.pop("lon")})
+    third = fine_quads(QUADS[1:2], sources, weights, blocks, ("lat",))
+    pieces |= shift({"lat": third.pop("lat")})
     blocks |= second | third
     blocks |= fine_quads(QUADS[3:], sources, weights, {}, ())
     parts = coarse(blocks, pieces, merge_weight, coarse_qkv, coarse_out)

time: 58.6 us -> 58.6 us (level)
  no operation moved by 1% of the time
where the time goes in v7:
time: 58.6 us; the launch traced here: 58.5 us
  Pallas kernels  27.3 us (47%)
  starting transfers between devices  16 us (27%)
  waiting for transfers between devices  13.6 us (23%)
  local copies, waits for them, and re-layouts  1.35 us (2%)
    pallas_call x7, Pallas kernels, run(): pl.pallas_call(kernel, out_shape=[jax.ShapeDtypeStruct(shape, BF16) for s...  27.3 us
    ppermute x8, starting transfers between devices, receive(): return lax.ppermute(array, ('lat', 'lon'), pairs)  16 us
    ppermute x8, waiting for transfers between devices, receive(): return lax.ppermute(array, ('lat', 'lon'), pairs)  13.6 us
    unnamed x32, local copies, waits for them, and re-layouts  1.35 us
  transfers between devices with their start and end apart: 8, of which 3 were waited for; matrix products, arithmetic and copies ran while one was open for 0% of the time, Pallas kernels for 30%

profile of v7, /device:TPU:0, one launch (start us, length us, event | category | flops | bytes accessed | tf_op | source)
XLA Modules:
  0.0 58.5 jit_solution(7696329805337328841)
XLA Ops:
  0.0 0.0 copy-start.5
  0.0 1.3 %copy-done.5 = bf16[4,12,24,512]{3,2,1,0:T(8,128)(2,1)S(1)} copy-done((bf16[4,12,24,512]{3,2,1,0:T(8,128)(2,1)S(1)}, bf16[4,12,24,512]{3,2,1,0:T(8,128)(2,1)}, u32[]{:S(2)}) %copy-start.5) | copy-done | bytes 1179672
  1.3 0.0 copy-start.7
  1.3 0.0 copy-start.12
  1.3 0.4 shard_map.137
  1.7 6.2 %collective-permute-start = (bf16[4,56,512]{2,1,0:T(8,128)(2,1)S(1)}, bf16[4,56,512]{2,1,0:T(8,128)(2,1)S(1)}, u32[]{:S(2)}, u32[]{:S(2)}) collective-permute-start(bf16[4,56,512]{2,1,0:T(8,128)(2,1)S(1)} %get-tuple-element.18), channel_id=1, source_target_pairs={{1,0},{2,1},{3,2},{4,3},{5,4},{6,5},{7,6},{8,7},{9,8},{10,9},{11,1... | collective-permute-start | bytes 688136 | tf_op jit(solution)/shard_map/ppermute | solution.py:391
  8.0 2.9 %collective-permute-start.1 = (bf16[4,56,512]{2,1,0:T(8,128)(2,1)S(1)}, bf16[4,56,512]{2,1,0:T(8,128)(2,1)S(1)}, u32[]{:S(2)}, u32[]{:S(2)}) collective-permute-start(bf16[4,56,512]{2,1,0:T(8,128)(2,1)S(1)} %get-tuple-element.20), channel_id=1, source_target_pairs={{16,0},{17,1},{18,2},{19,3},{20,4},{21,5},{22,6},{23,7},{24,8},{25... | collective-permute-start | bytes 688136 | tf_op jit(solution)/shard_map/ppermute | solution.py:391
  10.9 0.0 copy-done.1
  10.9 0.0 copy-done.2
  10.9 0.0 copy-done.4
  10.9 0.0 copy-done.6
  10.9 0.0 copy-done.7
  10.9 0.0 copy-done.12
  10.9 4.3 %shard_map.136 = (bf16[4,72,512]{2,1,0:T(8,128)(2,1)S(1)}, bf16[8,24,512]{2,1,0:T(8,128)(2,1)S(1)}) custom-call(bf16[4,288,512]{2,1,0:T(8,128)(2,1)S(1)} %bitcast.5, bf16[512,1536]{1,0:T(8,128)(2,1)S(1)} %copy-done.4, bf16[512,512]{1,0:T(8,128)(2,1)S(1)} %copy-done.7, bf16[512,2048]{1,0:T(8,128)(2,1)S(1)} %copy-done.1, bf16[2048,512]{1,0:T(8,128)(2,1)S(1)} %copy-done.2, ...), custom_call_target="tpu_custom_call" | custom-call | flops 2500000000 | bytes 7553024 | tf_op jit(solution)/shard_map/pallas_call | solution.py:211
  15.2 1.8 %collective-permute-start.2 = (bf16[8,24,512]{2,1,0:T(8,128)(2,1)S(1)}, bf16[8,24,512]{2,1,0:T(8,128)(2,1)S(1)}, u32[]{:S(2)}, u32[]{:S(2)}) collective-permute-start(bf16[8,24,512]{2,1,0:T(8,128)(2,1)S(1)} %get-tuple-element.22), channel_id=1, source_target_pairs={{17,0},{18,1},{19,2},{20,3},{21,4},{22,5},{23,6},{24,7},{25,8},{26... | collective-permute-start | bytes 589832 | tf_op jit(solution)/shard_map/ppermute | solution.py:391
  16.9 0.0 collective-permute-done.refs_0_.refs_2_
  16.9 0.0 copy-done.11
  16.9 4.3 %shard_map.138 = (bf16[4,72,512]{2,1,0:T(8,128)(2,1)S(1)}, bf16[4,56,512]{2,1,0:T(8,128)(2,1)S(1)}) custom-call(bf16[4,56,512]{2,1,0:T(8,128)(2,1)S(1)} %collective-permute-done.refs_0_.refs_2_, bf16[4,288,512]{2,1,0:T(8,128)(2,1)S(1)} %bitcast.6, bf16[512,1536]{1,0:T(8,128)(2,1)S(1)} %copy-done.4, bf16[512,512]{1,0:T(8,128)(2,1)S(1)} %copy-done.7, ...), custom_call_target="tpu_custom_call" | custom-call | flops 2500000000 | bytes 8077312 | tf_op jit(solution)/shard_map/pallas_call | solution.py:211
  21.3 0.0 copy-start.13
  21.3 1.4 %collective-permute-start.4 = (bf16[4,56,512]{2,1,0:T(8,128)(2,1)S(1)}, bf16[4,56,512]{2,1,0:T(8,128)(2,1)S(1)}, u32[]{:S(2)}, u32[]{:S(2)}) collective-permute-start(bf16[4,56,512]{2,1,0:T(8,128)(2,1)S(1)} %get-tuple-element.24), channel_id=1, source_target_pairs={{16,0},{17,1},{18,2},{19,3},{20,4},{21,5},{22,6},{23,7},{24,8},{25... | collective-permute-start | bytes 688136 | tf_op jit(solution)/shard_map/ppermute | solution.py:391
  22.7 0.0 collective-permute-done.1.refs_0_.refs_1_
  22.7 0.0 copy-done.10
  22.7 4.5 %shard_map.139 = (bf16[4,72,512]{2,1,0:T(8,128)(2,1)S(1)}, bf16[4,56,512]{2,1,0:T(8,128)(2,1)S(1)}) custom-call(bf16[4,56,512]{2,1,0:T(8,128)(2,1)S(1)} %collective-permute-done.1.refs_0_.refs_1_, bf16[4,288,512]{2,1,0:T(8,128)(2,1)S(1)} %bitcast.7, bf16[512,1536]{1,0:T(8,128)(2,1)S(1)} %copy-done.4, bf16[512,512]{1,0:T(8,128)(2,1)S(1)} %copy-done.7, ...), custom_call_target="tpu_custom_call" | custom-call | flops 2500000000 | bytes 8077312 | tf_op jit(solution)/shard_map/pallas_call | solution.py:211
  27.2 0.0 slice-start.1
  27.2 0.0 copy-start
  27.2 0.0 copy-start.3
  27.3 0.0 copy-start.8
  27.3 0.0 copy-start.9
  27.3 2.3 %collective-permute-start.3 = (bf16[4,56,512]{2,1,0:T(8,128)(2,1)S(1)}, bf16[4,56,512]{2,1,0:T(8,128)(2,1)S(1)}, u32[]{:S(2)}, u32[]{:S(2)}) collective-permute-start(bf16[4,56,512]{2,1,0:T(8,128)(2,1)S(1)} %get-tuple-element.23), channel_id=1, source_target_pairs={{1,0},{2,1},{3,2},{4,3},{5,4},{6,5},{7,6},{8,7},{9,8},{10,9},{11,1... | collective-permute-start | bytes 688136 | tf_op jit(solution)/shard_map/ppermute | solution.py:391
  29.5 0.0 collective-permute-done.2.refs_0_.refs_6_
  29.5 0.0 copy-done.13
  29.5 4.3 %shard_map.140.refs_3_ = bf16[4,72,512]{2,1,0:T(8,128)(2,1)S(1)} custom-call(bf16[8,24,512]{2,1,0:T(8,128)(2,1)S(1)} %collective-permute-done.2.refs_0_.refs_6_, bf16[4,56,512]{2,1,0:T(8,128)(2,1)S(1)} %collective-permute-done.1.refs_0_.refs_1_, bf16[4,56,512]{2,1,0:T(8,128)(2,1)S(1)} %collective-permute-done.refs_0_.refs_2_, ...), custom_call_target="tpu_custom_call" | custom-call | flops 2500000000 | bytes 8167424 | tf_op jit(solution)/shard_map/pallas_call | solution.py:211
  33.8 0.0 collective-permute-done.4.refs_5_
  33.8 0.0 collective-permute-done.3.refs_4_
  33.8 0.0 slice-done
  33.8 0.0 slice-done.1
  33.9 0.0 copy-done
  33.9 0.0 copy-done.3
  33.9 0.0 copy-done.8
  33.9 0.0 copy-done.9
  33.9 8.6 %shard_map.141 = (bf16[3,6,4,1024]{3,2,1,0:T(4,128)(2,1)S(1)}, bf16[3,6,4,1024]{3,2,1,0:T(4,128)(2,1)S(1)}, bf16[3,6,4,1024]{3,2,1,0:T(4,128)(2,1)S(1)}, bf16[3,6,4,1024]{3,2,1,0:T(4,128)(2,1)S(1)}) custom-call(bf16[4,72,512]{2,1,0:T(8,128)(2,1)S(1)} %get-tuple-element.17.refs_6_.refs_0_, bf16[4,72,512]{2,1,0:T(8,128)(2,1)S(1)} %get-tuple-element.19.refs_1_, ...), custom_call_target="tpu_custom_call" | custom-call | flops 5000000000 | bytes 14934016 | tf_op jit(solution)/shard_map/pallas_call | solution.py:211
  42.5 0.1 collective-permute-start.5
  42.6 0.3 collective-permute-start.6
  42.9 1.1 %collective-permute-start.7 = (bf16[3,6,4,1024]{3,2,1,0:T(4,128)(2,1)S(1)}, bf16[3,6,4,1024]{3,2,1,0:T(4,128)(2,1)S(1)}, u32[]{:S(2)}, u32[]{:S(2)}) collective-permute-start(bf16[3,6,4,1024]{3,2,1,0:T(4,128)(2,1)S(1)} %get-tuple-element.28), channel_id=1, source_target_pairs={{127,0},{112,1},{113,2},{114,3},{115,4},{116,5},{117,6},{118,7},{1... | collective-permute-start | bytes 442376 | tf_op jit(solution)/shard_map/ppermute | solution.py:391
  44.0 6.7 %collective-permute-done.5.refs_1_ = bf16[3,6,4,1024]{3,2,1,0:T(4,128)(2,1)S(1)} collective-permute-done((bf16[3,6,4,1024]{3,2,1,0:T(4,128)(2,1)S(1)}, bf16[3,6,4,1024]{3,2,1,0:T(4,128)(2,1)S(1)}, u32[]{:S(2)}, u32[]{:S(2)}) %collective-permute-start.5) | collective-permute-done | bytes 147488 | tf_op jit(solution)/shard_map/ppermute | solution.py:391
  50.8 0.7 %collective-permute-done.6.refs_2_ = bf16[3,6,4,1024]{3,2,1,0:T(4,128)(2,1)S(1)} collective-permute-done((bf16[3,6,4,1024]{3,2,1,0:T(4,128)(2,1)S(1)}, bf16[3,6,4,1024]{3,2,1,0:T(4,128)(2,1)S(1)}, u32[]{:S(2)}, u32[]{:S(2)}) %collective-permute-start.6) | collective-permute-done | bytes 147488 | tf_op jit(solution)/shard_map/ppermute | solution.py:391
  51.4 6.2 %collective-permute-done.7.refs_3_ = bf16[3,6,4,1024]{3,2,1,0:T(4,128)(2,1)S(1)} collective-permute-done((bf16[3,6,4,1024]{3,2,1,0:T(4,128)(2,1)S(1)}, bf16[3,6,4,1024]{3,2,1,0:T(4,128)(2,1)S(1)}, u32[]{:S(2)}, u32[]{:S(2)}) %collective-permute-start.7) | collective-permute-done | bytes 147488 | tf_op jit(solution)/shard_map/ppermute | solution.py:391
  57.6 0.9 %shard_map.142 = bf16[6,12,4,1024]{3,2,1,0:T(4,128)(2,1)} custom-call(bf16[3,6,4,1024]{3,2,1,0:T(4,128)(2,1)S(1)} %get-tuple-element.25.refs_0_, bf16[3,6,4,1024]{3,2,1,0:T(4,128)(2,1)S(1)} %collective-permute-done.5.refs_1_, bf16[3,6,4,1024]{3,2,1,0:T(4,128)(2,1)S(1)} %collective-permute-done.6.refs_2_, ...), custom_call_target="tpu_custom_call" | custom-call | bytes 589824 | tf_op jit(solution)/shard_map/pallas_call | solution.py:211
  (8 shorter events, 0.0 us)
Async XLA Ops:
  0.0 1.3 %copy-start.5 = (bf16[4,12,24,512]{3,2,1,0:T(8,128)(2,1)S(1)}, bf16[4,12,24,512]{3,2,1,0:T(8,128)(2,1)}, u32[]{:S(2)}) copy-start(bf16[4,12,24,512]{3,2,1,0:T(8,128)(2,1)} %param.14) | copy-start | bytes 3538948
  1.3 9.6 %copy-start.1 = (bf16[512,2048]{1,0:T(8,128)(2,1)S(1)}, bf16[512,2048]{1,0:T(8,128)(2,1)}, u32[]{:S(2)}) copy-start(bf16[512,2048]{1,0:T(8,128)(2,1)} %refs_6_.1) | copy-start | bytes 6291460
  1.3 9.6 %copy-start.2 = (bf16[2048,512]{1,0:T(8,128)(2,1)S(1)}, bf16[2048,512]{1,0:T(8,128)(2,1)}, u32[]{:S(2)}) copy-start(bf16[2048,512]{1,0:T(8,128)(2,1)} %refs_7_.4) | copy-start | bytes 6291460
  1.3 9.6 %copy-start.4 = (bf16[512,1536]{1,0:T(8,128)(2,1)S(1)}, bf16[512,1536]{1,0:T(8,128)(2,1)}, u32[]{:S(2)}) copy-start(bf16[512,1536]{1,0:T(8,128)(2,1)} %refs_4_.7) | copy-start | bytes 4718596
  1.3 9.6 %copy-start.6 = (bf16[4,12,24,512]{3,2,1,0:T(8,128)(2,1)S(1)}, bf16[4,12,24,512]{3,2,1,0:T(8,128)(2,1)}, u32[]{:S(2)}) copy-start(bf16[4,12,24,512]{3,2,1,0:T(8,128)(2,1)} %param.14) | copy-start | bytes 3538948
  1.3 9.6 %copy-start.7 = (bf16[512,512]{1,0:T(8,128)(2,1)S(1)}, bf16[512,512]{1,0:T(8,128)(2,1)}, u32[]{:S(2)}) copy-start(bf16[512,512]{1,0:T(8,128)(2,1)} %refs_5_.6) | copy-start | bytes 1572868
  1.3 9.6 %copy-start.12 = (bf16[4,80,128]{2,1,0:T(8,128)(2,1)S(1)}, bf16[4,80,128]{2,1,0:T(8,128)(2,1)}, u32[]{:S(2)}) copy-start(bf16[4,80,128]{2,1,0:T(8,128)(2,1)} %constant.12.clone.refs_5_) | copy-start | bytes 245764
  1.7 15.2 %collective-permute-start = (bf16[4,56,512]{2,1,0:T(8,128)(2,1)S(1)}, bf16[4,56,512]{2,1,0:T(8,128)(2,1)S(1)}, u32[]{:S(2)}, u32[]{:S(2)}) collective-permute-start(bf16[4,56,512]{2,1,0:T(8,128)(2,1)S(1)} %get-tuple-element.18), channel_id=1, source_target_pairs={{1,0},{2,1},{3,2},{4,3},{5,4},{6,5},{7,6},{8,7},{9,8},{10,9},{11,1... | collective-permute-start | bytes 688136 | tf_op jit(solution)/shard_map/ppermute | solution.py:391
  8.0 9.0 %copy-start.11 = (bf16[4,80,128]{2,1,0:T(8,128)(2,1)S(1)}, bf16[4,80,128]{2,1,0:T(8,128)(2,1)}, u32[]{:S(2)}) copy-start(bf16[4,80,128]{2,1,0:T(8,128)(2,1)} %constant.14.clone.refs_7_) | copy-start | bytes 245764
  8.0 14.7 %collective-permute-start.1 = (bf16[4,56,512]{2,1,0:T(8,128)(2,1)S(1)}, bf16[4,56,512]{2,1,0:T(8,128)(2,1)S(1)}, u32[]{:S(2)}, u32[]{:S(2)}) collective-permute-start(bf16[4,56,512]{2,1,0:T(8,128)(2,1)S(1)} %get-tuple-element.20), channel_id=1, source_target_pairs={{16,0},{17,1},{18,2},{19,3},{20,4},{21,5},{22,6},{23,7},{24,8},{25... | collective-permute-start | bytes 688136 | tf_op jit(solution)/shard_map/ppermute | solution.py:391
  15.2 14.4 %collective-permute-start.2 = (bf16[8,24,512]{2,1,0:T(8,128)(2,1)S(1)}, bf16[8,24,512]{2,1,0:T(8,128)(2,1)S(1)}, u32[]{:S(2)}, u32[]{:S(2)}) collective-permute-start(bf16[8,24,512]{2,1,0:T(8,128)(2,1)S(1)} %get-tuple-element.22), channel_id=1, source_target_pairs={{17,0},{18,1},{19,2},{20,3},{21,4},{22,5},{23,6},{24,7},{25,8},{26... | collective-permute-start | bytes 589832 | tf_op jit(solution)/shard_map/ppermute | solution.py:391
  16.9 5.7 %copy-start.10 = (bf16[4,80,128]{2,1,0:T(8,128)(2,1)S(1)}, bf16[4,80,128]{2,1,0:T(8,128)(2,1)}, u32[]{:S(2)}) copy-start(bf16[4,80,128]{2,1,0:T(8,128)(2,1)} %constant.13.clone.refs_7_) | copy-start | bytes 245764
  21.3 8.3 %copy-start.13 = (bf16[2,80,128]{2,1,0:T(8,128)(2,1)S(1)}, bf16[2,80,128]{2,1,0:T(8,128)(2,1)}, u32[]{:S(2)}) copy-start(bf16[2,80,128]{2,1,0:T(8,128)(2,1)} %constant.15.clone.refs_8_) | copy-start | bytes 122884
  21.3 12.5 %collective-permute-start.4 = (bf16[4,56,512]{2,1,0:T(8,128)(2,1)S(1)}, bf16[4,56,512]{2,1,0:T(8,128)(2,1)S(1)}, u32[]{:S(2)}, u32[]{:S(2)}) collective-permute-start(bf16[4,56,512]{2,1,0:T(8,128)(2,1)S(1)} %get-tuple-element.24), channel_id=1, source_target_pairs={{16,0},{17,1},{18,2},{19,3},{20,4},{21,5},{22,6},{23,7},{24,8},{25... | collective-permute-start | bytes 688136 | tf_op jit(solution)/shard_map/ppermute | solution.py:391
  22.7 11.2 %slice-start = ((s8[6291456]{0:T(1024)(128)(4,1)}), s8[4194304]{0:T(1024)(128)(4,1)S(1)}, s32[]{:S(2)}) async-start(s8[6291456]{0:T(1024)(128)(4,1)} %bitcast.2), calls=%async_computation | async-start | bytes 8388608
  27.2 6.6 %slice-start.1 = ((s8[6291456]{0:T(1024)(128)(4,1)}), s8[2097152]{0:T(1024)(128)(4,1)S(1)}, s32[]{:S(2)}) async-start(s8[6291456]{0:T(1024)(128)(4,1)} %bitcast.2), calls=%async_computation.1 | async-start | bytes 4194304
  27.2 6.6 %copy-start = (bf16[2048,1024]{1,0:T(8,128)(2,1)S(1)}, bf16[2048,1024]{1,0:T(8,128)(2,1)}, u32[]{:S(2)}) copy-start(bf16[2048,1024]{1,0:T(8,128)(2,1)} %refs_9_.1) | copy-start | bytes 12582916
  27.2 6.6 %copy-start.3 = (bf16[1024,1024]{1,0:T(8,128)(2,1)S(1)}, bf16[1024,1024]{1,0:T(8,128)(2,1)}, u32[]{:S(2)}) copy-start(bf16[1024,1024]{1,0:T(8,128)(2,1)} %refs_11_.1) | copy-start | bytes 6291460
  27.3 6.6 %copy-start.8 = (bf16[4,288,128]{2,1,0:T(8,128)(2,1)S(1)}, bf16[4,288,128]{2,1,0:T(8,128)(2,1)}, u32[]{:S(2)}) copy-start(bf16[4,288,128]{2,1,0:T(8,128)(2,1)} %constant.16.clone.refs_7_) | copy-start | bytes 884740
  27.3 6.6 %copy-start.9 = (bf16[3,288,128]{2,1,0:T(8,128)(2,1)S(1)}, bf16[3,288,128]{2,1,0:T(8,128)(2,1)}, u32[]{:S(2)}) copy-start(bf16[3,288,128]{2,1,0:T(8,128)(2,1)} %constant.17.clone.refs_8_) | copy-start | bytes 663556
  27.3 6.5 %collective-permute-start.3 = (bf16[4,56,512]{2,1,0:T(8,128)(2,1)S(1)}, bf16[4,56,512]{2,1,0:T(8,128)(2,1)S(1)}, u32[]{:S(2)}, u32[]{:S(2)}) collective-permute-start(bf16[4,56,512]{2,1,0:T(8,128)(2,1)S(1)} %get-tuple-element.23), channel_id=1, source_target_pairs={{1,0},{2,1},{3,2},{4,3},{5,4},{6,5},{7,6},{8,7},{9,8},{10,9},{11,1... | collective-permute-start | bytes 688136 | tf_op jit(solution)/shard_map/ppermute | solution.py:391
  42.5 8.3 %collective-permute-start.5 = (bf16[3,6,4,1024]{3,2,1,0:T(4,128)(2,1)S(1)}, bf16[3,6,4,1024]{3,2,1,0:T(4,128)(2,1)S(1)}, u32[]{:S(2)}, u32[]{:S(2)}) collective-permute-start(bf16[3,6,4,1024]{3,2,1,0:T(4,128)(2,1)S(1)} %get-tuple-element.26), channel_id=1, source_target_pairs={{15,0},{0,1},{1,2},{2,3},{3,4},{4,5},{5,6},{6,7},{7,8},{8,9},{9,10... | collective-permute-start | bytes 442376 | tf_op jit(solution)/shard_map/ppermute | solution.py:391
  42.6 8.9 %collective-permute-start.6 = (bf16[3,6,4,1024]{3,2,1,0:T(4,128)(2,1)S(1)}, bf16[3,6,4,1024]{3,2,1,0:T(4,128)(2,1)S(1)}, u32[]{:S(2)}, u32[]{:S(2)}) collective-permute-start(bf16[3,6,4,1024]{3,2,1,0:T(4,128)(2,1)S(1)} %get-tuple-element.27), channel_id=1, source_target_pairs={{112,0},{113,1},{114,2},{115,3},{116,4},{117,5},{118,6},{119,7},{1... | collective-permute-start | bytes 442376 | tf_op jit(solution)/shard_map/ppermute | solution.py:391
  42.9 14.7 %collective-permute-start.7 = (bf16[3,6,4,1024]{3,2,1,0:T(4,128)(2,1)S(1)}, bf16[3,6,4,1024]{3,2,1,0:T(4,128)(2,1)S(1)}, u32[]{:S(2)}, u32[]{:S(2)}) collective-permute-start(bf16[3,6,4,1024]{3,2,1,0:T(4,128)(2,1)S(1)} %get-tuple-element.28), channel_id=1, source_target_pairs={{127,0},{112,1},{113,2},{114,3},{115,4},{116,5},{117,6},{118,7},{1... | collective-permute-start | bytes 442376 | tf_op jit(solution)/shard_map/ppermute | solution.py:391
